TPU v7x, 256 devices: a whole 4x4x8 slice. The times are simulated.
256 devices in a mesh: seq: 4 (over x), half: 2 (over core), ctx: 32 (over y, z).
Axes of the slice: x: 4, y: 4, z: 8, core: 2. Of those that a mesh axis runs over, the one named last changes fastest.
Arguments:
- features: bfloat16 [12, 512, 32768], P('seq', None, ('half', 'ctx')), parts along dimension 0, may hold values from -6 to 6
- short_taps: float32 [7, 3, 512], replicated, may hold values from -2.5 to 2.5
- filters: float32 [512, 32768], P('ctx'), may hold values from -6 to 6
- skip: float32 [512], replicated, may hold values from -4 to 4
Outputs:
- mixed: bfloat16 [2048, 32768], P('seq', ('half', 'ctx')), parts along dimension 0
There are 4 independent parts, one for each index of `seq`. A program takes and returns all parts, laid end to end along the dimension named above; an argument that names none is the same for every part. Nothing has to cross between parts.
All inputs are finite; a program needn't handle non-finite values.
Results may differ from a plain program's by a relative error of at most 0.005.
Values may be sent and summed in bfloat16 or wider, within the bound.
No kernel may reach another device: no remote copies, remote signals or barrier semaphores. Data moves between devices by JAX's collectives and lax.ppermute only.
A program may use at most 128 MiB of HBM per device.

v0:
```python
import math

import jax
import jax.numpy as jnp
from jax import lax
from jax.sharding import PartitionSpec as P

TAPS = 7
COLS = 128


exact_mode = lax.Precision.HIGHEST


def shifted(x, axis, by):
    size = lax.axis_size(axis)
    pairs = [(i, i + by) for i in range(size) if 0 <= i + by < size]
    return lax.ppermute(x, axis, pairs)


def tables(rows_count, cols_count, period):
    row_ids = lax.broadcasted_iota(jnp.int32, (rows_count, cols_count), 0)
    col_ids = lax.broadcasted_iota(jnp.int32, (rows_count, cols_count), 1)
    phase = (row_ids * col_ids % period).astype(jnp.float32) * (2.0 * math.pi / period)
    return (jnp.cos(phase), -jnp.sin(phase))


def forward_spectrum(signal, total_len):
    channels = signal.shape[0]
    rows_total = total_len // COLS
    used_rows = signal.shape[1] // COLS
    grid = signal.reshape(channels, used_rows, COLS)
    first_re, first_im = tables(rows_total, used_rows, rows_total)
    part_re = jnp.einsum("kr,crm->ckm", first_re, grid, precision=exact_mode)
    part_im = jnp.einsum("kr,crm->ckm", first_im, grid, precision=exact_mode)
    twist_re, twist_im = tables(rows_total, COLS, total_len)
    turned_re = part_re * twist_re - part_im * twist_im
    turned_im = part_re * twist_im + part_im * twist_re
    second_re, second_im = tables(COLS, COLS, COLS)
    output_real = jnp.einsum(
        "ckm,mj->ckj", turned_re, second_re, precision=exact_mode
    ) - jnp.einsum("ckm,mj->ckj", turned_im, second_im, precision=exact_mode)
    out_im = jnp.einsum("ckm,mj->ckj", turned_re, second_im, precision=exact_mode) + jnp.einsum(
        "ckm,mj->ckj", turned_im, second_re, precision=exact_mode
    )
    return (output_real, out_im)


def inverse_head(spec_re, spec_im, total_len):
    channels = spec_re.shape[0]
    rows_total = spec_re.shape[1]
    second_re, second_im = tables(COLS, COLS, COLS)
    mid_re = jnp.einsum("ckj,jm->ckm", spec_re, second_re, precision=exact_mode) + jnp.einsum(
        "ckj,jm->ckm", spec_im, second_im, precision=exact_mode
    )
    mid_im = jnp.einsum("ckj,jm->ckm", spec_im, second_re, precision=exact_mode) - jnp.einsum(
        "ckj,jm->ckm", spec_re, second_im, precision=exact_mode
    )
    twist_re, twist_im = tables(rows_total, COLS, total_len)
    back_re = mid_re * twist_re + mid_im * twist_im
    back_im = mid_im * twist_re - mid_re * twist_im
    first_re, first_im = tables(rows_total // 2, rows_total, rows_total)
    head = jnp.einsum("nk,ckm->cnm", first_re, back_re, precision=exact_mode) + jnp.einsum(
        "nk,ckm->cnm", first_im, back_im, precision=exact_mode
    )
    return head.reshape(channels, -1) / total_len


def complex_product(left_re, left_im, right_re, right_im):
    return (left_re * right_re - left_im * right_im, left_re * right_im + left_im * right_re)


def shards(features, short_taps, filters, skip):
    rows = features.shape[2]
    rim_tail = features[:, :, rows - (TAPS - 1) :]
    before = shifted(rim_tail, ("half", "ctx"), 1)
    extended = jnp.concatenate([before, features], axis=2).astype(jnp.float32)
    shaped = jnp.zeros(features.shape, jnp.float32)
    for offset in range(TAPS):
        start = TAPS - 1 - offset
        shaped = shaped + short_taps[offset][:, :, None] * extended[:, :, start : start + rows]
    query = shaped[0]
    gated = shaped[1] * shaped[2]
    ctx_place = lax.axis_index("ctx")
    half_place = lax.axis_index("half")
    channel_block = lax.all_to_all(gated, "ctx", split_axis=0, concat_axis=1, tiled=True)
    per_dev = channel_block.shape[0]
    half_len = channel_block.shape[1]
    total_len = 2 * half_len
    rows_total = total_len // COLS
    skip_part = lax.dynamic_slice_in_dim(skip, ctx_place * per_dev, per_dev)
    own_re, own_im = forward_spectrum(channel_block, total_len)
    low_re, low_im = forward_spectrum(filters[:, :half_len], total_len)
    base_re, base_im = complex_product(own_re, own_im, low_re, low_im)
    parity = (1 - 2 * (lax.broadcasted_iota(jnp.int32, (rows_total,), 0) % 2)).astype(jnp.float32)[
        None, :, None
    ]

    def shifted_cross(spec_re, spec_im):
        full_re, full_im = forward_spectrum(filters, total_len)
        cross_re, cross_imaginary = complex_product(spec_re, spec_im, full_re, full_im)
        return (parity * cross_re, parity * cross_imaginary)

    def empty_pair():
        return (jnp.zeros_like(base_re), jnp.zeros_like(base_im))

    arrived = shifted(jnp.stack([own_re, own_im]), "half", 1)
    extra_re, extra_im = lax.cond(
        half_place > 0, lambda: shifted_cross(arrived[0], arrived[1]), empty_pair
    )
    linear = inverse_head(base_re + extra_re, base_im + extra_im, total_len)
    convolved = (linear + skip_part[:, None] * channel_block).astype(jnp.bfloat16)
    result_output = lax.all_to_all(convolved, "ctx", split_axis=1, concat_axis=0, tiled=True)
    return (query * result_output.astype(jnp.float32)).astype(jnp.bfloat16)


def solution(mesh):
    in_specs = (P("seq", None, ("half", "ctx")), P(), P("ctx", None), P())
    out_specs = P("seq", ("half", "ctx"))
    return jax.shard_map(shards, mesh=mesh, in_specs=in_specs, out_specs=out_specs, check_vma=False)
```

profile of v0, /device:TPU:1, one launch (start us, length us, event | category | flops | bytes accessed | tf_op | source)
XLA Modules:
  0.0 172.3 jit_solution(13896046182525165041)
XLA Ops:
  0.0 1.2 slice.64
  1.2 4.4 %collective-permute-start = (bf16[3,512,6]{2,1,0:T(8,128)(2,1)S(1)}, bf16[3,512,6]{2,1,0:T(8,128)(2,1)S(1)}, u32[]{:S(2)}, u32[]{:S(2)}) collective-permute-start(bf16[3,512,6]{2,1,0:T(8,128)(2,1)S(1)} %slice.64), channel_id=1, source_target_pairs={{0,1},{1,2},{2,3},{3,4},{4,5},{5,6},{6,7},{7,8},{8,9},{9,10},{10,1... | collective-permute-start | bytes 55304 | tf_op jit(solution)/shard_map/ppermute | solution.py:18
  5.6 1.2 fusion.271
  6.8 11.1 %collective-permute-done = bf16[3,512,6]{2,1,0:T(8,128)(2,1)S(1)} collective-permute-done((bf16[3,512,6]{2,1,0:T(8,128)(2,1)S(1)}, bf16[3,512,6]{2,1,0:T(8,128)(2,1)S(1)}, u32[]{:S(2)}, u32[]{:S(2)}) %collective-permute-start) | collective-permute-done | bytes 18464 | tf_op jit(solution)/shard_map/ppermute | solution.py:18
  18.0 2.3 %maximum_convert_fusion = f32[3,512,518]{2,1,0:T(8,128)S(1)} fusion(bf16[3,512,512]{2,1,0:T(8,128)(2,1)} %param.6, bf16[3,512,6]{2,1,0:T(8,128)(2,1)S(1)} %collective-permute-done), kind=kLoop, calls=%fused_computation.126 | loop fusion | flops 3182592 | bytes 4773888 | tf_op jit(solution)/shard_map/convert_element_type | solution.py:77
  20.2 7.0 %fusion.79 = f32[3,512,512]{2,1,0:T(8,128)S(1)} fusion(f32[3,512,518]{2,1,0:T(8,128)S(1)} %maximum_convert_fusion, f32[3,512]{1,0:T(4,128)S(1)} %get-tuple-element.33, f32[3,512]{1,0:T(4,128)S(1)} %get-tuple-element.34, f32[3,512]{1,0:T(4,128)S(1)} %get-tuple-element.35, f32[3,512]{1,0:T(4,128)S(1)} %get-tuple-element.36, ...), kind=kLoop, calls=%fused_computation.88 | loop fusion | flops 10223616 | bytes 25208832 | tf_op jit(solution)/shard_map/add | solution.py:81
  27.3 1.7 copy-done.1
  29.0 1.2 slice_multiply_fusion.7
  30.2 8.9 %all-to-all-start = ((f32[32,16,512]{2,1,0:T(8,128)}), f32[32,16,512]{2,1,0:T(8,128)S(1)}, u32[]{:S(2)}, u32[]{:S(2)}) async-start(f32[32,16,512]{2,1,0:T(8,128)} %bitcast.11), calls=%async_computation | async-start | bytes 2097152 | tf_op jit(solution)/shard_map/all_to_all | solution.py:86
  39.7 0.5 copy-done.5
  40.3 22.8 %all-to-all-done = f32[32,16,512]{2,1,0:T(8,128)S(1)} async-done(((f32[32,16,512]{2,1,0:T(8,128)}), f32[32,16,512]{2,1,0:T(8,128)S(1)}, u32[]{:S(2)}, u32[]{:S(2)}) %all-to-all-start) | async-done | bytes 1048608 | tf_op jit(solution)/shard_map/all_to_all | solution.py:86
  63.1 1.0 copy-done.2
  64.1 0.6 copy.28
  64.8 2.3 %fusion.142 = f32[16,128,256]{2,1,0:T(8,128)S(1)} fusion(f32[16,128,128]{2,1,0:T(8,128)S(1)} %reshape.123), kind=kOutput, calls=%fused_computation.168 | convolution fusion | flops 805797888 | bytes 3145728 | tf_op jit(solution)/shard_map/kr,crm->ckm/dot_general | solution.py:35
  67.1 2.3 %fusion.146 = f32[16,128,256]{2,1,0:T(8,128)S(1)} fusion(f32[16,128,128]{2,1,0:T(8,128)S(1)} %reshape.123), kind=kOutput, calls=%fused_computation.172 | convolution fusion | flops 805765120 | bytes 3145728 | tf_op jit(solution)/shard_map/kr,crm->ckm/dot_general | solution.py:34
  69.4 3.8 %fusion.129 = f32[16,256,128]{2,1,0:T(8,128)S(1)} fusion(f32[16,128,256]{2,1,0:T(8,128)S(1)} %fusion.142, f32[16,128,256]{2,1,0:T(8,128)S(1)} %fusion.146, f32[256,128]{0,1:T(8,128)S(1)} %copy.32, f32[256,128]{0,1:T(8,128)S(1)} %copy.30), kind=kOutput, calls=%fused_computation.148 | convolution fusion | flops 807108608 | bytes 6553600 | tf_op jit(solution)/shard_map/ckm,mj->ckj/dot_general | solution.py:40
  73.2 4.0 %fusion.127 = f32[16,256,128]{2,1,0:T(8,128)S(1)} fusion(f32[16,128,256]{2,1,0:T(8,128)S(1)} %fusion.142, f32[16,128,256]{2,1,0:T(8,128)S(1)} %fusion.146, f32[256,128]{0,1:T(8,128)S(1)} %copy.32, f32[256,128]{0,1:T(8,128)S(1)} %copy.30), kind=kOutput, calls=%fused_computation.147 | convolution fusion | flops 807124992 | bytes 6553600 | tf_op jit(solution)/shard_map/ckm,mj->ckj/dot_general | solution.py:43
  77.2 3.8 %convolution_subtract_fusion.1 = f32[16,256,128]{2,1,0:T(8,128)S(1)} fusion(f32[16,256,128]{2,1,0:T(8,128)S(1)} %fusion.129, f32[16,128,256]{2,1,0:T(8,128)S(1)} %fusion.142, f32[16,128,256]{2,1,0:T(8,128)S(1)} %fusion.146, f32[256,128]{0,1:T(8,128)S(1)} %copy.32, f32[256,128]{0,1:T(8,128)S(1)} %copy.30), kind=kOutput, calls=%fused_computation.132 | convolution fusion | flops 807649280 | bytes 8650752 | tf_op jit(solution)/shard_map/ckm,mj->ckj/dot_general | solution.py:42
  81.0 3.8 %convolution_add_fusion.1 = f32[16,256,128]{2,1,0:T(8,128)S(1)} fusion(f32[16,256,128]{2,1,0:T(8,128)S(1)} %fusion.127, f32[16,128,256]{2,1,0:T(8,128)S(1)} %fusion.142, f32[16,128,256]{2,1,0:T(8,128)S(1)} %fusion.146, f32[256,128]{0,1:T(8,128)S(1)} %copy.32, f32[256,128]{0,1:T(8,128)S(1)} %copy.30), kind=kOutput, calls=%fused_computation.131 | convolution fusion | flops 807632896 | bytes 8650752 | tf_op jit(solution)/shard_map/ckm,mj->ckj/dot_general | solution.py:43
  84.9 2.5 %pad_maximum_fusion = f32[2,16,256,128]{3,2,1,0:T(8,128)} fusion(f32[1,16,256,128]{3,2,1,0:T(8,128)S(1)} %bitcast.182, f32[1,16,256,128]{3,2,1,0:T(8,128)S(1)} %bitcast.181), kind=kLoop, calls=%fused_computation.86 | loop fusion | flops 1048576 | bytes 8388608 | tf_op jit(solution)/shard_map/stack | solution.py:107
  87.5 1.7 collective-permute-start.1
  89.2 1.3 slice_bitcast_fusion.1
  90.7 0.8 dynamic_slice.3
  91.5 2.3 %fusion.140 = f32[256,16,128]{2,0,1:T(8,128)S(1)} fusion(f32[16,128,128]{2,1,0:T(8,128)S(1)} %bitcast.183), kind=kOutput, calls=%fused_computation.166 | convolution fusion | flops 805797888 | bytes 3145728 | tf_op jit(solution)/shard_map/kr,crm->ckm/dot_general | solution.py:35
  93.8 2.3 %fusion.144 = f32[256,16,128]{2,0,1:T(8,128)S(1)} fusion(f32[16,128,128]{2,1,0:T(8,128)S(1)} %bitcast.184), kind=kOutput, calls=%fused_computation.170 | convolution fusion | flops 805765120 | bytes 3145728 | tf_op jit(solution)/shard_map/kr,crm->ckm/dot_general | solution.py:34
  96.1 2.2 %fusion.87 = f32[16,256,128]{2,1,0:T(8,128)S(1)} fusion(f32[256,16,128]{2,0,1:T(8,128)S(1)} %fusion.140, f32[256,16,128]{2,0,1:T(8,128)S(1)} %fusion.144, f32[256,128]{1,0:T(8,128)S(1)} %get-tuple-element.39, f32[256,128]{1,0:T(8,128)S(1)} %copy-done.6), kind=kOutput, calls=%fused_computation.102 | convolution fusion | flops 807124992 | bytes 6553600 | tf_op jit(solution)/shard_map/ckm,mj->ckj/dot_general | solution.py:42
  98.3 2.2 %fusion.85 = f32[16,256,128]{2,1,0:T(8,128)S(1)} fusion(f32[256,16,128]{2,0,1:T(8,128)S(1)} %fusion.140, f32[256,16,128]{2,0,1:T(8,128)S(1)} %fusion.144, f32[256,128]{1,0:T(8,128)S(1)} %get-tuple-element.39, f32[256,128]{1,0:T(8,128)S(1)} %copy-done.6), kind=kOutput, calls=%fused_computation.100 | convolution fusion | flops 807108608 | bytes 6553600 | tf_op jit(solution)/shard_map/ckm,mj->ckj/dot_general | solution.py:43
  100.5 3.6 %fusion.103 = f32[16,256,128]{2,1,0:T(8,128)} fusion(f32[16,256,128]{2,1,0:T(8,128)S(1)} %fusion.87, f32[256,16,128]{2,0,1:T(8,128)S(1)} %fusion.140, f32[256,16,128]{2,0,1:T(8,128)S(1)} %fusion.144, f32[256,128]{1,0:T(8,128)S(1)} %get-tuple-element.39, f32[256,128]{1,0:T(8,128)S(1)} %copy-done.6), kind=kOutput, calls=%fused_computation.127 | convolution fusion | flops 807632896 | bytes 8650752 | tf_op jit(solution)/shard_map/ckm,mj->ckj/dot_general | solution.py:40
  104.1 3.8 %fusion.106 = f32[16,256,128]{2,1,0:T(8,128)} fusion(f32[16,256,128]{2,1,0:T(8,128)S(1)} %fusion.85, f32[256,16,128]{2,0,1:T(8,128)S(1)} %fusion.140, f32[256,16,128]{2,0,1:T(8,128)S(1)} %fusion.144, f32[256,128]{1,0:T(8,128)S(1)} %get-tuple-element.39, f32[256,128]{1,0:T(8,128)S(1)} %copy-done.6), kind=kOutput, calls=%fused_computation.128 | convolution fusion | flops 807649280 | bytes 8650752 | tf_op jit(solution)/shard_map/ckm,mj->ckj/dot_general | solution.py:43
  108.0 19.4 %conditional.1 = (f32[16,256,128]{2,1,0:T(8,128)S(1)}, f32[16,256,128]{2,1,0:T(8,128)}) conditional(s32[]{:T(128)} %convert_element_type.144, () %tuple.13, (f32[1,256,1]{1,2,0:T(1,128)S(1)}, f32[1,256,1]{1,2,0:T(1,128)S(1)}, f32[2,16,256,128]{3,2,1,0:T(8,128)}, f32[16,32768]{1,0:T(8,128)S(1)}) %tuple.30), branch_computations={%region_0.1_spmd, %region_1.2_spmd} | conditional | flops 6457327616 | bytes 51644432 | solution.py:108
  108.4 2.9 %fusion.21 = f32[256,16,128]{2,0,1:T(8,128)S(1)} fusion(f32[16,256,128]{2,1,0:T(8,128)S(1)} %bitcast.179), kind=kOutput, calls=%fused_computation.26 | convolution fusion | flops 1611595776 | bytes 4194304 | tf_op jit(solution)/shard_map/cond/branch_1_fun/kr,crm->ckm/dot_general | solution.py:35
  111.3 2.9 %fusion.23 = f32[256,16,128]{2,0,1:T(8,128)S(1)} fusion(f32[16,256,128]{2,1,0:T(8,128)S(1)} %bitcast.180), kind=kOutput, calls=%fused_computation.28 | convolution fusion | flops 1611530240 | bytes 4194304 | tf_op jit(solution)/shard_map/cond/branch_1_fun/kr,crm->ckm/dot_general | solution.py:34
  114.7 2.2 %fusion.4 = f32[16,256,128]{2,1,0:T(8,128)S(1)} fusion(f32[256,16,128]{2,0,1:T(8,128)S(1)} %fusion.21, f32[256,16,128]{2,0,1:T(8,128)S(1)} %fusion.23, f32[256,128]{1,0:T(8,128)S(1)} %get-tuple-element.22, f32[256,128]{1,0:T(8,128)S(1)} %get-tuple-element.23), kind=kOutput, calls=%fused_computation.6 | convolution fusion | flops 807108608 | bytes 6553600 | tf_op jit(solution)/shard_map/cond/branch_1_fun/ckm,mj->ckj/dot_general | solution.py:43
  116.9 2.3 %fusion.15 = f32[16,256,128]{2,1,0:T(8,128)S(1)} fusion(f32[16,256,128]{2,1,0:T(8,128)S(1)} %fusion.4, f32[256,16,128]{2,0,1:T(8,128)S(1)} %fusion.21, f32[256,16,128]{2,0,1:T(8,128)S(1)} %fusion.23, f32[256,128]{1,0:T(8,128)S(1)} %get-tuple-element.22, f32[256,128]{1,0:T(8,128)S(1)} %get-tuple-element.23), kind=kOutput, calls=%fused_computation.19 | convolution fusion | flops 807649280 | bytes 8650752 | tf_op jit(solution)/shard_map/cond/branch_1_fun/ckm,mj->ckj/dot_general | solution.py:43
  119.3 2.2 %fusion.6 = f32[16,256,128]{2,1,0:T(8,128)S(1)} fusion(f32[256,16,128]{2,0,1:T(8,128)S(1)} %fusion.21, f32[256,16,128]{2,0,1:T(8,128)S(1)} %fusion.23, f32[256,128]{1,0:T(8,128)S(1)} %get-tuple-element.22, f32[256,128]{1,0:T(8,128)S(1)} %get-tuple-element.23), kind=kOutput, calls=%fused_computation.8 | convolution fusion | flops 807124992 | bytes 6553600 | tf_op jit(solution)/shard_map/cond/branch_1_fun/ckm,mj->ckj/dot_general | solution.py:42
  121.5 5.7 %fusion.3 = (f32[16,256,128]{2,1,0:T(8,128)}, f32[16,256,128]{2,1,0:T(8,128)S(1)}) fusion(f32[16,256,128]{2,1,0:T(8,128)S(1)} %fusion.15, f32[2,16,256,128]{3,2,1,0:T(8,128)} %get-tuple-element.13, f32[256]{0:T(256)S(1)} %bitcast.188, f32[256]{0:T(256)S(1)} %bitcast.189, f32[16,256,128]{2,1,0:T(8,128)S(1)} %fusion.6, f32[256,16,128]{2,0,1:T(8,128)S(1)} %fusion.21, ...), kind=kOutput, calls=%fused_computation.5 | convolution fusion | flops 811827200 | bytes 17041408 | tf_op jit(solution)/shard_map/cond/branch_1_fun/ckm,mj->ckj/dot_general | solution.py:40
  127.4 1.3 copy-done.4
  128.7 5.3 %subtract_add_fusion = (f32[16,256,128]{2,1,0:T(8,128)S(1)}, f32[16,256,128]{2,1,0:T(8,128)S(1)}) fusion(f32[16,256,128]{2,1,0:T(8,128)} %copy-done.4, f32[16,256,128]{2,1,0:T(8,128)} %copy-done, f32[16,256,128]{2,1,0:T(8,128)} %fusion.106, f32[16,256,128]{2,1,0:T(8,128)S(1)} %convolution_subtract_fusion.1, f32[16,256,128]{2,1,0:T(8,128)} %fusion.103, ...), kind=kLoop, calls=%fused_computation.123 | loop fusion | flops 4194304 | bytes 16777216 | tf_op jit(solution)/shard_map/add | solution.py:111
  134.0 2.2 %fusion.164 = f32[16,256,128]{1,2,0:T(8,128)S(1)} fusion(f32[16,256,128]{2,1,0:T(8,128)S(1)} %get-tuple-element.24), kind=kOutput, calls=%fused_computation.196 | convolution fusion | flops 805552128 | bytes 4194304 | tf_op jit(solution)/shard_map/ckj,jm->ckm/dot_general | solution.py:56
  136.2 2.2 %fusion.166 = f32[16,256,128]{1,2,0:T(8,128)S(1)} fusion(f32[16,256,128]{2,1,0:T(8,128)S(1)} %get-tuple-element.25), kind=kOutput, calls=%fused_computation.198 | convolution fusion | flops 805552128 | bytes 4194304 | tf_op jit(solution)/shard_map/ckj,jm->ckm/dot_general | solution.py:53
  138.5 2.3 %convolution_subtract_fusion = f32[16,256,128]{1,2,0:T(8,128)S(1)} fusion(f32[16,256,128]{1,2,0:T(8,128)S(1)} %fusion.164, f32[16,256,128]{2,1,0:T(8,128)S(1)} %get-tuple-element.25), kind=kOutput, calls=%fused_computation.129 | convolution fusion | flops 806060032 | bytes 6291456 | tf_op jit(solution)/shard_map/ckj,jm->ckm/dot_general | solution.py:56
  140.8 2.3 %convolution_add_fusion = f32[16,256,128]{1,2,0:T(8,128)S(1)} fusion(f32[16,256,128]{1,2,0:T(8,128)S(1)} %fusion.166, f32[16,256,128]{2,1,0:T(8,128)S(1)} %get-tuple-element.24), kind=kOutput, calls=%fused_computation.130 | convolution fusion | flops 806060032 | bytes 6291456 | tf_op jit(solution)/shard_map/ckj,jm->ckm/dot_general | solution.py:53
  143.1 2.7 %fusion.95 = f32[16,128,128]{2,1,0:T(8,128)S(1)} fusion(f32[16,256,128]{1,2,0:T(8,128)S(1)} %convolution_add_fusion, f32[16,256,128]{1,2,0:T(8,128)S(1)} %convolution_subtract_fusion, f32[256,128]{0,1:T(8,128)S(1)} %copy.32, f32[256,128]{0,1:T(8,128)S(1)} %copy.30), kind=kOutput, calls=%fused_computation.114 | convolution fusion | flops 807370752 | bytes 5505024 | tf_op jit(solution)/shard_map/nk,ckm->cnm/dot_general | solution.py:63
  145.7 2.4 %fusion.115 = f32[16,128,128]{1,2,0:T(8,128)S(1)} fusion(f32[16,128,128]{2,1,0:T(8,128)S(1)} %fusion.95, f32[16,256,128]{1,2,0:T(8,128)S(1)} %convolution_subtract_fusion, f32[16,256,128]{1,2,0:T(8,128)S(1)} %convolution_add_fusion, f32[256,128]{0,1:T(8,128)S(1)} %copy.32, f32[256,128]{0,1:T(8,128)S(1)} %copy.30), kind=kOutput, calls=%fused_computation.135 | convolution fusion | flops 807862272 | bytes 6553600 | tf_op jit(solution)/shard_map/nk,ckm->cnm/dot_general | solution.py:63
  148.7 0.7 copy-done.3
  149.4 0.7 fusion.120
  150.1 19.6 %all_to_all.23 = bf16[16,32,512]{2,0,1:T(8,128)(2,1)S(1)} all-to-all(bf16[16,32,512]{2,0,1:T(8,128)(2,1)S(1)} %fusion.120), channel_id=1, replica_groups=mesh['seq'=4,'half'=2,'ctx'=32] {'ctx'}, dimensions={1} | all-to-all | bytes 1048576 | tf_op jit(solution)/shard_map/all_to_all | solution.py:113
  169.7 2.2 %fusion.119 = bf16[512,512]{1,0:T(8,128)(2,1)} fusion(f32[3,512,512]{2,1,0:T(8,128)} %copy-done.1, bf16[16,32,512]{2,0,1:T(8,128)(2,1)S(1)} %all_to_all.23), kind=kLoop, calls=%fused_computation.139 | loop fusion | flops 786432 | bytes 2097152 | tf_op jit(solution)/shard_map/convert_element_type | solution.py:114
  (26 shorter events, 2.7 us)
Async XLA Ops:
  1.2 16.8 %collective-permute-start = (bf16[3,512,6]{2,1,0:T(8,128)(2,1)S(1)}, bf16[3,512,6]{2,1,0:T(8,128)(2,1)S(1)}, u32[]{:S(2)}, u32[]{:S(2)}) collective-permute-start(bf16[3,512,6]{2,1,0:T(8,128)(2,1)S(1)} %slice.64), channel_id=1, source_target_pairs={{0,1},{1,2},{2,3},{3,4},{4,5},{5,6},{6,7},{7,8},{8,9},{9,10},{10,1... | collective-permute-start | bytes 55304 | tf_op jit(solution)/shard_map/ppermute | solution.py:18
  27.3 1.7 copy-start.1
  30.2 33.0 %all-to-all-start = ((f32[32,16,512]{2,1,0:T(8,128)}), f32[32,16,512]{2,1,0:T(8,128)S(1)}, u32[]{:S(2)}, u32[]{:S(2)}) async-start(f32[32,16,512]{2,1,0:T(8,128)} %bitcast.11), calls=%async_computation | async-start | bytes 2097152 | tf_op jit(solution)/shard_map/all_to_all | solution.py:86
  39.6 0.7 copy-start.5
  63.1 1.0 copy-start.2
  84.9 2.6 %copy-start = (f32[16,256,128]{2,1,0:T(8,128)}, f32[16,256,128]{2,1,0:T(8,128)S(1)}, u32[]{:S(2)}) copy-start(f32[16,256,128]{2,1,0:T(8,128)S(1)} %convolution_add_fusion.1) | copy-start | bytes 6291460
  87.5 20.5 %collective-permute-start.1 = (f32[2,16,256,128]{3,2,1,0:T(8,128)}, f32[2,16,256,128]{3,2,1,0:T(8,128)}, u32[]{:S(2)}, u32[]{:S(2)}) collective-permute-start(f32[2,16,256,128]{3,2,1,0:T(8,128)} %pad_maximum_fusion), channel_id=1, source_target_pairs={{0,32},{1,33},{2,34},{3,35},{4,36},{5,37},{6,38},{7,39},{8,40},{9,... | collective-permute-start | bytes 12582920 | tf_op jit(solution)/shard_map/ppermute | solution.py:18
  93.8 2.3 %copy-start.6 = (f32[256,128]{1,0:T(8,128)S(1)}, f32[256,128]{1,0:T(8,128)}, u32[]{:S(2)}) copy-start(f32[256,128]{1,0:T(8,128)} %copy-done.5) | copy-start | bytes 393220
  104.1 3.8 %copy-start.7 = (f32[16,32768]{1,0:T(8,128)S(1)}, f32[16,32768]{1,0:T(8,128)}, u32[]{:S(2)}) copy-start(f32[16,32768]{1,0:T(8,128)} %param.8) | copy-start | bytes 6291460
  127.4 1.3 copy-start.4
  148.2 1.2 copy-start.3
where the time goes:
time: 176 us; the launch traced here: 172 us
  matrix products  68.8 us (39%)
  waiting for transfers between devices  33.9 us (19%)
  other arithmetic  22.2 us (13%)
  blocking collectives  19.6 us (11%)
  starting transfers between devices  14.9 us (8%)
  local copies, waits for them, and re-layouts  11.9 us (7%)
    all_to_all x1, waiting for transfers between devices, shards(): lax.all_to_all(gated, 'ctx', split_axis=0, concat_axis=1, tiled=True)  22.8 us
    all_to_all x1, blocking collectives, shards(): lax.all_to_all(convolved, 'ctx', split_axis=1, concat_axis=0, tiled=True)  19.6 us
    dot_general x3, matrix products, forward_spectrum(): jnp.einsum('ckm,mj->ckj', turned_re, second_re, precision=exact_mode)  13.1 us
    ppermute x2, waiting for transfers between devices, shifted(): return lax.ppermute(x, axis, pairs)  11.1 us
    dot_general x3, matrix products, forward_spectrum(): jnp.einsum('ckm,mj->ckj', turned_re, second_im, precision=exact_mode)  10.1 us
    all_to_all x1, starting transfers between devices, shards(): lax.all_to_all(gated, 'ctx', split_axis=0, concat_axis=1, tiled=True)  8.87 us
    dot_general x3, matrix products, forward_spectrum(): jnp.einsum('ckm,mj->ckj', turned_im, second_im, precision=exact_mode)  8.25 us
    dot_general x3, matrix products, forward_spectrum(): jnp.einsum('ckm,mj->ckj', turned_im, second_re, precision=exact_mode)  8.22 us
  transfers between devices with their start and end apart: 3, of which 2 were waited for; matrix products, arithmetic and copies ran while one was open for 12% of the time, Pallas kernels for 0%

commit v1 on v0

v1 whole, which is shorter than its diff:
```python
import math

import jax
import jax.numpy as jnp
import ml_dtypes
import numpy as np
from jax import lax
from jax.experimental import pallas as pl
from jax.experimental.pallas import tpu as pltpu
from jax.sharding import PartitionSpec as P

TAPS = 7
EDGE = TAPS - 1
LANES = 128
N1 = 256
N2 = 128
TOTAL = N1 * N2
F32 = jnp.float32
BF16 = jnp.bfloat16


def halves(table):
    hi = table.astype(ml_dtypes.bfloat16)
    lo = (table - hi.astype(np.float64)).astype(ml_dtypes.bfloat16)
    return hi, lo


def transform_tables():
    k1 = np.arange(N1) + 0.25
    first = np.exp(-2j * np.pi * np.outer(k1, np.arange(N1)) / N1)
    twist = np.exp(-2j * np.pi * np.outer(k1, np.arange(N2)) / TOTAL)
    second = np.exp(-2j * np.pi * np.outer(np.arange(N2), np.arange(N2)) / N2)
    rows = np.concatenate([first.real, first.imag], 0)
    forward = np.block([[second.real, second.imag], [-second.imag, second.real]])
    backward = np.block([[second.real, -second.imag], [second.imag, second.real]])
    back_rows = np.concatenate([first.real.T, first.imag.T], 1)
    return dict(
        rows=halves(rows),
        twist=(twist.real.astype(np.float32), twist.imag.astype(np.float32)),
        forward=halves(forward),
        backward=halves(backward),
        back_rows=halves(back_rows),
    )


def mm(a, b):
    return jnp.dot(a, b, preferred_element_type=F32)


def split(x):
    hi = x.astype(BF16)
    return hi, (x - hi.astype(F32)).astype(BF16)


def mm3(x, whi, wlo):
    hi, lo = split(x)
    return mm(hi, whi) + mm(lo, whi) + mm(hi, wlo)


def twice(x):
    return jnp.concatenate([x, x], 1)


def tap_columns(taps_ref, branch, start, count):
    rows = [taps_ref[j, branch : branch + 1, pl.ds(start, count)] for j in range(TAPS)]
    rows.append(jnp.zeros((1, count), F32))
    return jnp.concatenate(rows, 0).T


GATE_ROWS = 128
STEP = 16


def gate_kernel(taps_ref, k_ref, v_ref, o_ref, ktap, vtap):
    start = pl.multiple_of(pl.program_id(0) * GATE_ROWS, GATE_ROWS)
    ktap[...] = tap_columns(taps_ref, 1, start, GATE_ROWS)
    vtap[...] = tap_columns(taps_ref, 2, start, GATE_ROWS)
    lane = lax.broadcasted_iota(jnp.int32, (STEP, LANES), 1)

    def step(g, carry):
        at = pl.ds(pl.multiple_of(g * STEP, STEP), STEP)
        k = k_ref[0, at, :].astype(F32)
        v = v_ref[0, at, :].astype(F32)
        kt, vt = ktap[at, :], vtap[at, :]

        def shaped(x, taps):
            total = taps[:, 0:1] * x
            for j in range(1, TAPS):
                total = total + taps[:, j : j + 1] * pltpu.roll(x, j, 1)
            return total

        size = k.shape[1]
        o_ref[at, :size] = (shaped(k, kt) * shaped(v, vt)).astype(BF16)

        def edges(x, by):
            ends = jnp.where(lane >= LANES - EDGE, x[:, size - LANES :], x[:, :LANES])
            return pltpu.roll(ends, by, 1)

        o_ref[at, size:] = jnp.where(
            lane < LANES // 2, edges(k, EDGE), edges(v, EDGE + LANES // 2)
        ).astype(BF16)
        return carry

    lax.fori_loop(0, GATE_ROWS // STEP, step, 0, unroll=2)


def gate_call(features, short_taps):
    _, channels, size = features.shape
    return pl.pallas_call(
        gate_kernel,
        grid=(channels // GATE_ROWS,),
        in_specs=[
            pl.BlockSpec(short_taps.shape, lambda g: (0, 0, 0)),
            pl.BlockSpec((1, GATE_ROWS, size), lambda g: (1, g, 0)),
            pl.BlockSpec((1, GATE_ROWS, size), lambda g: (2, g, 0)),
        ],
        out_specs=pl.BlockSpec((GATE_ROWS, size + LANES), lambda g: (g, 0)),
        out_shape=jax.ShapeDtypeStruct((channels, size + LANES), BF16),
        scratch_shapes=[pltpu.VMEM((GATE_ROWS, 8), F32)] * 2,
        cost_estimate=pl.CostEstimate(flops=60 * channels * size, bytes_accessed=6 * channels * size, transcendentals=0),
        name="gate",
    )(short_taps, features, features)


def query_kernel(taps_ref, halo_ref, q_ref, o_ref, qtap, before):
    start = pl.multiple_of(pl.program_id(0) * GATE_ROWS, GATE_ROWS)
    qtap[...] = tap_columns(taps_ref, 0, start, GATE_ROWS)
    halo = halo_ref[...].astype(F32)
    before[...] = jnp.concatenate([jnp.zeros((LANES - EDGE, GATE_ROWS), F32), halo], 0).T

    def step(g, carry):
        at = pl.ds(pl.multiple_of(g * STEP, STEP), STEP)
        x = jnp.concatenate([before[at, :], q_ref[0, at, :].astype(F32)], 1)
        taps = qtap[at, :]
        total = taps[:, 0:1] * x[:, LANES:]
        for j in range(1, TAPS):
            total = total + taps[:, j : j + 1] * pltpu.roll(x, j, 1)[:, LANES:]
        o_ref[at, :] = total
        return carry

    lax.fori_loop(0, GATE_ROWS // STEP, step, 0)


def query_call(features, short_taps, halo):
    _, channels, size = features.shape
    return pl.pallas_call(
        query_kernel,
        grid=(channels // GATE_ROWS,),
        in_specs=[
            pl.BlockSpec(short_taps.shape, lambda g: (0, 0, 0)),
            pl.BlockSpec((EDGE, GATE_ROWS), lambda g: (0, g)),
            pl.BlockSpec((1, GATE_ROWS, size), lambda g: (0, g, 0)),
        ],
        out_specs=pl.BlockSpec((GATE_ROWS, size), lambda g: (g, 0)),
        out_shape=jax.ShapeDtypeStruct((channels, size), F32),
        scratch_shapes=[pltpu.VMEM((GATE_ROWS, 8), F32), pltpu.VMEM((GATE_ROWS, LANES), F32)],
        cost_estimate=pl.CostEstimate(flops=30 * channels * size, bytes_accessed=6 * channels * size, transcendentals=0),
        name="query",
    )(short_taps, halo, features)


def filter_kernel(place_ref, skip_ref, f_ref, rhi, rlo, twr, twi, fhi, flo, o_ref, grid_ref):
    own = f_ref.shape[0]
    for j in range(N1):
        grid_ref[j * own : (j + 1) * own, :] = f_ref[:, j * N2 : (j + 1) * N2]

    def pair(c, carry):
        x = jnp.concatenate([grid_ref[pl.ds(2 * c + a, N1, stride=own), :] for a in range(2)], 1)
        hi, lo = split(x)
        part = mm(rhi[...], hi) + mm(rlo[...], hi) + mm(rhi[...], lo)
        re, im = part[:N1], part[N1:]
        tr, ti = twice(twr[...]), twice(twi[...])
        turned_re, turned_im = re * tr - im * ti, re * ti + im * tr
        for a in range(2):
            at = slice(a * N2, (a + 1) * N2)
            spec = mm3(jnp.concatenate([turned_re[:, at], turned_im[:, at]], 1), fhi[...], flo[...])
            skip = skip_ref[place_ref[1] + 2 * c + a]
            o_ref[2 * c + a, :, :N2] = (spec[:, :N2] + skip) * (1.0 / TOTAL)
            o_ref[2 * c + a, :, N2:] = spec[:, N2:] * (1.0 / TOTAL)
        return carry

    lax.fori_loop(0, own // 2, pair, 0)


def whole(x):
    return pl.BlockSpec(x.shape, lambda *_: (0,) * x.ndim)


def filter_call(filters, skip, half_place, first_channel, own, tables):
    consts = [*tables["rows"], *tables["twist"], *tables["forward"]]
    return pl.pallas_call(
        filter_kernel,
        grid_spec=pltpu.PrefetchScalarGridSpec(
            num_scalar_prefetch=1,
            grid=(1,),
            in_specs=[
                pl.BlockSpec(memory_space=pltpu.SMEM),
                pl.BlockSpec((own, filters.shape[1]), lambda g, place: (place[0], 0)),
                *[whole(c) for c in consts],
            ],
            out_specs=pl.BlockSpec((own, N1, 2 * N2), lambda g, place: (0, 0, 0)),
            scratch_shapes=[pltpu.VMEM((N1 * own, N2), F32)],
        ),
        out_shape=jax.ShapeDtypeStruct((own, N1, 2 * N2), F32),
        compiler_params=pltpu.CompilerParams(vmem_limit_bytes=32 * 1024 * 1024),
        cost_estimate=pl.CostEstimate(flops=12 * own * N1 * N1 * 2 * N2, bytes_accessed=4 << 20, transcendentals=0),
        name="filter_spectrum",
    )(jnp.stack([half_place, first_channel]).astype(jnp.int32), skip, filters, *consts)


def conv_kernel(x_ref, h_ref, taps_ref, rhi, rlo, twr, twi, fhi, flo, bhi, blo, chi, clo, o_ref, grid_ref, edge_ref, res_ref):
    own = h_ref.shape[0]
    blocks = x_ref.shape[0] // own
    size = x_ref.shape[1] - LANES
    tiles = size // LANES
    pairs = blocks // 2

    def unpack(i, carry):
        rows = pl.ds(pl.multiple_of(i * 2 * own, 2 * own), 2 * own)
        for q in range(tiles + 1):
            tile = x_ref[rows, q * LANES : (q + 1) * LANES].astype(F32)
            for h in range(2):
                place = i + h * pairs
                if q < tiles:
                    at, to = place * tiles + q, grid_ref
                else:
                    at, to = place, edge_ref
                to[pl.ds(pl.multiple_of(at * own, own), own), :] = tile[h * own : (h + 1) * own]
        return carry

    lax.fori_loop(0, pairs, unpack, 0, unroll=4)

    lane = lax.broadcasted_iota(jnp.int32, (own, LANES), 1)

    def mend(p, carry):
        here = edge_ref[pl.ds(pl.multiple_of(p * own, own), own), :]
        previous = edge_ref[pl.ds(pl.multiple_of(jnp.maximum(p - 1, 0) * own, own), own), :]
        previous = jnp.where(p > 0, previous, 0.0)
        both = jnp.where(lane % (LANES // 2) < EDGE, previous, here)
        total = taps_ref[0] * both
        for j in range(1, TAPS):
            total = total + taps_ref[j] * pltpu.roll(both, j, 1)
        gated = pltpu.roll(total * pltpu.roll(total, LANES // 2, 1), LANES - EDGE, 1)
        at = pl.ds(pl.multiple_of(p * tiles * own, own), own)
        grid_ref[at, :] = jnp.where(lane < EDGE, gated, grid_ref[at, :])
        return carry

    lax.fori_loop(0, blocks, mend, 0, unroll=8)

    def pair(c, carry):
        x = jnp.concatenate([grid_ref[pl.ds(2 * c + a, N1, stride=own), :] for a in range(2)], 1).astype(BF16)
        part = mm(rhi[...], x) + mm(rlo[...], x)
        re, im = part[:N1], part[N1:]
        tr, ti = twice(twr[...]), twice(twi[...])
        turned_re, turned_im = re * tr - im * ti, re * ti + im * tr
        back_re, back_im = [], []
        for a in range(2):
            at = slice(a * N2, (a + 1) * N2)
            spec = mm3(jnp.concatenate([turned_re[:, at], turned_im[:, at]], 1), fhi[...], flo[...])
            sr, si = spec[:, :N2], spec[:, N2:]
            hr, hi = h_ref[2 * c + a, :, :N2], h_ref[2 * c + a, :, N2:]
            mid = mm3(jnp.concatenate([sr * hr - si * hi, sr * hi + si * hr], 1), bhi[...], blo[...])
            mr, mi = mid[:, :N2], mid[:, N2:]
            back_re.append(mr * twr[...] + mi * twi[...])
            back_im.append(mi * twr[...] - mr * twi[...])
        back = jnp.concatenate([jnp.concatenate(back_re, 1), jnp.concatenate(back_im, 1)], 0)
        hi, lo = split(back)
        y = mm(chi[...], hi) + mm(chi[...], lo) + mm(clo[...], hi)
        for a in range(2):
            res_ref[pl.ds(2 * c + a, N1, stride=own), :] = y[:, a * N2 : (a + 1) * N2]
        return carry

    lax.fori_loop(0, own // 2, pair, 0)

    def pack(i, carry):
        rows = pl.ds(pl.multiple_of(i * 2 * own, 2 * own), 2 * own)
        for q in range(tiles):
            tile = [
                res_ref[pl.ds(pl.multiple_of(((i + h * pairs) * tiles + q) * own, own), own), :] for h in range(2)
            ]
            o_ref[rows, q * LANES : (q + 1) * LANES] = jnp.concatenate(tile, 0).astype(BF16)
        return carry

    lax.fori_loop(0, pairs, pack, 0, unroll=4)


def conv_call(blocks, spectrum, taps, tables):
    own = spectrum.shape[0]
    rows, width = blocks.shape
    args = [
        blocks, spectrum, taps, *tables["rows"], *tables["twist"], *tables["forward"], *tables["backward"],
        *tables["back_rows"],
    ]
    return pl.pallas_call(
        conv_kernel,
        grid=(1,),
        in_specs=[whole(a) for a in args],
        out_specs=pl.BlockSpec((rows, width - LANES), lambda g: (0, 0)),
        out_shape=jax.ShapeDtypeStruct((rows, width - LANES), BF16),
        scratch_shapes=[
            pltpu.VMEM((N1 * own, N2), F32),
            pltpu.VMEM((rows, LANES), F32),
            pltpu.VMEM((N1 * own, N2), F32),
        ],
        compiler_params=pltpu.CompilerParams(vmem_limit_bytes=40 * 1024 * 1024),
        cost_estimate=pl.CostEstimate(flops=22 * own * N1 * N1 * 2 * N2, bytes_accessed=6 << 20, transcendentals=0),
        name="long_convolution",
    )(*args)


def shards(features, short_taps, filters, skip):
    size = features.shape[2]
    positions = lax.axis_size("half") * lax.axis_size("ctx")
    own = filters.shape[0] // lax.axis_size("half")
    half_place, ctx_place = lax.axis_index("half"), lax.axis_index("ctx")
    first_channel = ctx_place * filters.shape[0] + half_place * own
    tables = transform_tables()

    gated = gate_call(features, short_taps)
    blocks = lax.all_to_all(gated, ("ctx", "half"), 0, 0, tiled=True)

    tail = features[0, :, size - EDGE :].T
    halo = lax.ppermute(tail, ("half", "ctx"), [(i, i + 1) for i in range(positions - 1)])
    query = query_call(features, short_taps, halo)
    spectrum = filter_call(filters, skip, half_place, first_channel, own, tables)
    own_taps = lax.dynamic_slice_in_dim(short_taps[:, 1:], first_channel, own, 2)
    own_taps = jnp.repeat(jnp.swapaxes(own_taps, 1, 2), LANES // 2, axis=2)

    convolved = conv_call(blocks, spectrum, own_taps, tables)
    back = lax.all_to_all(convolved, ("ctx", "half"), 0, 0, tiled=True)
    return (query * back.astype(F32)).astype(BF16)


def solution(mesh):
    in_specs = (P("seq", None, ("half", "ctx")), P(), P("ctx", None), P())
    out_specs = P("seq", ("half", "ctx"))
    return jax.shard_map(shards, mesh=mesh, in_specs=in_specs, out_specs=out_specs, check_vma=False)
```

time: 176 us -> 92.3 us (0.52); the launches traced: 172 us -> 91.7 us
  matrix products: 68.8 us -> 0 us
  Pallas kernels: 0 us -> 28.9 us
  other arithmetic: 22.2 us -> 2.25 us
  blocking collectives: 19.6 us -> 0 us
  waiting for transfers between devices: 33.9 us -> 22 us
  starting transfers between devices: 14.9 us -> 22.7 us
  local copies, waits for them, and re-layouts: 11.9 us -> 15.6 us
    dot_general x24 -> x0, matrix products: 68.8 us -> none  [the longest x3 13.1 us: forward_spectrum(): jnp.einsum('ckm,mj->ckj', turned_re, second_re, precision=exact_mode)]
    pallas_call x0 -> x4, Pallas kernels: none -> 28.9 us  [the longest x1 9.66 us: conv_call(): pl.pallas_call(conv_kernel, grid=(1,), in_specs=[whole(a) for a in args],...]
    all_to_all x1 -> x0, blocking collectives: 19.6 us -> none  [shards(): lax.all_to_all(convolved, 'ctx', split_axis=1, concat_axis=0, tiled=True)]
    all_to_all x1 -> x2, waiting for transfers between devices: 22.8 us -> 10.2 us  [the longest x1 10.2 us: shards(): blocks = lax.all_to_all(gated, ('ctx', 'half'), 0, 0, tiled=True)]
    add x2 -> x0, other arithmetic: 12.3 us -> none  [the longest x1 7.04 us: shards(): shaped + short_taps[offset][:, :, None] * extended[:, :, start:start + rows]]
    all_to_all x1 -> x2, starting transfers between devices: 8.87 us -> 19.4 us  [the longest x1 13.2 us: shards(): blocks = lax.all_to_all(gated, ('ctx', 'half'), 0, 0, tiled=True)]
    unnamed x22 -> x38, local copies, waits for them, and re-layouts: 6.96 us -> 14.2 us
    convert_element_type x4 -> x1, other arithmetic: 5.15 us -> 2.18 us  [shards(): return (query * back.astype(F32)).astype(BF16)]
  transfers between devices with their start and end apart: 3 -> 3, of which waited for: 2 -> 2; matrix products, arithmetic and copies ran while one was open for 12% -> 2% of each run, Pallas kernels for 0% -> 13%
where the time goes in v1:
time: 92.3 us; the launch traced here: 91.7 us
  Pallas kernels  28.9 us (31%)
  starting transfers between devices  22.7 us (25%)
  waiting for transfers between devices  22 us (24%)
  local copies, waits for them, and re-layouts  15.6 us (17%)
  other arithmetic  2.25 us (2%)
    unnamed x38, local copies, waits for them, and re-layouts  14.2 us
    all_to_all x1, starting transfers between devices, shards(): blocks = lax.all_to_all(gated, ('ctx', 'half'), 0, 0, tiled=True)  13.2 us
    ppermute x1, waiting for transfers between devices, shards(): lax.ppermute(tail, ('half', 'ctx'), [(i, i + 1) for i in range(positions...  11.9 us
    all_to_all x1, waiting for transfers between devices, shards(): blocks = lax.all_to_all(gated, ('ctx', 'half'), 0, 0, tiled=True)  10.2 us
    pallas_call x1, Pallas kernels, conv_call(): pl.pallas_call(conv_kernel, grid=(1,), in_specs=[whole(a) for a in args],...  9.66 us
    pallas_call x1, Pallas kernels, gate_call(): pl.pallas_call(gate_kernel, grid=(channels // GATE_ROWS,), in_specs=[pl.B...  7.35 us
    pallas_call x1, Pallas kernels, query_call(): pl.pallas_call(query_kernel, grid=(channels // GATE_ROWS,), in_specs=[pl....  6.54 us
    all_to_all x1, starting transfers between devices, shards(): back = lax.all_to_all(convolved, ('ctx', 'half'), 0, 0, tiled=True)  6.26 us
  transfers between devices with their start and end apart: 3, of which 2 were waited for; matrix products, arithmetic and copies ran while one was open for 2% of the time, Pallas kernels for 13%

profile of v1, /device:TPU:1, one launch (start us, length us, event | category | flops | bytes accessed | tf_op | source)
XLA Modules:
  0.0 91.7 jit_solution(14916129577072167975)
XLA Ops:
  0.0 1.5 %copy.16.taps_ref = f32[7,3,512]{2,1,0:T(4,128)} copy(f32[7,3,512]{2,0,1:T(8,128)} %param.15) | data formatting | bytes 86016 | tf_op args[1]
  1.5 0.0 slice-start
  1.5 0.0 copy-start
  1.5 0.0 copy-start.1
  1.5 0.0 copy-start.2
  1.5 0.0 copy-start.3
  1.5 0.0 copy-start.6
  1.5 7.4 %gate.1 = bf16[512,640]{1,0:T(8,128)(2,1)} custom-call(f32[7,3,512]{2,1,0:T(4,128)} %copy.16.taps_ref, bf16[3,512,512]{2,1,0:T(8,128)(2,1)} %v_ref.1, bf16[3,512,512]{2,1,0:T(8,128)(2,1)} %v_ref.1), custom_call_target="tpu_custom_call" | custom-call | flops 15728640 | bytes 1572864 | tf_op jit(solution)/shard_map/gate/pallas_call | solution.py:109
  8.8 13.2 %all-to-all-start = ((bf16[64,8,640]{2,1,0:T(8,128)(2,1)}), bf16[64,8,640]{2,1,0:T(8,128)(2,1)S(1)}, u32[]{:S(2)}, u32[]{:S(2)}) async-start(bf16[64,8,640]{2,1,0:T(8,128)(2,1)} %bitcast.14), calls=%async_computation | async-start | bytes 1310720 | tf_op jit(solution)/shard_map/all_to_all | solution.py:320
  22.0 0.0 slice-done
  22.0 0.1 dynamic-slice_bitcast_fusion
  22.1 0.1 copy.18
  22.2 0.1 broadcast_in_dim.3
  22.3 0.1 reshape.9.taps_ref
  22.4 0.1 pad_add_fusion.place_ref
  22.5 0.0 copy-done
  22.5 0.0 copy-done.1
  22.5 0.0 copy-done.2
  22.5 0.0 copy-done.3
  22.5 0.0 copy-done.6
  22.6 0.0 copy-start.7
  22.6 0.9 copy-done.7
  23.5 0.0 copy-start.9
  23.5 0.9 copy-done.9
  24.4 0.0 copy-start.11
  24.4 0.9 copy-done.11
  25.3 5.4 %filter_spectrum.1.h_ref = f32[8,256,256]{2,1,0:T(8,128)S(1)} custom-call(s32[2]{0:T(128)S(1)} %pad_add_fusion.place_ref, f32[512]{0:T(512)S(1)} %copy-done.1, f32[16,32768]{1,0:T(8,128)S(1)} %copy-done, bf16[512,256]{1,0:T(8,128)(2,1)S(1)} %copy-done.2, bf16[512,256]{1,0:T(8,128)(2,1)S(1)} %copy-done.3, f32[256,128]{1,0:T(8,128)S(1)} %copy-done.6, ...), custom_call_target="tpu_custom_call" | custom-call | flops 1610612736 | bytes 4194304 | tf_op jit(solution)/shard_map/filter_spectrum/pallas_call | solution.py:191
  30.6 0.0 copy-start.15
  30.7 1.3 %copy-done.15 = f32[8,256,256]{2,1,0:T(8,128)} copy-done((f32[8,256,256]{2,1,0:T(8,128)}, f32[8,256,256]{2,1,0:T(8,128)S(1)}, u32[]{:S(2)}) %copy-start.15) | copy-done | bytes 2097176
  32.0 10.2 %all-to-all-done = bf16[64,8,640]{2,1,0:T(8,128)(2,1)S(1)} async-done(((bf16[64,8,640]{2,1,0:T(8,128)(2,1)}), bf16[64,8,640]{2,1,0:T(8,128)(2,1)S(1)}, u32[]{:S(2)}, u32[]{:S(2)}) %all-to-all-start) | async-done | bytes 655392 | tf_op jit(solution)/shard_map/all_to_all | solution.py:320
  42.1 0.9 %copy-done.4 = bf16[256,512]{1,0:T(8,128)(2,1)S(1)} copy-done((bf16[256,512]{1,0:T(8,128)(2,1)S(1)}, bf16[256,512]{1,0:T(8,128)(2,1)}, u32[]{:S(2)}) %copy-start.4) | copy-done | bytes 262168
  43.1 0.9 %copy-done.5 = bf16[256,512]{1,0:T(8,128)(2,1)S(1)} copy-done((bf16[256,512]{1,0:T(8,128)(2,1)S(1)}, bf16[256,512]{1,0:T(8,128)(2,1)}, u32[]{:S(2)}) %copy-start.5) | copy-done | bytes 262168
  44.0 0.9 copy-done.8
  44.9 0.9 copy-done.10
  45.9 0.9 copy-done.12
  46.8 0.9 copy-done.13
  47.7 0.9 copy-done.14
  48.6 1.6 %copy-done.16 = f32[8,256,256]{2,1,0:T(8,128)S(1)} copy-done((f32[8,256,256]{2,1,0:T(8,128)S(1)}, f32[8,256,256]{2,1,0:T(8,128)}, u32[]{:S(2)}) %copy-start.16) | copy-done | bytes 2097176
  50.2 9.7 %long_convolution.1 = bf16[512,512]{1,0:T(8,128)(2,1)} custom-call(bf16[512,640]{1,0:T(8,128)(2,1)S(1)} %bitcast.13, f32[8,256,256]{2,1,0:T(8,128)S(1)} %copy-done.16, f32[7,8,128]{2,1,0:T(8,128)S(1)} %reshape.9.taps_ref, bf16[512,256]{1,0:T(8,128)(2,1)S(1)} %copy-done.2, bf16[512,256]{1,0:T(8,128)(2,1)S(1)} %copy-done.3, f32[256,128]{1,0:T(8,128)S(1)} %copy-done.6, ...), custom_call_target="tpu_custom_call" | custom-call | flops 2952790016 | bytes 6291456 | tf_op jit(solution)/shard_map/long_convolution/pallas_call | solution.py:294
  59.8 6.3 %all-to-all-start.1 = ((bf16[64,8,512]{2,1,0:T(8,128)(2,1)}), bf16[64,8,512]{2,1,0:T(8,128)(2,1)S(1)}, u32[]{:S(2)}, u32[]{:S(2)}) async-start(bf16[64,8,512]{2,1,0:T(8,128)(2,1)} %bitcast.7), calls=%async_computation.1 | async-start | bytes 1048576 | tf_op jit(solution)/shard_map/all_to_all | solution.py:330
  66.1 1.0 %slice.6 = bf16[1,512,6]{2,1,0:T(8,128)(2,1)S(1)} slice(bf16[3,512,512]{2,1,0:T(8,128)(2,1)} %v_ref.1), slice={[0:1], [0:512], [506:512]} | slice | bytes 12288 | tf_op jit(solution)/shard_map/slice | solution.py:322
  67.1 0.1 copy.19
  67.2 3.3 %collective-permute-start = (bf16[6,512]{1,0:T(8,128)(2,1)S(1)}, bf16[6,512]{1,0:T(8,128)(2,1)S(1)}, u32[]{:S(2)}, u32[]{:S(2)}) collective-permute-start(bf16[6,512]{1,0:T(8,128)(2,1)S(1)} %bitcast.15), channel_id=1, source_target_pairs={{0,1},{1,2},{2,3},{3,4},{4,5},{5,6},{6,7},{7,8},{8,9},{9,10},{10,1... | collective-permute-start | bytes 18440 | tf_op jit(solution)/shard_map/ppermute | solution.py:323
  70.5 11.9 %collective-permute-done.halo_ref = bf16[6,512]{1,0:T(8,128)(2,1)S(1)} collective-permute-done((bf16[6,512]{1,0:T(8,128)(2,1)S(1)}, bf16[6,512]{1,0:T(8,128)(2,1)S(1)}, u32[]{:S(2)}, u32[]{:S(2)}) %collective-permute-start) | collective-permute-done | bytes 6176 | tf_op jit(solution)/shard_map/ppermute | solution.py:323
  82.4 0.6 copy-done.17
  83.0 6.5 %query.1 = f32[512,512]{1,0:T(8,128)} custom-call(f32[7,3,512]{2,1,0:T(4,128)} %copy.16.taps_ref, bf16[6,512]{1,0:T(8,128)(2,1)} %copy-done.17, bf16[3,512,512]{2,1,0:T(8,128)(2,1)} %v_ref.1), custom_call_target="tpu_custom_call" | custom-call | flops 7864320 | bytes 1572864 | tf_op jit(solution)/shard_map/query/pallas_call | solution.py:146
  89.5 0.0 all-to-all-done.1
  89.5 2.2 %fusion = bf16[512,512]{1,0:T(8,128)(2,1)} fusion(f32[512,512]{1,0:T(8,128)} %query.1, bf16[64,8,512]{2,1,0:T(8,128)(2,1)S(1)} %all-to-all-done.1), kind=kLoop, calls=%fused_computation.1 | loop fusion | flops 786432 | bytes 2097152 | tf_op jit(solution)/shard_map/convert_element_type | solution.py:331
  (9 shorter events, 0.0 us)
Async XLA Ops:
  1.5 20.6 %slice-start = ((f32[7,3,512]{2,0,1:T(8,128)}), f32[7,2,512]{2,0,1:T(8,128)S(1)}, s32[]{:S(2)}) async-start(f32[7,3,512]{2,0,1:T(8,128)} %param.15), calls=%async_computation.2 | async-start | bytes 65536 | tf_op jit(solution)/shard_map/slice | solution.py:326
  1.5 21.1 %copy-start = (f32[16,32768]{1,0:T(8,128)S(1)}, f32[16,32768]{1,0:T(8,128)}, u32[]{:S(2)}) copy-start(f32[16,32768]{1,0:T(8,128)} %f_ref.1) | copy-start | bytes 6291460
  1.5 21.1 %copy-start.1 = (f32[512]{0:T(512)S(1)}, f32[512]{0:T(512)}, u32[]{:S(2)}) copy-start(f32[512]{0:T(512)} %skip_ref.1) | copy-start | bytes 6148
  1.5 21.1 %copy-start.2 = (bf16[512,256]{1,0:T(8,128)(2,1)S(1)}, bf16[512,256]{1,0:T(8,128)(2,1)}, u32[]{:S(2)}) copy-start(bf16[512,256]{1,0:T(8,128)(2,1)} %constant.37.clone.rhi) | copy-start | bytes 786436
  1.5 21.1 %copy-start.3 = (bf16[512,256]{1,0:T(8,128)(2,1)S(1)}, bf16[512,256]{1,0:T(8,128)(2,1)}, u32[]{:S(2)}) copy-start(bf16[512,256]{1,0:T(8,128)(2,1)} %constant.38.clone.rlo) | copy-start | bytes 786436
  1.5 21.1 %copy-start.6 = (f32[256,128]{1,0:T(8,128)S(1)}, f32[256,128]{1,0:T(8,128)}, u32[]{:S(2)}) copy-start(f32[256,128]{1,0:T(8,128)} %constant.39.clone.twr) | copy-start | bytes 393220
  8.8 33.3 %all-to-all-start = ((bf16[64,8,640]{2,1,0:T(8,128)(2,1)}), bf16[64,8,640]{2,1,0:T(8,128)(2,1)S(1)}, u32[]{:S(2)}, u32[]{:S(2)}) async-start(bf16[64,8,640]{2,1,0:T(8,128)(2,1)} %bitcast.14), calls=%async_computation | async-start | bytes 1310720 | tf_op jit(solution)/shard_map/all_to_all | solution.py:320
  22.6 0.9 copy-start.7
  23.5 0.9 copy-start.9
  24.4 0.9 copy-start.11
  30.6 1.3 %copy-start.15 = (f32[8,256,256]{2,1,0:T(8,128)}, f32[8,256,256]{2,1,0:T(8,128)S(1)}, u32[]{:S(2)}) copy-start(f32[8,256,256]{2,1,0:T(8,128)S(1)} %filter_spectrum.1.h_ref) | copy-start | bytes 6291460
  42.1 1.0 %copy-start.4 = (bf16[256,512]{1,0:T(8,128)(2,1)S(1)}, bf16[256,512]{1,0:T(8,128)(2,1)}, u32[]{:S(2)}) copy-start(bf16[256,512]{1,0:T(8,128)(2,1)} %constant.45.clone.chi) | copy-start | bytes 786436
  43.1 0.9 %copy-start.5 = (bf16[256,512]{1,0:T(8,128)(2,1)S(1)}, bf16[256,512]{1,0:T(8,128)(2,1)}, u32[]{:S(2)}) copy-start(bf16[256,512]{1,0:T(8,128)(2,1)} %constant.46.clone.clo) | copy-start | bytes 786436
  44.0 0.9 copy-start.8
  44.9 0.9 copy-start.10
  45.8 0.9 copy-start.12
  46.8 0.9 copy-start.13
  47.7 0.9 copy-start.14
  48.6 1.6 %copy-start.16 = (f32[8,256,256]{2,1,0:T(8,128)S(1)}, f32[8,256,256]{2,1,0:T(8,128)}, u32[]{:S(2)}) copy-start(f32[8,256,256]{2,1,0:T(8,128)} %copy-done.15) | copy-start | bytes 6291460
  59.8 29.7 %all-to-all-start.1 = ((bf16[64,8,512]{2,1,0:T(8,128)(2,1)}), bf16[64,8,512]{2,1,0:T(8,128)(2,1)S(1)}, u32[]{:S(2)}, u32[]{:S(2)}) async-start(bf16[64,8,512]{2,1,0:T(8,128)(2,1)} %bitcast.7), calls=%async_computation.1 | async-start | bytes 1048576 | tf_op jit(solution)/shard_map/all_to_all | solution.py:330
  67.2 15.2 %collective-permute-start = (bf16[6,512]{1,0:T(8,128)(2,1)S(1)}, bf16[6,512]{1,0:T(8,128)(2,1)S(1)}, u32[]{:S(2)}, u32[]{:S(2)}) collective-permute-start(bf16[6,512]{1,0:T(8,128)(2,1)S(1)} %bitcast.15), channel_id=1, source_target_pairs={{0,1},{1,2},{2,3},{3,4},{4,5},{5,6},{6,7},{7,8},{8,9},{9,10},{10,1... | collective-permute-start | bytes 18440 | tf_op jit(solution)/shard_map/ppermute | solution.py:323
  82.4 0.6 copy-start.17

commit v2 on v1

v2 whole, which is shorter than its diff:
```python
import math

import jax
import jax.numpy as jnp
import ml_dtypes
import numpy as np
from jax import lax
from jax.experimental import pallas as pl
from jax.experimental.pallas import tpu as pltpu
from jax.sharding import PartitionSpec as P

TAPS = 7
EDGE = TAPS - 1
LANES = 128
N1 = 256
N2 = 128
TOTAL = N1 * N2
F32 = jnp.float32
BF16 = jnp.bfloat16


def halves(table):
    hi = table.astype(ml_dtypes.bfloat16)
    lo = (table - hi.astype(np.float64)).astype(ml_dtypes.bfloat16)
    return hi, lo


def transform_tables():
    k1 = np.arange(N1) + 0.25
    first = np.exp(-2j * np.pi * np.outer(k1, np.arange(N1)) / N1)
    twist = np.exp(-2j * np.pi * np.outer(k1, np.arange(N2)) / TOTAL)
    second = np.exp(-2j * np.pi * np.outer(np.arange(N2), np.arange(N2)) / N2)
    rows = np.concatenate([first.real, first.imag], 0)
    columns = np.block([[second.real, second.imag], [-second.imag, second.real]])
    back = np.concatenate([first.real.T, -first.imag.T], 0)
    table = np.concatenate([*halves(rows), *halves(columns), *halves(back)], 0)
    return jnp.asarray(table), jnp.asarray(np.concatenate([twist.real, twist.imag], 0).astype(np.float32))


ROWS = slice(0, 4 * N1)
COLS_HI, COLS_LO = slice(4 * N1, 5 * N1), slice(5 * N1, 6 * N1)
BACK = 6 * N1
FORWARD = slice(0, BACK)
VMEM_LIMIT = 60 * 1024 * 1024
CONV_LIMIT = 54525952


def mm(a, b):
    return jnp.dot(a, b, preferred_element_type=F32)


def split(x):
    hi = x.astype(BF16)
    return hi, (x - hi.astype(F32)).astype(BF16)


def mm3(x, whi, wlo):
    hi, lo = split(x)
    return mm(hi, whi) + mm(lo, whi) + mm(hi, wlo)


def rows_at(i, count):
    return pl.ds(pl.multiple_of(i * count, count), count)


STEP = 256


def fill_selectors(shift_ref, spread_ref):
    shape = shift_ref.shape
    row, col = lax.broadcasted_iota(jnp.int32, shape, 0), lax.broadcasted_iota(jnp.int32, shape, 1)
    shift_ref[...] = jnp.where(row == LANES + col % LANES - (col // LANES + 1), 1.0, 0.0).astype(BF16)
    shape = spread_ref.shape
    row, col = lax.broadcasted_iota(jnp.int32, shape, 0), lax.broadcasted_iota(jnp.int32, shape, 1)
    spread_ref[...] = jnp.where((row < 24) & (row % 8 == col // LANES), 1.0, 0.0).astype(BF16)


def spread_taps(taps_ref, branch, start, spread):
    taps = jnp.concatenate([taps_ref[branch, :, pl.ds(start, STEP)], jnp.zeros((1, STEP), F32)], 0)
    hi = taps.astype(BF16).astype(F32)
    mid = (taps - hi).astype(BF16).astype(F32)
    columns = jnp.concatenate([hi, mid, taps - hi - mid, jnp.zeros((LANES - 24, STEP), F32)], 0).T
    return mm(columns.astype(BF16), spread)


def shaped_tile(previous, current, taps, shift):
    moved = mm(jnp.concatenate([previous, current], 1), shift)
    total = taps[:, :LANES] * current.astype(F32)
    for j in range(1, TAPS):
        total = total + taps[:, j * LANES : (j + 1) * LANES] * moved[:, (j - 1) * LANES : j * LANES]
    return total


def gate_kernel(taps_ref, k_ref, v_ref, o_ref, shift, spread, ktaps, vtaps):
    @pl.when(pl.program_id(0) == 0)
    def _():
        fill_selectors(shift, spread)

    start = pl.multiple_of(pl.program_id(0) * STEP, STEP)
    size = k_ref.shape[2]
    tiles = size // LANES
    ktaps[...] = spread_taps(taps_ref, 1, start, spread[...])
    vtaps[...] = spread_taps(taps_ref, 2, start, spread[...])

    def tile(ref, q):
        return ref[0, :, q * LANES : (q + 1) * LANES]

    for q in range(tiles):
        key = shaped_tile(tile(k_ref, (q - 1) % tiles), tile(k_ref, q), ktaps[...], shift[...])
        value = shaped_tile(tile(v_ref, (q - 1) % tiles), tile(v_ref, q), vtaps[...], shift[...])
        o_ref[:, q * LANES : (q + 1) * LANES] = (key * value).astype(BF16)
    lane = lax.broadcasted_iota(jnp.int32, (STEP, LANES), 1)

    def edges(ref, by):
        ends = jnp.where(lane >= LANES - EDGE, tile(ref, tiles - 1).astype(F32), tile(ref, 0).astype(F32))
        return pltpu.roll(ends, by, 1)

    both = jnp.where(lane < LANES // 2, edges(k_ref, EDGE), edges(v_ref, EDGE + LANES // 2))
    o_ref[:, size:] = both.astype(BF16)


def short_scratch(count):
    return [
        pltpu.VMEM((2 * LANES, EDGE * LANES), BF16),
        pltpu.VMEM((LANES, TAPS * LANES), BF16),
        *[pltpu.VMEM((STEP, TAPS * LANES), F32)] * count,
    ]


def gate_call(features, taps):
    _, channels, size = features.shape
    return pl.pallas_call(
        gate_kernel,
        grid=(channels // STEP,),
        in_specs=[
            pl.BlockSpec(taps.shape, lambda g: (0, 0, 0)),
            pl.BlockSpec((1, STEP, size), lambda g: (1, g, 0)),
            pl.BlockSpec((1, STEP, size), lambda g: (2, g, 0)),
        ],
        out_specs=pl.BlockSpec((STEP, size + LANES), lambda g: (g, 0)),
        out_shape=jax.ShapeDtypeStruct((channels, size + LANES), BF16),
        scratch_shapes=short_scratch(2),
        compiler_params=pltpu.CompilerParams(vmem_limit_bytes=VMEM_LIMIT),
        cost_estimate=pl.CostEstimate(flops=60 * channels * size, bytes_accessed=6 * channels * size, transcendentals=0),
        name="gate",
    )(taps, features, features)


def query_kernel(taps_ref, halo_ref, q_ref, o_ref, shift, spread, qtaps):
    @pl.when(pl.program_id(0) == 0)
    def _():
        fill_selectors(shift, spread)

    start = pl.multiple_of(pl.program_id(0) * STEP, STEP)
    qtaps[...] = spread_taps(taps_ref, 0, start, spread[...])
    halo = halo_ref[...].astype(F32)
    previous = jnp.concatenate([jnp.zeros((LANES - EDGE, STEP), F32), halo], 0).T.astype(BF16)
    for q in range(q_ref.shape[2] // LANES):
        current = q_ref[0, :, q * LANES : (q + 1) * LANES]
        o_ref[:, q * LANES : (q + 1) * LANES] = shaped_tile(previous, current, qtaps[...], shift[...])
        previous = current


def query_call(features, taps, halo):
    _, channels, size = features.shape
    return pl.pallas_call(
        query_kernel,
        grid=(channels // STEP,),
        in_specs=[
            pl.BlockSpec(taps.shape, lambda g: (0, 0, 0)),
            pl.BlockSpec((EDGE, STEP), lambda g: (0, g)),
            pl.BlockSpec((1, STEP, size), lambda g: (0, g, 0)),
        ],
        out_specs=pl.BlockSpec((STEP, size), lambda g: (g, 0)),
        out_shape=jax.ShapeDtypeStruct((channels, size), F32),
        scratch_shapes=short_scratch(1),
        cost_estimate=pl.CostEstimate(flops=30 * channels * size, bytes_accessed=6 * channels * size, transcendentals=0),
        name="query",
    )(taps, halo, features)


ANY = pl.BlockSpec(memory_space=pl.ANY)


def pair_of(grid_ref, c, own):
    return jnp.concatenate([grid_ref[pl.ds(2 * c + a, N1, stride=own), :] for a in range(2)], 1)


def filter_kernel(place_ref, skip_ref, f_ref, table_any, twist_ref, o_ref, grid_ref, table, sem):
    copy = pltpu.make_async_copy(table_any.at[FORWARD, :], table, sem)
    copy.start()
    own = f_ref.shape[0]
    for j in range(N1):
        grid_ref[j * own : (j + 1) * own, :] = f_ref[:, j * N2 : (j + 1) * N2]
    copy.wait()

    def pair(c, carry):
        hi, lo = split(pair_of(grid_ref, c, own))
        top, low = table[: 2 * N1], table[2 * N1 : 4 * N1]
        part = mm(top, hi) + mm(low, hi) + mm(top, lo)
        twr, twi = twist_ref[:N1], twist_ref[N1:]
        for a in range(2):
            re, im = part[:N1, a * N2 : (a + 1) * N2], part[N1:, a * N2 : (a + 1) * N2]
            turned = jnp.concatenate([re * twr - im * twi, re * twi + im * twr], 1)
            spec = mm3(turned, table[COLS_HI], table[COLS_LO])
            skip = skip_ref[place_ref[1] + 2 * c + a]
            o_ref[2 * c + a, :, :N2] = (spec[:, :N2] + skip) * (1.0 / TOTAL)
            o_ref[2 * c + a, :, N2:] = spec[:, N2:] * (-1.0 / TOTAL)
        return carry

    lax.fori_loop(0, own // 2, pair, 0)


def filter_call(filters, skip, half_place, first_channel, own, table, twist):
    return pl.pallas_call(
        filter_kernel,
        grid_spec=pltpu.PrefetchScalarGridSpec(
            num_scalar_prefetch=1,
            grid=(1,),
            in_specs=[
                pl.BlockSpec(memory_space=pltpu.SMEM),
                pl.BlockSpec((own, filters.shape[1]), lambda g, place: (place[0], 0)),
                ANY,
                pl.BlockSpec(twist.shape, lambda g, place: (0, 0)),
            ],
            out_specs=pl.BlockSpec((own, N1, 2 * N2), lambda g, place: (0, 0, 0)),
            scratch_shapes=[pltpu.VMEM((N1 * own, N2), F32), pltpu.VMEM((BACK, N1), BF16), pltpu.SemaphoreType.DMA],
        ),
        out_shape=jax.ShapeDtypeStruct((own, N1, 2 * N2), F32),
        compiler_params=pltpu.CompilerParams(vmem_limit_bytes=VMEM_LIMIT),
        cost_estimate=pl.CostEstimate(flops=12 * own * N1 * N1 * 2 * N2, bytes_accessed=6 << 20, transcendentals=0),
        name="filter_spectrum",
    )(jnp.stack([half_place, first_channel]).astype(jnp.int32), skip, filters, table, twist)


PIECES = 4


def conv_kernel(
    x_any, h_any, taps_ref, table_any, twist_any, o_any,
    grid_ref, edge_ref, res_ref, x_ref, h_ref, table, twist, o_ref, x_sem, h_sem, t_sem, o_sem,
):
    own = h_ref.shape[0]
    rows, width = x_ref.shape
    blocks = rows // own
    tiles = width // LANES - 1
    half = blocks // 2
    share = rows // PIECES
    x_copies = [
        pltpu.make_async_copy(x_any.at[pl.ds(i * share, share), :], x_ref.at[pl.ds(i * share, share), :], x_sem.at[i])
        for i in range(PIECES)
    ]
    cuts = [(0, 4 * N1), (4 * N1, 2 * N1), (6 * N1, 4 * N1)]
    t_copies = [
        pltpu.make_async_copy(table_any.at[pl.ds(at, n), :], table.at[pl.ds(at, n), :], t_sem.at[i])
        for i, (at, n) in enumerate(cuts)
    ]
    t_copies.insert(1, pltpu.make_async_copy(twist_any, twist, t_sem.at[len(cuts)]))
    h_copies = [
        pltpu.make_async_copy(h_any.at[pl.ds(2 * i, 2)], h_ref.at[pl.ds(2 * i, 2)], h_sem.at[i]) for i in range(own // 2)
    ]
    for copy in [*x_copies, *t_copies[:3], h_copies[0], t_copies[3], *h_copies[1:]]:
        copy.start()

    def unpack(i, carry):
        for q in range(tiles + 1):
            tile = x_ref[rows_at(i, 2 * own), q * LANES : (q + 1) * LANES].astype(F32)
            for h in range(2):
                place = i + h * half
                if q < tiles:
                    grid_ref[rows_at(place * tiles + q, own), :] = tile[h * own : (h + 1) * own]
                else:
                    edge_ref[rows_at(place, own), :] = tile[h * own : (h + 1) * own]
        return carry

    per_piece = half // PIECES
    for i in range(PIECES):
        x_copies[i].wait()
        lax.fori_loop(i * per_piece, (i + 1) * per_piece, unpack, 0, unroll=4)

    lane = lax.broadcasted_iota(jnp.int32, (own, LANES), 1)

    def mend(p, carry):
        here = edge_ref[rows_at(p, own), :]
        previous = jnp.where(p > 0, edge_ref[rows_at(jnp.maximum(p - 1, 0), own), :], 0.0)
        both = jnp.where(lane % (LANES // 2) < EDGE, previous, here)
        total = taps_ref[0] * both
        for j in range(1, TAPS):
            total = total + taps_ref[j] * pltpu.roll(both, j, 1)
        gated = pltpu.roll(total * pltpu.roll(total, LANES // 2, 1), LANES - EDGE, 1)
        at = rows_at(p * tiles, own)
        grid_ref[at, :] = jnp.where(lane < EDGE, gated, grid_ref[at, :])
        return carry

    lax.fori_loop(0, blocks, mend, 0, unroll=8)
    for copy in t_copies[:3]:
        copy.wait()

    for c in range(own // 2):
        x = pair_of(grid_ref, c, own).astype(BF16)
        part = mm(table[: 2 * N1], x) + mm(table[2 * N1 : 4 * N1], x)
        twr, twi = twist[:N1], twist[N1:]
        back_re, back_im = [], []
        h_copies[c].wait()
        for a in range(2):
            re, im = part[:N1, a * N2 : (a + 1) * N2], part[N1:, a * N2 : (a + 1) * N2]
            turned = jnp.concatenate([re * twr - im * twi, re * twi + im * twr], 1)
            spec = mm3(turned, table[COLS_HI], table[COLS_LO])
            sr, si = spec[:, :N2], spec[:, N2:]
            hr, hi = h_ref[2 * c + a, :, :N2], h_ref[2 * c + a, :, N2:]
            mid = mm3(jnp.concatenate([sr * hr + si * hi, sr * hi - si * hr], 1), table[COLS_HI], table[COLS_LO])
            mr, mi = mid[:, :N2], mid[:, N2:]
            back_re.append(mr * twr - mi * twi)
            back_im.append(mi * twr + mr * twi)
        if c == 0:
            t_copies[3].wait()
        y = None
        for at, back in ((BACK, back_re), (BACK + N1, back_im)):
            hi, lo = split(jnp.concatenate(back, 1))
            top, low = table[at : at + N1], table[at + 2 * N1 : at + 3 * N1]
            term = mm(top, hi) + mm(top, lo) + mm(low, hi)
            y = term if y is None else y + term
        for a in range(2):
            res_ref[pl.ds(2 * c + a, N1, stride=own), :] = y[:, a * N2 : (a + 1) * N2]

    def pack(i, carry):
        for q in range(tiles):
            tile = [res_ref[rows_at((i + h * half) * tiles + q, own), :] for h in range(2)]
            o_ref[rows_at(i, 2 * own), q * LANES : (q + 1) * LANES] = jnp.concatenate(tile, 0).astype(BF16)
        return carry

    o_copies = []
    for i in range(PIECES):
        lax.fori_loop(i * per_piece, (i + 1) * per_piece, pack, 0, unroll=4)
        piece = pl.ds(i * share, share)
        o_copies.append(pltpu.make_async_copy(o_ref.at[piece, :], o_any.at[piece, :], o_sem.at[i]))
        o_copies[-1].start()
    for copy in o_copies:
        copy.wait()


def conv_call(blocks, spectrum, taps, table, twist):
    own = spectrum.shape[0]
    rows, width = blocks.shape
    out = (rows, width - LANES)
    return pl.pallas_call(
        conv_kernel,
        in_specs=[ANY, ANY, pl.BlockSpec(memory_space=pltpu.VMEM), ANY, ANY],
        out_specs=ANY,
        out_shape=jax.ShapeDtypeStruct(out, BF16),
        scratch_shapes=[
            pltpu.VMEM((N1 * own, N2), F32),
            pltpu.VMEM((rows, LANES), F32),
            pltpu.VMEM((N1 * own, N2), F32),
            pltpu.VMEM(blocks.shape, BF16),
            pltpu.VMEM(spectrum.shape, F32),
            pltpu.VMEM(table.shape, BF16),
            pltpu.VMEM(twist.shape, F32),
            pltpu.VMEM(out, BF16),
            pltpu.SemaphoreType.DMA((PIECES,)),
            pltpu.SemaphoreType.DMA((own // 2,)),
            pltpu.SemaphoreType.DMA((4,)),
            pltpu.SemaphoreType.DMA((PIECES,)),
        ],
        compiler_params=pltpu.CompilerParams(vmem_limit_bytes=CONV_LIMIT),
        cost_estimate=pl.CostEstimate(flops=22 * own * N1 * N1 * 2 * N2, bytes_accessed=6 << 20, transcendentals=0),
        name="long_convolution",
    )(blocks, spectrum, taps, table, twist)


def shards(features, short_taps, filters, skip):
    size = features.shape[2]
    positions = lax.axis_size("half") * lax.axis_size("ctx")
    own = filters.shape[0] // lax.axis_size("half")
    half_place, ctx_place = lax.axis_index("half"), lax.axis_index("ctx")
    first_channel = ctx_place * filters.shape[0] + half_place * own
    table, twist = transform_tables()
    taps = jnp.swapaxes(short_taps, 0, 1)

    gated = gate_call(features, taps)
    blocks = lax.all_to_all(gated, ("ctx", "half"), 0, 0, tiled=True)

    tail = features[0, :, size - EDGE :].T
    halo = lax.ppermute(tail, ("half", "ctx"), [(i, i + 1) for i in range(positions - 1)])
    spectrum = filter_call(filters, skip, half_place, first_channel, own, table, twist)
    own_taps = lax.dynamic_slice_in_dim(taps[1:], first_channel, own, 2)
    own_taps = jnp.repeat(own_taps.transpose(1, 2, 0), LANES // 2, axis=2)
    halo, spectrum = lax.optimization_barrier((halo, spectrum))

    convolved = conv_call(blocks, spectrum, own_taps, table, twist)
    back = lax.all_to_all(convolved, ("ctx", "half"), 0, 0, tiled=True)
    query = query_call(features, taps, halo)
    return (query * back.astype(F32)).astype(BF16)


def solution(mesh):
    in_specs = (P("seq", None, ("half", "ctx")), P(), P("ctx", None), P())
    out_specs = P("seq", ("half", "ctx"))
    return jax.shard_map(shards, mesh=mesh, in_specs=in_specs, out_specs=out_specs, check_vma=False)
```

time: 92.3 us -> 74 us (0.80)
  local copies, waits for them, and re-layouts: 15.6 us -> 1.54 us
  Pallas kernels: 28.9 us -> 26.7 us
  waiting for transfers between devices: 22 us -> 20.1 us
    unnamed x38 -> x7, local copies, waits for them, and re-layouts: 14.2 us -> 0.11 us
    all_to_all x1, waiting for transfers between devices: 0.01 us -> 13.9 us  [shards(): back = lax.all_to_all(convolved, ('ctx', 'half'), 0, 0, tiled=True)]
    all_to_all x1, waiting for transfers between devices: 10.2 us -> 1.19 us  [shards(): blocks = lax.all_to_all(gated, ('ctx', 'half'), 0, 0, tiled=True)]
    ppermute x1, waiting for transfers between devices: 11.9 us -> 4.97 us  [shards(): lax.ppermute(tail, ('half', 'ctx'), [(i, i + 1) for i in range(positions...]
    pallas_call x3, Pallas kernels: 23.6 us -> 17.9 us  [the longest x1 9.99 us: conv_call(): pl.pallas_call(conv_kernel, in_specs=[ANY, ANY, pl.BlockSpec(memory_space...]
    pallas_call x1, Pallas kernels: 5.36 us -> 8.81 us  [filter_call(): pl.pallas_call(filter_kernel, grid_spec=pltpu.PrefetchScalarGridSpec(num_...]
  transfers between devices with their start and end apart: 3 -> 3, of which waited for: 2 -> 3; matrix products, arithmetic and copies ran while one was open for 2% -> 3% of each run, Pallas kernels for 13% -> 17%
where the time goes in v2:
time: 74 us; the launch traced here: 73.6 us
  Pallas kernels  26.7 us (36%)
  starting transfers between devices  22.3 us (30%)
  waiting for transfers between devices  20.1 us (27%)
  other arithmetic  2.83 us (4%)
  local copies, waits for them, and re-layouts  1.54 us (2%)
    all_to_all x1, waiting for transfers between devices, shards(): back = lax.all_to_all(convolved, ('ctx', 'half'), 0, 0, tiled=True)  13.9 us
    all_to_all x1, starting transfers between devices, shards(): blocks = lax.all_to_all(gated, ('ctx', 'half'), 0, 0, tiled=True)  13.2 us
    pallas_call x1, Pallas kernels, conv_call(): pl.pallas_call(conv_kernel, in_specs=[ANY, ANY, pl.BlockSpec(memory_space...  9.99 us
    pallas_call x1, Pallas kernels, filter_call(): pl.pallas_call(filter_kernel, grid_spec=pltpu.PrefetchScalarGridSpec(num_...  8.81 us
    all_to_all x1, starting transfers between devices, shards(): back = lax.all_to_all(convolved, ('ctx', 'half'), 0, 0, tiled=True)  5.89 us
    ppermute x1, waiting for transfers between devices, shards(): lax.ppermute(tail, ('half', 'ctx'), [(i, i + 1) for i in range(positions...  4.97 us
    pallas_call x1, Pallas kernels, gate_call(): pl.pallas_call(gate_kernel, grid=(channels // STEP,), in_specs=[pl.BlockS...  4.49 us
    pallas_call x1, Pallas kernels, query_call(): pl.pallas_call(query_kernel, grid=(channels // STEP,), in_specs=[pl.Block...  3.41 us
  transfers between devices with their start and end apart: 3, of which 3 were waited for; matrix products, arithmetic and copies ran while one was open for 3% of the time, Pallas kernels for 17%

profile of v2, /device:TPU:1, one launch (start us, length us, event | category | flops | bytes accessed | tf_op | source)
XLA Modules:
  0.0 73.6 jit_solution(5072010478569913386)
XLA Ops:
  0.0 0.0 copy-start.1
  0.0 4.5 %gate.1 = bf16[512,640]{1,0:T(8,128)(2,1)} custom-call(f32[3,7,512]{2,1,0:T(8,128)} %bitcast.16, bf16[3,512,512]{2,1,0:T(8,128)(2,1)} %v_ref.1, bf16[3,512,512]{2,1,0:T(8,128)(2,1)} %v_ref.1), custom_call_target="tpu_custom_call" | custom-call | flops 15728640 | bytes 1572864 | tf_op jit(solution)/shard_map/gate/pallas_call | solution.py:132
  4.5 13.2 %all-to-all-start = ((bf16[64,8,640]{2,1,0:T(8,128)(2,1)}), bf16[64,8,640]{2,1,0:T(8,128)(2,1)S(1)}, u32[]{:S(2)}, u32[]{:S(2)}) async-start(bf16[64,8,640]{2,1,0:T(8,128)(2,1)} %bitcast.15), calls=%async_computation | async-start | bytes 1310720 | tf_op jit(solution)/shard_map/all_to_all | solution.py:381
  17.7 1.0 %slice.6 = bf16[1,512,6]{2,1,0:T(8,128)(2,1)S(1)} slice(bf16[3,512,512]{2,1,0:T(8,128)(2,1)} %v_ref.1), slice={[0:1], [0:512], [506:512]} | slice | bytes 12288 | tf_op jit(solution)/shard_map/slice | solution.py:383
  18.7 0.1 copy.9
  18.8 3.3 %collective-permute-start = (bf16[6,512]{1,0:T(8,128)(2,1)S(1)}, bf16[6,512]{1,0:T(8,128)(2,1)S(1)}, u32[]{:S(2)}, u32[]{:S(2)}) collective-permute-start(bf16[6,512]{1,0:T(8,128)(2,1)S(1)} %bitcast.19), channel_id=1, source_target_pairs={{0,1},{1,2},{2,3},{3,4},{4,5},{5,6},{6,7},{7,8},{8,9},{9,10},{10,1... | collective-permute-start | bytes 18440 | tf_op jit(solution)/shard_map/ppermute | solution.py:384
  22.1 0.0 copy-done.1
  22.1 0.6 pad_add_fusion.place_ref
  22.8 0.0 copy-start
  22.8 8.8 %filter_spectrum.1.h_any = f32[8,256,256]{2,1,0:T(8,128)} custom-call(s32[2]{0:T(128)} %pad_add_fusion.place_ref, f32[512]{0:T(512)} %skip_ref.1, f32[16,32768]{1,0:T(8,128)} %f_ref.1, bf16[2560,256]{1,0:T(8,128)(2,1)} %constant.21.clone.table_any, f32[512,128]{1,0:T(8,128)} %constant.22.clone.twist_ref.twist_any), custom_call_target="tpu_custom_call" | custom-call | flops 1610612736 | bytes 6291456 | tf_op jit(solution)/shard_map/filter_spectrum/pallas_call | solution.py:215
  31.6 0.1 dynamic-slice_bitcast_fusion
  31.7 0.1 copy.8
  31.8 0.1 broadcast_in_dim.3
  31.9 0.1 reshape.9.taps_ref
  32.0 5.0 %collective-permute-done.halo_ref = bf16[6,512]{1,0:T(8,128)(2,1)S(1)} collective-permute-done((bf16[6,512]{1,0:T(8,128)(2,1)S(1)}, bf16[6,512]{1,0:T(8,128)(2,1)S(1)}, u32[]{:S(2)}, u32[]{:S(2)}) %collective-permute-start) | collective-permute-done | bytes 6176 | tf_op jit(solution)/shard_map/ppermute | solution.py:384
  37.0 0.0 copy-start.2
  37.0 1.2 %all-to-all-done = bf16[64,8,640]{2,1,0:T(8,128)(2,1)S(1)} async-done(((bf16[64,8,640]{2,1,0:T(8,128)(2,1)}), bf16[64,8,640]{2,1,0:T(8,128)(2,1)S(1)}, u32[]{:S(2)}, u32[]{:S(2)}) %all-to-all-start) | async-done | bytes 655392 | tf_op jit(solution)/shard_map/all_to_all | solution.py:381
  38.2 0.0 copy-done
  38.2 10.0 %long_convolution.1 = bf16[512,512]{1,0:T(8,128)(2,1)} custom-call(bf16[512,640]{1,0:T(8,128)(2,1)S(1)} %bitcast.14, f32[8,256,256]{2,1,0:T(8,128)} %filter_spectrum.1.h_any, f32[7,8,128]{2,1,0:T(8,128)S(1)} %reshape.9.taps_ref, bf16[2560,256]{1,0:T(8,128)(2,1)} %constant.21.clone.table_any, f32[512,128]{1,0:T(8,128)S(1)} %copy-done), custom_call_target="tpu_custom_call" | custom-call | flops 2952790016 | bytes 6291456 | tf_op jit(solution)/shard_map/long_convolution/pallas_call | solution.py:346
  48.2 0.0 copy-done.2
  48.2 5.9 %all-to-all-start.1 = ((bf16[64,8,512]{2,1,0:T(8,128)(2,1)}), bf16[64,8,512]{2,1,0:T(8,128)(2,1)S(1)}, u32[]{:S(2)}, u32[]{:S(2)}) async-start(bf16[64,8,512]{2,1,0:T(8,128)(2,1)} %bitcast.8), calls=%async_computation.1 | async-start | bytes 1048576 | tf_op jit(solution)/shard_map/all_to_all | solution.py:391
  54.1 3.4 %query.1 = f32[512,512]{1,0:T(8,128)} custom-call(f32[3,7,512]{2,1,0:T(8,128)} %bitcast.17, bf16[6,512]{1,0:T(8,128)(2,1)} %copy-done.2, bf16[3,512,512]{2,1,0:T(8,128)(2,1)} %v_ref.1), custom_call_target="tpu_custom_call" | custom-call | flops 7864320 | bytes 1572864 | tf_op jit(solution)/shard_map/query/pallas_call | solution.py:166
  57.5 13.9 %all-to-all-done.1 = bf16[64,8,512]{2,1,0:T(8,128)(2,1)S(1)} async-done(((bf16[64,8,512]{2,1,0:T(8,128)(2,1)}), bf16[64,8,512]{2,1,0:T(8,128)(2,1)S(1)}, u32[]{:S(2)}, u32[]{:S(2)}) %all-to-all-start.1) | async-done | bytes 524320 | tf_op jit(solution)/shard_map/all_to_all | solution.py:391
  71.4 2.2 %fusion = bf16[512,512]{1,0:T(8,128)(2,1)} fusion(f32[512,512]{1,0:T(8,128)} %query.1, bf16[64,8,512]{2,1,0:T(8,128)(2,1)S(1)} %all-to-all-done.1), kind=kLoop, calls=%fused_computation.1 | loop fusion | flops 786432 | bytes 2097152 | tf_op jit(solution)/shard_map/convert_element_type | solution.py:393
  (1 shorter events, 0.0 us)
Async XLA Ops:
  0.0 22.1 %copy-start.1 = (f32[7,3,512]{2,0,1:T(8,128)S(1)}, f32[7,3,512]{2,0,1:T(8,128)}, u32[]{:S(2)}) copy-start(f32[7,3,512]{2,0,1:T(8,128)} %param.7) | copy-start | bytes 129028
  4.5 33.7 %all-to-all-start = ((bf16[64,8,640]{2,1,0:T(8,128)(2,1)}), bf16[64,8,640]{2,1,0:T(8,128)(2,1)S(1)}, u32[]{:S(2)}, u32[]{:S(2)}) async-start(bf16[64,8,640]{2,1,0:T(8,128)(2,1)} %bitcast.15), calls=%async_computation | async-start | bytes 1310720 | tf_op jit(solution)/shard_map/all_to_all | solution.py:381
  18.8 18.2 %collective-permute-start = (bf16[6,512]{1,0:T(8,128)(2,1)S(1)}, bf16[6,512]{1,0:T(8,128)(2,1)S(1)}, u32[]{:S(2)}, u32[]{:S(2)}) collective-permute-start(bf16[6,512]{1,0:T(8,128)(2,1)S(1)} %bitcast.19), channel_id=1, source_target_pairs={{0,1},{1,2},{2,3},{3,4},{4,5},{5,6},{6,7},{7,8},{8,9},{9,10},{10,1... | collective-permute-start | bytes 18440 | tf_op jit(solution)/shard_map/ppermute | solution.py:384
  22.8 15.4 %copy-start = (f32[512,128]{1,0:T(8,128)S(1)}, f32[512,128]{1,0:T(8,128)}, u32[]{:S(2)}) copy-start(f32[512,128]{1,0:T(8,128)} %constant.22.clone.twist_ref.twist_any) | copy-start | bytes 786436
  37.0 11.2 %copy-start.2 = (bf16[6,512]{1,0:T(8,128)(2,1)}, bf16[6,512]{1,0:T(8,128)(2,1)S(1)}, u32[]{:S(2)}) copy-start(bf16[6,512]{1,0:T(8,128)(2,1)S(1)} %collective-permute-done.halo_ref) | copy-start | bytes 18436
  48.2 23.2 %all-to-all-start.1 = ((bf16[64,8,512]{2,1,0:T(8,128)(2,1)}), bf16[64,8,512]{2,1,0:T(8,128)(2,1)S(1)}, u32[]{:S(2)}, u32[]{:S(2)}) async-start(bf16[64,8,512]{2,1,0:T(8,128)(2,1)} %bitcast.8), calls=%async_computation.1 | async-start | bytes 1048576 | tf_op jit(solution)/shard_map/all_to_all | solution.py:391

commit v3 on v2

--- a/solution.py
+++ b/solution.py
@@ -33,13 +33,22 @@
     rows = np.concatenate([first.real, first.imag], 0)
     columns = np.block([[second.real, second.imag], [-second.imag, second.real]])
     back = np.concatenate([first.real.T, -first.imag.T], 0)
-    table = np.concatenate([*halves(rows), *halves(columns), *halves(back)], 0)
+    gather, add = np.zeros((LANES, 2 * LANES)), np.zeros((LANES, 2 * LANES))
+    for branch in range(2):
+        for j in range(TAPS):
+            for t in range(EDGE):
+                at = branch * LANES // 2 + j * 8 + t
+                gather[branch * LANES // 2 + EDGE + t - j, at] = 1
+                add[at, branch * LANES + t] = 1
+    exact = [gather.astype(ml_dtypes.bfloat16), add.astype(ml_dtypes.bfloat16)]
+    table = np.concatenate([*halves(rows), *halves(columns), *halves(back), *exact], 0)
     return jnp.asarray(table), jnp.asarray(np.concatenate([twist.real, twist.imag], 0).astype(np.float32))
 
 
 ROWS = slice(0, 4 * N1)
 COLS_HI, COLS_LO = slice(4 * N1, 5 * N1), slice(5 * N1, 6 * N1)
 BACK = 6 * N1
+GATHER = 10 * N1
 FORWARD = slice(0, BACK)
 VMEM_LIMIT = 60 * 1024 * 1024
 CONV_LIMIT = 54525952
@@ -250,16 +259,16 @@
         pltpu.make_async_copy(x_any.at[pl.ds(i * share, share), :], x_ref.at[pl.ds(i * share, share), :], x_sem.at[i])
         for i in range(PIECES)
     ]
-    cuts = [(0, 4 * N1), (4 * N1, 2 * N1), (6 * N1, 4 * N1)]
+    cuts = [(0, 4 * N1), (4 * N1, 2 * N1), (BACK, 4 * N1), (GATHER, 2 * LANES)]
     t_copies = [
         pltpu.make_async_copy(table_any.at[pl.ds(at, n), :], table.at[pl.ds(at, n), :], t_sem.at[i])
         for i, (at, n) in enumerate(cuts)
     ]
-    t_copies.insert(1, pltpu.make_async_copy(twist_any, twist, t_sem.at[len(cuts)]))
+    twist_copy = pltpu.make_async_copy(twist_any, twist, t_sem.at[len(cuts)])
     h_copies = [
         pltpu.make_async_copy(h_any.at[pl.ds(2 * i, 2)], h_ref.at[pl.ds(2 * i, 2)], h_sem.at[i]) for i in range(own // 2)
     ]
-    for copy in [*x_copies, *t_copies[:3], h_copies[0], t_copies[3], *h_copies[1:]]:
+    for copy in [*x_copies, t_copies[3], t_copies[0], twist_copy, t_copies[1], *h_copies, t_copies[2]]:
         copy.start()
 
     def unpack(i, carry):
@@ -270,7 +279,7 @@
                 if q < tiles:
                     grid_ref[rows_at(place * tiles + q, own), :] = tile[h * own : (h + 1) * own]
                 else:
-                    edge_ref[rows_at(place, own), :] = tile[h * own : (h + 1) * own]
+                    edge_ref[rows_at(place + 1, own), :] = tile[h * own : (h + 1) * own]
         return carry
 
     per_piece = half // PIECES
@@ -278,45 +287,46 @@
         x_copies[i].wait()
         lax.fori_loop(i * per_piece, (i + 1) * per_piece, unpack, 0, unroll=4)
 
-    lane = lax.broadcasted_iota(jnp.int32, (own, LANES), 1)
-
-    def mend(p, carry):
-        here = edge_ref[rows_at(p, own), :]
-        previous = jnp.where(p > 0, edge_ref[rows_at(jnp.maximum(p - 1, 0), own), :], 0.0)
-        both = jnp.where(lane % (LANES // 2) < EDGE, previous, here)
-        total = taps_ref[0] * both
-        for j in range(1, TAPS):
-            total = total + taps_ref[j] * pltpu.roll(both, j, 1)
-        gated = pltpu.roll(total * pltpu.roll(total, LANES // 2, 1), LANES - EDGE, 1)
-        at = rows_at(p * tiles, own)
-        grid_ref[at, :] = jnp.where(lane < EDGE, gated, grid_ref[at, :])
-        return carry
-
-    lax.fori_loop(0, blocks, mend, 0, unroll=8)
-    for copy in t_copies[:3]:
-        copy.wait()
-
-    for c in range(own // 2):
+    edge_ref[:own, :] = jnp.zeros((own, LANES), F32)
+    lane = lax.broadcasted_iota(jnp.int32, (rows, LANES), 1)
+    both = jnp.where(lane % (LANES // 2) < EDGE, edge_ref[:rows, :], edge_ref[own:, :]).astype(BF16)
+    t_copies[3].wait()
+    terms = mm(both, table[GATHER : GATHER + LANES, :LANES]).reshape(blocks, own, LANES) * taps_ref[...][None]
+    hi, lo = split(terms.reshape(rows, LANES))
+    add = table[GATHER + LANES : GATHER + 2 * LANES]
+    sums = mm(hi, add) + mm(lo, add)
+    gated = sums[:, :LANES] * sums[:, LANES:]
+    for p in range(blocks):
+        grid_ref[p * tiles * own : (p * tiles + 1) * own, :EDGE] = gated[p * own : (p + 1) * own, :EDGE]
+
+    pairs = range(own // 2)
+    t_copies[0].wait()
+    twist_copy.wait()
+    twr, twi = twist[:N1], twist[N1:]
+    turned = []
+    for c in pairs:
         x = pair_of(grid_ref, c, own).astype(BF16)
         part = mm(table[: 2 * N1], x) + mm(table[2 * N1 : 4 * N1], x)
-        twr, twi = twist[:N1], twist[N1:]
-        back_re, back_im = [], []
-        h_copies[c].wait()
         for a in range(2):
             re, im = part[:N1, a * N2 : (a + 1) * N2], part[N1:, a * N2 : (a + 1) * N2]
-            turned = jnp.concatenate([re * twr - im * twi, re * twi + im * twr], 1)
-            spec = mm3(turned, table[COLS_HI], table[COLS_LO])
-            sr, si = spec[:, :N2], spec[:, N2:]
-            hr, hi = h_ref[2 * c + a, :, :N2], h_ref[2 * c + a, :, N2:]
-            mid = mm3(jnp.concatenate([sr * hr + si * hi, sr * hi - si * hr], 1), table[COLS_HI], table[COLS_LO])
-            mr, mi = mid[:, :N2], mid[:, N2:]
-            back_re.append(mr * twr - mi * twi)
-            back_im.append(mi * twr + mr * twi)
-        if c == 0:
-            t_copies[3].wait()
+            turned.append(jnp.concatenate([re * twr - im * twi, re * twi + im * twr], 1))
+    t_copies[1].wait()
+    back = []
+    for c in range(own):
+        if c % 2 == 0:
+            h_copies[c // 2].wait()
+        spec = mm3(turned[c], table[COLS_HI], table[COLS_LO])
+        sr, si = spec[:, :N2], spec[:, N2:]
+        hr, hi = h_ref[c, :, :N2], h_ref[c, :, N2:]
+        mid = mm3(jnp.concatenate([sr * hr + si * hi, sr * hi - si * hr], 1), table[COLS_HI], table[COLS_LO])
+        mr, mi = mid[:, :N2], mid[:, N2:]
+        back.append((mr * twr - mi * twi, mi * twr + mr * twi))
+    t_copies[2].wait()
+    for c in pairs:
         y = None
-        for at, back in ((BACK, back_re), (BACK + N1, back_im)):
-            hi, lo = split(jnp.concatenate(back, 1))
+        for part in range(2):
+            at = BACK + part * N1
+            hi, lo = split(jnp.concatenate([back[2 * c][part], back[2 * c + 1][part]], 1))
             top, low = table[at : at + N1], table[at + 2 * N1 : at + 3 * N1]
             term = mm(top, hi) + mm(top, lo) + mm(low, hi)
             y = term if y is None else y + term
@@ -350,7 +360,7 @@
         out_shape=jax.ShapeDtypeStruct(out, BF16),
         scratch_shapes=[
             pltpu.VMEM((N1 * own, N2), F32),
-            pltpu.VMEM((rows, LANES), F32),
+            pltpu.VMEM((rows + own, LANES), F32),
             pltpu.VMEM((N1 * own, N2), F32),
             pltpu.VMEM(blocks.shape, BF16),
             pltpu.VMEM(spectrum.shape, F32),
@@ -359,7 +369,7 @@
             pltpu.VMEM(out, BF16),
             pltpu.SemaphoreType.DMA((PIECES,)),
             pltpu.SemaphoreType.DMA((own // 2,)),
-            pltpu.SemaphoreType.DMA((4,)),
+            pltpu.SemaphoreType.DMA((5,)),
             pltpu.SemaphoreType.DMA((PIECES,)),
         ],
         compiler_params=pltpu.CompilerParams(vmem_limit_bytes=CONV_LIMIT),
@@ -384,7 +394,8 @@
     halo = lax.ppermute(tail, ("half", "ctx"), [(i, i + 1) for i in range(positions - 1)])
     spectrum = filter_call(filters, skip, half_place, first_channel, own, table, twist)
     own_taps = lax.dynamic_slice_in_dim(taps[1:], first_channel, own, 2)
-    own_taps = jnp.repeat(own_taps.transpose(1, 2, 0), LANES // 2, axis=2)
+    own_taps = jnp.pad(own_taps.transpose(2, 0, 1), ((0, 0), (0, 0), (0, 8 - TAPS)))
+    own_taps = jnp.repeat(own_taps.reshape(own, 16), 8, axis=1)
     halo, spectrum = lax.optimization_barrier((halo, spectrum))
 
     convolved = conv_call(blocks, spectrum, own_taps, table, twist)

time: 74 us -> 72.5 us (0.980)
  Pallas kernels: 26.7 us -> 25.2 us
    pallas_call x1, Pallas kernels: 9.99 us -> 8.48 us  [conv_call(): pl.pallas_call(conv_kernel, in_specs=[ANY, ANY, pl.BlockSpec(memory_space...]
where the time goes in v3:
time: 72.5 us; the launch traced here: 72.1 us
  Pallas kernels  25.2 us (35%)
  starting transfers between devices  22.3 us (31%)
  waiting for transfers between devices  20.2 us (28%)
  other arithmetic  2.83 us (4%)
  local copies, waits for them, and re-layouts  1.45 us (2%)
    all_to_all x1, waiting for transfers between devices, shards(): back = lax.all_to_all(convolved, ('ctx', 'half'), 0, 0, tiled=True)  13.9 us
    all_to_all x1, starting transfers between devices, shards(): blocks = lax.all_to_all(gated, ('ctx', 'half'), 0, 0, tiled=True)  13.2 us
    pallas_call x1, Pallas kernels, filter_call(): pl.pallas_call(filter_kernel, grid_spec=pltpu.PrefetchScalarGridSpec(num_...  8.81 us
    pallas_call x1, Pallas kernels, conv_call(): pl.pallas_call(conv_kernel, in_specs=[ANY, ANY, pl.BlockSpec(memory_space...  8.48 us
    all_to_all x1, starting transfers between devices, shards(): back = lax.all_to_all(convolved, ('ctx', 'half'), 0, 0, tiled=True)  5.89 us
    ppermute x1, waiting for transfers between devices, shards(): lax.ppermute(tail, ('half', 'ctx'), [(i, i + 1) for i in range(positions...  5.06 us
    pallas_call x1, Pallas kernels, gate_call(): pl.pallas_call(gate_kernel, grid=(channels // STEP,), in_specs=[pl.BlockS...  4.49 us
    pallas_call x1, Pallas kernels, query_call(): pl.pallas_call(query_kernel, grid=(channels // STEP,), in_specs=[pl.Block...  3.41 us
  transfers between devices with their start and end apart: 3, of which 3 were waited for; matrix products, arithmetic and copies ran while one was open for 3% of the time, Pallas kernels for 17%

profile of v3, /device:TPU:1, one launch (start us, length us, event | category | flops | bytes accessed | tf_op | source)
XLA Modules:
  0.0 72.1 jit_solution(8119928341912629621)
XLA Ops:
  0.0 0.0 copy-start.1
  0.0 4.5 %gate.1 = bf16[512,640]{1,0:T(8,128)(2,1)} custom-call(f32[3,7,512]{2,1,0:T(8,128)} %bitcast.18, bf16[3,512,512]{2,1,0:T(8,128)(2,1)} %v_ref.1, bf16[3,512,512]{2,1,0:T(8,128)(2,1)} %v_ref.1), custom_call_target="tpu_custom_call" | custom-call | flops 15728640 | bytes 1572864 | tf_op jit(solution)/shard_map/gate/pallas_call | solution.py:141
  4.5 13.2 %all-to-all-start = ((bf16[64,8,640]{2,1,0:T(8,128)(2,1)}), bf16[64,8,640]{2,1,0:T(8,128)(2,1)S(1)}, u32[]{:S(2)}, u32[]{:S(2)}) async-start(bf16[64,8,640]{2,1,0:T(8,128)(2,1)} %bitcast.17), calls=%async_computation | async-start | bytes 1310720 | tf_op jit(solution)/shard_map/all_to_all | solution.py:391
  17.7 1.0 %slice.6 = bf16[1,512,6]{2,1,0:T(8,128)(2,1)S(1)} slice(bf16[3,512,512]{2,1,0:T(8,128)(2,1)} %v_ref.1), slice={[0:1], [0:512], [506:512]} | slice | bytes 12288 | tf_op jit(solution)/shard_map/slice | solution.py:393
  18.7 0.1 copy.12
  18.8 3.3 %collective-permute-start = (bf16[6,512]{1,0:T(8,128)(2,1)S(1)}, bf16[6,512]{1,0:T(8,128)(2,1)S(1)}, u32[]{:S(2)}, u32[]{:S(2)}) collective-permute-start(bf16[6,512]{1,0:T(8,128)(2,1)S(1)} %bitcast.21), channel_id=1, source_target_pairs={{0,1},{1,2},{2,3},{3,4},{4,5},{5,6},{6,7},{7,8},{8,9},{9,10},{10,1... | collective-permute-start | bytes 18440 | tf_op jit(solution)/shard_map/ppermute | solution.py:394
  22.1 0.0 copy-done.1
  22.1 0.6 pad_add_fusion.place_ref
  22.8 0.1 dynamic-slice_bitcast_fusion
  22.8 0.0 copy-start
  22.8 8.8 %filter_spectrum.1.h_any = f32[8,256,256]{2,1,0:T(8,128)} custom-call(s32[2]{0:T(128)} %pad_add_fusion.place_ref, f32[512]{0:T(512)} %skip_ref.1, f32[16,32768]{1,0:T(8,128)} %f_ref.1, bf16[2816,256]{1,0:T(8,128)(2,1)} %constant.23.clone.table_any, f32[512,128]{1,0:T(8,128)} %constant.24.clone.twist_ref.twist_any), custom_call_target="tpu_custom_call" | custom-call | flops 1610612736 | bytes 6291456 | tf_op jit(solution)/shard_map/filter_spectrum/pallas_call | solution.py:224
  31.7 0.1 copy.11
  31.7 0.1 broadcast_in_dim.3
  31.8 0.1 reshape.13.taps_ref
  31.9 5.1 %collective-permute-done.halo_ref = bf16[6,512]{1,0:T(8,128)(2,1)S(1)} collective-permute-done((bf16[6,512]{1,0:T(8,128)(2,1)S(1)}, bf16[6,512]{1,0:T(8,128)(2,1)S(1)}, u32[]{:S(2)}, u32[]{:S(2)}) %collective-permute-start) | collective-permute-done | bytes 6176 | tf_op jit(solution)/shard_map/ppermute | solution.py:394
  37.0 0.0 copy-start.2
  37.0 1.2 %all-to-all-done = bf16[64,8,640]{2,1,0:T(8,128)(2,1)S(1)} async-done(((bf16[64,8,640]{2,1,0:T(8,128)(2,1)}), bf16[64,8,640]{2,1,0:T(8,128)(2,1)S(1)}, u32[]{:S(2)}, u32[]{:S(2)}) %all-to-all-start) | async-done | bytes 655392 | tf_op jit(solution)/shard_map/all_to_all | solution.py:391
  38.2 0.0 copy-done
  38.2 8.5 %long_convolution.1 = bf16[512,512]{1,0:T(8,128)(2,1)} custom-call(bf16[512,640]{1,0:T(8,128)(2,1)S(1)} %bitcast.16, f32[8,256,256]{2,1,0:T(8,128)} %filter_spectrum.1.h_any, f32[8,128]{1,0:T(8,128)S(1)} %reshape.13.taps_ref, bf16[2816,256]{1,0:T(8,128)(2,1)} %constant.23.clone.table_any, f32[512,128]{1,0:T(8,128)S(1)} %copy-done), custom_call_target="tpu_custom_call" | custom-call | flops 2952790016 | bytes 6291456 | tf_op jit(solution)/shard_map/long_convolution/pallas_call | solution.py:356
  46.7 0.0 copy-done.2
  46.7 5.9 %all-to-all-start.1 = ((bf16[64,8,512]{2,1,0:T(8,128)(2,1)}), bf16[64,8,512]{2,1,0:T(8,128)(2,1)S(1)}, u32[]{:S(2)}, u32[]{:S(2)}) async-start(bf16[64,8,512]{2,1,0:T(8,128)(2,1)} %bitcast.9), calls=%async_computation.1 | async-start | bytes 1048576 | tf_op jit(solution)/shard_map/all_to_all | solution.py:402
  52.6 3.4 %query.1 = f32[512,512]{1,0:T(8,128)} custom-call(f32[3,7,512]{2,1,0:T(8,128)} %bitcast.19, bf16[6,512]{1,0:T(8,128)(2,1)} %copy-done.2, bf16[3,512,512]{2,1,0:T(8,128)(2,1)} %v_ref.1), custom_call_target="tpu_custom_call" | custom-call | flops 7864320 | bytes 1572864 | tf_op jit(solution)/shard_map/query/pallas_call | solution.py:175
  56.0 13.9 %all-to-all-done.1 = bf16[64,8,512]{2,1,0:T(8,128)(2,1)S(1)} async-done(((bf16[64,8,512]{2,1,0:T(8,128)(2,1)}), bf16[64,8,512]{2,1,0:T(8,128)(2,1)S(1)}, u32[]{:S(2)}, u32[]{:S(2)}) %all-to-all-start.1) | async-done | bytes 524320 | tf_op jit(solution)/shard_map/all_to_all | solution.py:402
  69.9 2.2 %fusion = bf16[512,512]{1,0:T(8,128)(2,1)} fusion(f32[512,512]{1,0:T(8,128)} %query.1, bf16[64,8,512]{2,1,0:T(8,128)(2,1)S(1)} %all-to-all-done.1), kind=kLoop, calls=%fused_computation.1 | loop fusion | flops 786432 | bytes 2097152 | tf_op jit(solution)/shard_map/convert_element_type | solution.py:404
  (2 shorter events, 0.0 us)
Async XLA Ops:
  0.0 22.1 %copy-start.1 = (f32[7,3,512]{2,0,1:T(8,128)S(1)}, f32[7,3,512]{2,0,1:T(8,128)}, u32[]{:S(2)}) copy-start(f32[7,3,512]{2,0,1:T(8,128)} %param.7) | copy-start | bytes 129028
  4.5 33.7 %all-to-all-start = ((bf16[64,8,640]{2,1,0:T(8,128)(2,1)}), bf16[64,8,640]{2,1,0:T(8,128)(2,1)S(1)}, u32[]{:S(2)}, u32[]{:S(2)}) async-start(bf16[64,8,640]{2,1,0:T(8,128)(2,1)} %bitcast.17), calls=%async_computation | async-start | bytes 1310720 | tf_op jit(solution)/shard_map/all_to_all | solution.py:391
  18.8 18.2 %collective-permute-start = (bf16[6,512]{1,0:T(8,128)(2,1)S(1)}, bf16[6,512]{1,0:T(8,128)(2,1)S(1)}, u32[]{:S(2)}, u32[]{:S(2)}) collective-permute-start(bf16[6,512]{1,0:T(8,128)(2,1)S(1)} %bitcast.21), channel_id=1, source_target_pairs={{0,1},{1,2},{2,3},{3,4},{4,5},{5,6},{6,7},{7,8},{8,9},{9,10},{10,1... | collective-permute-start | bytes 18440 | tf_op jit(solution)/shard_map/ppermute | solution.py:394
  22.8 15.3 %copy-start = (f32[512,128]{1,0:T(8,128)S(1)}, f32[512,128]{1,0:T(8,128)}, u32[]{:S(2)}) copy-start(f32[512,128]{1,0:T(8,128)} %constant.24.clone.twist_ref.twist_any) | copy-start | bytes 786436
  37.0 9.7 %copy-start.2 = (bf16[6,512]{1,0:T(8,128)(2,1)}, bf16[6,512]{1,0:T(8,128)(2,1)S(1)}, u32[]{:S(2)}) copy-start(bf16[6,512]{1,0:T(8,128)(2,1)S(1)} %collective-permute-done.halo_ref) | copy-start | bytes 18436
  46.7 23.2 %all-to-all-start.1 = ((bf16[64,8,512]{2,1,0:T(8,128)(2,1)}), bf16[64,8,512]{2,1,0:T(8,128)(2,1)S(1)}, u32[]{:S(2)}, u32[]{:S(2)}) async-start(bf16[64,8,512]{2,1,0:T(8,128)(2,1)} %bitcast.9), calls=%async_computation.1 | async-start | bytes 1048576 | tf_op jit(solution)/shard_map/all_to_all | solution.py:402

commit v4 on v3

--- a/solution.py
+++ b/solution.py
@@ -181,7 +181,7 @@
             pl.BlockSpec((1, STEP, size), lambda g: (0, g, 0)),
         ],
         out_specs=pl.BlockSpec((STEP, size), lambda g: (g, 0)),
-        out_shape=jax.ShapeDtypeStruct((channels, size), F32),
+        out_shape=pltpu.VMEM((channels, size), F32),
         scratch_shapes=short_scratch(1),
         cost_estimate=pl.CostEstimate(flops=30 * channels * size, bytes_accessed=6 * channels * size, transcendentals=0),
         name="query",
@@ -246,8 +246,8 @@
 
 
 def conv_kernel(
-    x_any, h_any, taps_ref, table_any, twist_any, o_any,
-    grid_ref, edge_ref, res_ref, x_ref, h_ref, table, twist, o_ref, x_sem, h_sem, t_sem, o_sem,
+    x_ref, h_any, taps_ref, table_any, twist_any, o_any,
+    grid_ref, edge_ref, res_ref, h_ref, table, twist, o_ref, h_sem, t_sem, o_sem,
 ):
     own = h_ref.shape[0]
     rows, width = x_ref.shape
@@ -255,10 +255,6 @@
     tiles = width // LANES - 1
     half = blocks // 2
     share = rows // PIECES
-    x_copies = [
-        pltpu.make_async_copy(x_any.at[pl.ds(i * share, share), :], x_ref.at[pl.ds(i * share, share), :], x_sem.at[i])
-        for i in range(PIECES)
-    ]
     cuts = [(0, 4 * N1), (4 * N1, 2 * N1), (BACK, 4 * N1), (GATHER, 2 * LANES)]
     t_copies = [
         pltpu.make_async_copy(table_any.at[pl.ds(at, n), :], table.at[pl.ds(at, n), :], t_sem.at[i])
@@ -268,7 +264,7 @@
     h_copies = [
         pltpu.make_async_copy(h_any.at[pl.ds(2 * i, 2)], h_ref.at[pl.ds(2 * i, 2)], h_sem.at[i]) for i in range(own // 2)
     ]
-    for copy in [*x_copies, t_copies[3], t_copies[0], twist_copy, t_copies[1], *h_copies, t_copies[2]]:
+    for copy in [t_copies[3], t_copies[0], twist_copy, t_copies[1], *h_copies, t_copies[2]]:
         copy.start()
 
     def unpack(i, carry):
@@ -283,9 +279,7 @@
         return carry
 
     per_piece = half // PIECES
-    for i in range(PIECES):
-        x_copies[i].wait()
-        lax.fori_loop(i * per_piece, (i + 1) * per_piece, unpack, 0, unroll=4)
+    lax.fori_loop(0, half, unpack, 0, unroll=8)
 
     edge_ref[:own, :] = jnp.zeros((own, LANES), F32)
     lane = lax.broadcasted_iota(jnp.int32, (rows, LANES), 1)
@@ -355,19 +349,17 @@
     out = (rows, width - LANES)
     return pl.pallas_call(
         conv_kernel,
-        in_specs=[ANY, ANY, pl.BlockSpec(memory_space=pltpu.VMEM), ANY, ANY],
+        in_specs=[pl.BlockSpec(memory_space=pltpu.VMEM), ANY, pl.BlockSpec(memory_space=pltpu.VMEM), ANY, ANY],
         out_specs=ANY,
         out_shape=jax.ShapeDtypeStruct(out, BF16),
         scratch_shapes=[
             pltpu.VMEM((N1 * own, N2), F32),
             pltpu.VMEM((rows + own, LANES), F32),
             pltpu.VMEM((N1 * own, N2), F32),
-            pltpu.VMEM(blocks.shape, BF16),
             pltpu.VMEM(spectrum.shape, F32),
             pltpu.VMEM(table.shape, BF16),
             pltpu.VMEM(twist.shape, F32),
             pltpu.VMEM(out, BF16),
-            pltpu.SemaphoreType.DMA((PIECES,)),
             pltpu.SemaphoreType.DMA((own // 2,)),
             pltpu.SemaphoreType.DMA((5,)),
             pltpu.SemaphoreType.DMA((PIECES,)),

time: 72.5 us -> 70.4 us (0.971)
  Pallas kernels: 25.2 us -> 23.6 us
  other arithmetic: 2.83 us -> 1.6 us
    convert_element_type x1, other arithmetic: 2.18 us -> 0.95 us  [shards(): return (query * back.astype(F32)).astype(BF16)]
    pallas_call x1, Pallas kernels: 8.48 us -> 7.62 us  [conv_call(): pl.pallas_call(conv_kernel, in_specs=[pl.BlockSpec(memory_space=pltpu.VME...]
    pallas_call x1, Pallas kernels: 3.41 us -> 2.63 us  [query_call(): pl.pallas_call(query_kernel, grid=(channels // STEP,), in_specs=[pl.Block...]
    all_to_all x1, waiting for transfers between devices: 13.9 us -> 14.7 us  [shards(): back = lax.all_to_all(convolved, ('ctx', 'half'), 0, 0, tiled=True)]
  transfers between devices with their start and end apart: 3 -> 3, of which waited for: 3 -> 3; matrix products, arithmetic and copies ran while one was open for 3% -> 3% of each run, Pallas kernels for 17% -> 16%
where the time goes in v4:
time: 70.4 us; the launch traced here: 70 us
  Pallas kernels  23.6 us (34%)
  starting transfers between devices  22.3 us (32%)
  waiting for transfers between devices  20.9 us (30%)
  other arithmetic  1.6 us (2%)
  local copies, waits for them, and re-layouts  1.45 us (2%)
    all_to_all x1, waiting for transfers between devices, shards(): back = lax.all_to_all(convolved, ('ctx', 'half'), 0, 0, tiled=True)  14.7 us
    all_to_all x1, starting transfers between devices, shards(): blocks = lax.all_to_all(gated, ('ctx', 'half'), 0, 0, tiled=True)  13.2 us
    pallas_call x1, Pallas kernels, filter_call(): pl.pallas_call(filter_kernel, grid_spec=pltpu.PrefetchScalarGridSpec(num_...  8.81 us
    pallas_call x1, Pallas kernels, conv_call(): pl.pallas_call(conv_kernel, in_specs=[pl.BlockSpec(memory_space=pltpu.VME...  7.62 us
    all_to_all x1, starting transfers between devices, shards(): back = lax.all_to_all(convolved, ('ctx', 'half'), 0, 0, tiled=True)  5.89 us
    ppermute x1, waiting for transfers between devices, shards(): lax.ppermute(tail, ('half', 'ctx'), [(i, i + 1) for i in range(positions...  5.06 us
    pallas_call x1, Pallas kernels, gate_call(): pl.pallas_call(gate_kernel, grid=(channels // STEP,), in_specs=[pl.BlockS...  4.49 us
    ppermute x1, starting transfers between devices, shards(): lax.ppermute(tail, ('half', 'ctx'), [(i, i + 1) for i in range(positions...  3.29 us
  transfers between devices with their start and end apart: 3, of which 3 were waited for; matrix products, arithmetic and copies ran while one was open for 3% of the time, Pallas kernels for 16%

profile of v4, /device:TPU:1, one launch (start us, length us, event | category | flops | bytes accessed | tf_op | source)
XLA Modules:
  0.0 70.0 jit_solution(18429390049775522324)
XLA Ops:
  0.0 0.0 copy-start.1
  0.0 4.5 %gate.1 = bf16[512,640]{1,0:T(8,128)(2,1)} custom-call(f32[3,7,512]{2,1,0:T(8,128)} %bitcast.18, bf16[3,512,512]{2,1,0:T(8,128)(2,1)} %v_ref.1, bf16[3,512,512]{2,1,0:T(8,128)(2,1)} %v_ref.1), custom_call_target="tpu_custom_call" | custom-call | flops 15728640 | bytes 1572864 | tf_op jit(solution)/shard_map/gate/pallas_call | solution.py:141
  4.5 13.2 %all-to-all-start = ((bf16[64,8,640]{2,1,0:T(8,128)(2,1)}), bf16[64,8,640]{2,1,0:T(8,128)(2,1)S(1)}, u32[]{:S(2)}, u32[]{:S(2)}) async-start(bf16[64,8,640]{2,1,0:T(8,128)(2,1)} %bitcast.17), calls=%async_computation | async-start | bytes 1310720 | tf_op jit(solution)/shard_map/all_to_all | solution.py:383
  17.7 1.0 %slice.6 = bf16[1,512,6]{2,1,0:T(8,128)(2,1)S(1)} slice(bf16[3,512,512]{2,1,0:T(8,128)(2,1)} %v_ref.1), slice={[0:1], [0:512], [506:512]} | slice | bytes 12288 | tf_op jit(solution)/shard_map/slice | solution.py:385
  18.7 0.1 copy.12
  18.8 3.3 %collective-permute-start = (bf16[6,512]{1,0:T(8,128)(2,1)S(1)}, bf16[6,512]{1,0:T(8,128)(2,1)S(1)}, u32[]{:S(2)}, u32[]{:S(2)}) collective-permute-start(bf16[6,512]{1,0:T(8,128)(2,1)S(1)} %bitcast.21), channel_id=1, source_target_pairs={{0,1},{1,2},{2,3},{3,4},{4,5},{5,6},{6,7},{7,8},{8,9},{9,10},{10,1... | collective-permute-start | bytes 18440 | tf_op jit(solution)/shard_map/ppermute | solution.py:386
  22.1 0.0 copy-done.1
  22.1 0.6 pad_add_fusion.place_ref
  22.8 0.1 dynamic-slice_bitcast_fusion
  22.8 0.0 copy-start
  22.8 8.8 %filter_spectrum.1.h_any = f32[8,256,256]{2,1,0:T(8,128)} custom-call(s32[2]{0:T(128)} %pad_add_fusion.place_ref, f32[512]{0:T(512)} %skip_ref.1, f32[16,32768]{1,0:T(8,128)} %f_ref.1, bf16[2816,256]{1,0:T(8,128)(2,1)} %constant.23.clone.table_any, f32[512,128]{1,0:T(8,128)} %constant.24.clone.twist_ref.twist_any), custom_call_target="tpu_custom_call" | custom-call | flops 1610612736 | bytes 6291456 | tf_op jit(solution)/shard_map/filter_spectrum/pallas_call | solution.py:224
  31.7 0.1 copy.11
  31.7 0.1 broadcast_in_dim.3
  31.8 0.1 reshape.13.taps_ref
  31.9 5.1 %collective-permute-done.halo_ref = bf16[6,512]{1,0:T(8,128)(2,1)S(1)} collective-permute-done((bf16[6,512]{1,0:T(8,128)(2,1)S(1)}, bf16[6,512]{1,0:T(8,128)(2,1)S(1)}, u32[]{:S(2)}, u32[]{:S(2)}) %collective-permute-start) | collective-permute-done | bytes 6176 | tf_op jit(solution)/shard_map/ppermute | solution.py:386
  37.0 0.0 copy-start.2
  37.0 1.2 %all-to-all-done = bf16[64,8,640]{2,1,0:T(8,128)(2,1)S(1)} async-done(((bf16[64,8,640]{2,1,0:T(8,128)(2,1)}), bf16[64,8,640]{2,1,0:T(8,128)(2,1)S(1)}, u32[]{:S(2)}, u32[]{:S(2)}) %all-to-all-start) | async-done | bytes 655392 | tf_op jit(solution)/shard_map/all_to_all | solution.py:383
  38.2 0.0 copy-done
  38.2 7.6 %long_convolution.1 = bf16[512,512]{1,0:T(8,128)(2,1)} custom-call(bf16[512,640]{1,0:T(8,128)(2,1)S(1)} %bitcast.16, f32[8,256,256]{2,1,0:T(8,128)} %filter_spectrum.1.h_any, f32[8,128]{1,0:T(8,128)S(1)} %reshape.13.taps_ref, bf16[2816,256]{1,0:T(8,128)(2,1)} %constant.23.clone.table_any, f32[512,128]{1,0:T(8,128)S(1)} %copy-done), custom_call_target="tpu_custom_call" | custom-call | flops 2952790016 | bytes 6291456 | tf_op jit(solution)/shard_map/long_convolution/pallas_call | solution.py:350
  45.8 0.0 copy-done.2
  45.8 5.9 %all-to-all-start.1 = ((bf16[64,8,512]{2,1,0:T(8,128)(2,1)}), bf16[64,8,512]{2,1,0:T(8,128)(2,1)S(1)}, u32[]{:S(2)}, u32[]{:S(2)}) async-start(bf16[64,8,512]{2,1,0:T(8,128)(2,1)} %bitcast.9), calls=%async_computation.1 | async-start | bytes 1048576 | tf_op jit(solution)/shard_map/all_to_all | solution.py:394
  51.7 2.6 %query.1 = f32[512,512]{1,0:T(8,128)S(1)} custom-call(f32[3,7,512]{2,1,0:T(8,128)} %bitcast.19, bf16[6,512]{1,0:T(8,128)(2,1)} %copy-done.2, bf16[3,512,512]{2,1,0:T(8,128)(2,1)} %v_ref.1), custom_call_target="tpu_custom_call" | custom-call | flops 7864320 | bytes 1572864 | tf_op jit(solution)/shard_map/query/pallas_call | solution.py:175
  54.4 14.7 %all-to-all-done.1 = bf16[64,8,512]{2,1,0:T(8,128)(2,1)S(1)} async-done(((bf16[64,8,512]{2,1,0:T(8,128)(2,1)}), bf16[64,8,512]{2,1,0:T(8,128)(2,1)S(1)}, u32[]{:S(2)}, u32[]{:S(2)}) %all-to-all-start.1) | async-done | bytes 524320 | tf_op jit(solution)/shard_map/all_to_all | solution.py:394
  69.0 1.0 %fusion = bf16[512,512]{1,0:T(8,128)(2,1)} fusion(f32[512,512]{1,0:T(8,128)S(1)} %query.1, bf16[64,8,512]{2,1,0:T(8,128)(2,1)S(1)} %all-to-all-done.1), kind=kLoop, calls=%fused_computation.1 | loop fusion | flops 786432 | bytes 2097152 | tf_op jit(solution)/shard_map/convert_element_type | solution.py:396
  (2 shorter events, 0.0 us)
Async XLA Ops:
  0.0 22.1 %copy-start.1 = (f32[7,3,512]{2,0,1:T(8,128)S(1)}, f32[7,3,512]{2,0,1:T(8,128)}, u32[]{:S(2)}) copy-start(f32[7,3,512]{2,0,1:T(8,128)} %param.7) | copy-start | bytes 129028
  4.5 33.7 %all-to-all-start = ((bf16[64,8,640]{2,1,0:T(8,128)(2,1)}), bf16[64,8,640]{2,1,0:T(8,128)(2,1)S(1)}, u32[]{:S(2)}, u32[]{:S(2)}) async-start(bf16[64,8,640]{2,1,0:T(8,128)(2,1)} %bitcast.17), calls=%async_computation | async-start | bytes 1310720 | tf_op jit(solution)/shard_map/all_to_all | solution.py:383
  18.8 18.2 %collective-permute-start = (bf16[6,512]{1,0:T(8,128)(2,1)S(1)}, bf16[6,512]{1,0:T(8,128)(2,1)S(1)}, u32[]{:S(2)}, u32[]{:S(2)}) collective-permute-start(bf16[6,512]{1,0:T(8,128)(2,1)S(1)} %bitcast.21), channel_id=1, source_target_pairs={{0,1},{1,2},{2,3},{3,4},{4,5},{5,6},{6,7},{7,8},{8,9},{9,10},{10,1... | collective-permute-start | bytes 18440 | tf_op jit(solution)/shard_map/ppermute | solution.py:386
  22.8 15.3 %copy-start = (f32[512,128]{1,0:T(8,128)S(1)}, f32[512,128]{1,0:T(8,128)}, u32[]{:S(2)}) copy-start(f32[512,128]{1,0:T(8,128)} %constant.24.clone.twist_ref.twist_any) | copy-start | bytes 786436
  37.0 8.8 %copy-start.2 = (bf16[6,512]{1,0:T(8,128)(2,1)}, bf16[6,512]{1,0:T(8,128)(2,1)S(1)}, u32[]{:S(2)}) copy-start(bf16[6,512]{1,0:T(8,128)(2,1)S(1)} %collective-permute-done.halo_ref) | copy-start | bytes 18436
  45.8 23.2 %all-to-all-start.1 = ((bf16[64,8,512]{2,1,0:T(8,128)(2,1)}), bf16[64,8,512]{2,1,0:T(8,128)(2,1)S(1)}, u32[]{:S(2)}, u32[]{:S(2)}) async-start(bf16[64,8,512]{2,1,0:T(8,128)(2,1)} %bitcast.9), calls=%async_computation.1 | async-start | bytes 1048576 | tf_op jit(solution)/shard_map/all_to_all | solution.py:394

commit v5 on v4

--- a/solution.py
+++ b/solution.py
@@ -38,7 +38,7 @@
         for j in range(TAPS):
             for t in range(EDGE):
                 at = branch * LANES // 2 + j * 8 + t
-                gather[branch * LANES // 2 + EDGE + t - j, at] = 1
+                gather[branch * LANES // 4 + EDGE + t - j, at] = 1
                 add[at, branch * LANES + t] = 1
     exact = [gather.astype(ml_dtypes.bfloat16), add.astype(ml_dtypes.bfloat16)]
     table = np.concatenate([*halves(rows), *halves(columns), *halves(back), *exact], 0)
@@ -72,6 +72,14 @@
     return pl.ds(pl.multiple_of(i * count, count), count)
 
 
+GROUP = 8
+PAIR = 2 * GROUP
+
+
+def block_rows(tiles):
+    return tiles * PAIR + GROUP
+
+
 STEP = 256
 
 
@@ -92,11 +100,20 @@
     return mm(columns.astype(BF16), spread)
 
 
+BY_MATRIX = 4
+
+
 def shaped_tile(previous, current, taps, shift):
-    moved = mm(jnp.concatenate([previous, current], 1), shift)
-    total = taps[:, :LANES] * current.astype(F32)
+    moved = mm(jnp.concatenate([previous, current], 1), shift[:, : BY_MATRIX * LANES])
+    before, here = previous.astype(F32), current.astype(F32)
+    lane = lax.broadcasted_iota(jnp.int32, here.shape, 1)
+    total = taps[:, :LANES] * here
     for j in range(1, TAPS):
-        total = total + taps[:, j * LANES : (j + 1) * LANES] * moved[:, (j - 1) * LANES : j * LANES]
+        if j <= BY_MATRIX:
+            x = moved[:, (j - 1) * LANES : j * LANES]
+        else:
+            x = pltpu.roll(jnp.where(lane >= LANES - j, before, here), j, 1)
+        total = total + taps[:, j * LANES : (j + 1) * LANES] * x
     return total
 
 
@@ -114,23 +131,32 @@
     def tile(ref, q):
         return ref[0, :, q * LANES : (q + 1) * LANES]
 
+    each = block_rows(tiles)
+    blocks = STEP // PAIR
     for q in range(tiles):
         key = shaped_tile(tile(k_ref, (q - 1) % tiles), tile(k_ref, q), ktaps[...], shift[...])
         value = shaped_tile(tile(v_ref, (q - 1) % tiles), tile(v_ref, q), vtaps[...], shift[...])
-        o_ref[:, q * LANES : (q + 1) * LANES] = (key * value).astype(BF16)
+        gated = (key * value).astype(BF16)
+        for d in range(blocks):
+            o_ref[d * each + q * PAIR : d * each + (q + 1) * PAIR, :] = gated[d * PAIR : (d + 1) * PAIR]
     lane = lax.broadcasted_iota(jnp.int32, (STEP, LANES), 1)
 
     def edges(ref, by):
         ends = jnp.where(lane >= LANES - EDGE, tile(ref, tiles - 1).astype(F32), tile(ref, 0).astype(F32))
         return pltpu.roll(ends, by, 1)
 
-    both = jnp.where(lane < LANES // 2, edges(k_ref, EDGE), edges(v_ref, EDGE + LANES // 2))
-    o_ref[:, size:] = both.astype(BF16)
+    both = jnp.where(lane < LANES // 4, edges(k_ref, EDGE), edges(v_ref, EDGE + LANES // 4))
+    moved = pltpu.roll(both, LANES // 2, 1)
+    lane = lax.broadcasted_iota(jnp.int32, (GROUP, LANES), 1)
+    for d in range(blocks):
+        at = d * PAIR
+        first, second = both[at : at + GROUP], moved[at + GROUP : at + PAIR]
+        o_ref[d * each + tiles * PAIR : (d + 1) * each, :] = jnp.where(lane < LANES // 2, first, second).astype(BF16)
 
 
 def short_scratch(count):
     return [
-        pltpu.VMEM((2 * LANES, EDGE * LANES), BF16),
+        pltpu.VMEM((2 * LANES, BY_MATRIX * LANES), BF16),
         pltpu.VMEM((LANES, TAPS * LANES), BF16),
         *[pltpu.VMEM((STEP, TAPS * LANES), F32)] * count,
     ]
@@ -138,6 +164,7 @@
 
 def gate_call(features, taps):
     _, channels, size = features.shape
+    each = block_rows(size // LANES)
     return pl.pallas_call(
         gate_kernel,
         grid=(channels // STEP,),
@@ -146,8 +173,8 @@
             pl.BlockSpec((1, STEP, size), lambda g: (1, g, 0)),
             pl.BlockSpec((1, STEP, size), lambda g: (2, g, 0)),
         ],
-        out_specs=pl.BlockSpec((STEP, size + LANES), lambda g: (g, 0)),
-        out_shape=jax.ShapeDtypeStruct((channels, size + LANES), BF16),
+        out_specs=pl.BlockSpec((STEP // PAIR * each, LANES), lambda g: (g, 0)),
+        out_shape=jax.ShapeDtypeStruct((channels // PAIR * each, LANES), BF16),
         scratch_shapes=short_scratch(2),
         compiler_params=pltpu.CompilerParams(vmem_limit_bytes=VMEM_LIMIT),
         cost_estimate=pl.CostEstimate(flops=60 * channels * size, bytes_accessed=6 * channels * size, transcendentals=0),
@@ -246,15 +273,16 @@
 
 
 def conv_kernel(
-    x_ref, h_any, taps_ref, table_any, twist_any, o_any,
+    half_ref, own_ref, other_ref, h_any, taps_ref, table_any, twist_any, o_any,
     grid_ref, edge_ref, res_ref, h_ref, table, twist, o_ref, h_sem, t_sem, o_sem,
 ):
     own = h_ref.shape[0]
-    rows, width = x_ref.shape
+    rows, size = o_ref.shape
     blocks = rows // own
-    tiles = width // LANES - 1
+    tiles = size // LANES
     half = blocks // 2
     share = rows // PIECES
+    per_piece = half // PIECES
     cuts = [(0, 4 * N1), (4 * N1, 2 * N1), (BACK, 4 * N1), (GATHER, 2 * LANES)]
     t_copies = [
         pltpu.make_async_copy(table_any.at[pl.ds(at, n), :], table.at[pl.ds(at, n), :], t_sem.at[i])
@@ -267,23 +295,20 @@
     for copy in [t_copies[3], t_copies[0], twist_copy, t_copies[1], *h_copies, t_copies[2]]:
         copy.start()
 
-    def unpack(i, carry):
-        for q in range(tiles + 1):
-            tile = x_ref[rows_at(i, 2 * own), q * LANES : (q + 1) * LANES].astype(F32)
-            for h in range(2):
-                place = i + h * half
-                if q < tiles:
-                    grid_ref[rows_at(place * tiles + q, own), :] = tile[h * own : (h + 1) * own]
-                else:
-                    edge_ref[rows_at(place + 1, own), :] = tile[h * own : (h + 1) * own]
-        return carry
-
-    per_piece = half // PIECES
-    lax.fori_loop(0, half, unpack, 0, unroll=8)
+    place = half_ref[0]
+    each = block_rows(tiles)
+    for ref, side in ((own_ref, place), (other_ref, 1 - place)):
+        for i in range(half):
+            to = i + side * half
+            for q in range(tiles):
+                tile = ref[i * each + q * PAIR : i * each + (q + 1) * PAIR, :].astype(F32)
+                grid_ref[rows_at(to * tiles + q, own), :] = jnp.where(place == 0, tile[:own], tile[own:])
+            edge = ref[i * each + tiles * PAIR : (i + 1) * each, :].astype(F32)
+            edge_ref[rows_at(to + 1, own), :] = jnp.where(place == 0, edge, pltpu.roll(edge, LANES // 2, 1))
 
     edge_ref[:own, :] = jnp.zeros((own, LANES), F32)
     lane = lax.broadcasted_iota(jnp.int32, (rows, LANES), 1)
-    both = jnp.where(lane % (LANES // 2) < EDGE, edge_ref[:rows, :], edge_ref[own:, :]).astype(BF16)
+    both = jnp.where(lane % (LANES // 4) < EDGE, edge_ref[:rows, :], edge_ref[own:, :]).astype(BF16)
     t_copies[3].wait()
     terms = mm(both, table[GATHER : GATHER + LANES, :LANES]).reshape(blocks, own, LANES) * taps_ref[...][None]
     hi, lo = split(terms.reshape(rows, LANES))
@@ -327,15 +352,13 @@
         for a in range(2):
             res_ref[pl.ds(2 * c + a, N1, stride=own), :] = y[:, a * N2 : (a + 1) * N2]
 
-    def pack(i, carry):
-        for q in range(tiles):
-            tile = [res_ref[rows_at((i + h * half) * tiles + q, own), :] for h in range(2)]
-            o_ref[rows_at(i, 2 * own), q * LANES : (q + 1) * LANES] = jnp.concatenate(tile, 0).astype(BF16)
-        return carry
-
     o_copies = []
     for i in range(PIECES):
-        lax.fori_loop(i * per_piece, (i + 1) * per_piece, pack, 0, unroll=4)
+        for g in range(i * per_piece, (i + 1) * per_piece):
+            for q in range(tiles):
+                at = [((g + h * half) * tiles + q) * own for h in range(2)]
+                tile = jnp.concatenate([res_ref[a : a + own, :] for a in at], 0)
+                o_ref[g * 2 * own : (g + 1) * 2 * own, q * LANES : (q + 1) * LANES] = tile.astype(BF16)
         piece = pl.ds(i * share, share)
         o_copies.append(pltpu.make_async_copy(o_ref.at[piece, :], o_any.at[piece, :], o_sem.at[i]))
         o_copies[-1].start()
@@ -343,13 +366,13 @@
         copy.wait()
 
 
-def conv_call(blocks, spectrum, taps, table, twist):
+def conv_call(half_place, blocks, others, spectrum, taps, table, twist, out):
     own = spectrum.shape[0]
-    rows, width = blocks.shape
-    out = (rows, width - LANES)
+    rows = out[0]
+    vmem = pl.BlockSpec(memory_space=pltpu.VMEM)
     return pl.pallas_call(
         conv_kernel,
-        in_specs=[pl.BlockSpec(memory_space=pltpu.VMEM), ANY, pl.BlockSpec(memory_space=pltpu.VMEM), ANY, ANY],
+        in_specs=[pl.BlockSpec(memory_space=pltpu.SMEM), vmem, vmem, ANY, vmem, ANY, ANY],
         out_specs=ANY,
         out_shape=jax.ShapeDtypeStruct(out, BF16),
         scratch_shapes=[
@@ -367,7 +390,7 @@
         compiler_params=pltpu.CompilerParams(vmem_limit_bytes=CONV_LIMIT),
         cost_estimate=pl.CostEstimate(flops=22 * own * N1 * N1 * 2 * N2, bytes_accessed=6 << 20, transcendentals=0),
         name="long_convolution",
-    )(blocks, spectrum, taps, table, twist)
+    )(half_place.reshape(1).astype(jnp.int32), blocks, others, spectrum, taps, table, twist)
 
 
 def shards(features, short_taps, filters, skip):
@@ -380,7 +403,7 @@
     taps = jnp.swapaxes(short_taps, 0, 1)
 
     gated = gate_call(features, taps)
-    blocks = lax.all_to_all(gated, ("ctx", "half"), 0, 0, tiled=True)
+    blocks = lax.all_to_all(gated, "ctx", 0, 0, tiled=True)
 
     tail = features[0, :, size - EDGE :].T
     halo = lax.ppermute(tail, ("half", "ctx"), [(i, i + 1) for i in range(positions - 1)])
@@ -388,9 +411,11 @@
     own_taps = lax.dynamic_slice_in_dim(taps[1:], first_channel, own, 2)
     own_taps = jnp.pad(own_taps.transpose(2, 0, 1), ((0, 0), (0, 0), (0, 8 - TAPS)))
     own_taps = jnp.repeat(own_taps.reshape(own, 16), 8, axis=1)
-    halo, spectrum = lax.optimization_barrier((halo, spectrum))
-
-    convolved = conv_call(blocks, spectrum, own_taps, table, twist)
+    blocks, halo, spectrum, own_taps = lax.optimization_barrier((blocks, halo, spectrum, own_taps))
+    others = lax.ppermute(blocks, "half", [(0, 1), (1, 0)])
+
+    out = (positions * own, size)
+    convolved = conv_call(half_place, blocks, others, spectrum, own_taps, table, twist, out)
     back = lax.all_to_all(convolved, ("ctx", "half"), 0, 0, tiled=True)
     query = query_call(features, taps, halo)
     return (query * back.astype(F32)).astype(BF16)

time: 70.4 us -> 69.7 us (0.990)
  waiting for transfers between devices: 20.9 us -> 19.6 us
  starting transfers between devices: 22.3 us -> 23.5 us
    ppermute x0 -> x1, starting transfers between devices: none -> 2.83 us  [shards(): others = lax.ppermute(blocks, 'half', [(0, 1), (1, 0)])]
    ppermute x1, waiting for transfers between devices: 5.06 us -> 2.98 us  [shards(): lax.ppermute(tail, ('half', 'ctx'), [(i, i + 1) for i in range(positions...]
    ppermute x0 -> x1, waiting for transfers between devices: none -> 1.63 us  [shards(): others = lax.ppermute(blocks, 'half', [(0, 1), (1, 0)])]
    all_to_all x1, waiting for transfers between devices: 1.19 us -> 0.01 us  [shards(): blocks = lax.all_to_all(gated, 'ctx', 0, 0, tiled=True)]
    all_to_all x1, starting transfers between devices: 13.2 us -> 12 us  [shards(): blocks = lax.all_to_all(gated, 'ctx', 0, 0, tiled=True)]
  transfers between devices with their start and end apart: 3 -> 4, of which waited for: 3 -> 3; matrix products, arithmetic and copies ran while one was open for 3% -> 3% of each run, Pallas kernels for 16% -> 16%
where the time goes in v5:
time: 69.7 us; the launch traced here: 69.3 us
  starting transfers between devices  23.5 us (34%)
  Pallas kernels  23.1 us (33%)
  waiting for transfers between devices  19.6 us (28%)
  other arithmetic  1.53 us (2%)
  local copies, waits for them, and re-layouts  1.45 us (2%)
    all_to_all x1, waiting for transfers between devices, shards(): back = lax.all_to_all(convolved, ('ctx', 'half'), 0, 0, tiled=True)  15 us
    all_to_all x1, starting transfers between devices, shards(): blocks = lax.all_to_all(gated, 'ctx', 0, 0, tiled=True)  12 us
    pallas_call x1, Pallas kernels, filter_call(): pl.pallas_call(filter_kernel, grid_spec=pltpu.PrefetchScalarGridSpec(num_...  8.81 us
    pallas_call x1, Pallas kernels, conv_call(): pl.pallas_call(conv_kernel, in_specs=[pl.BlockSpec(memory_space=pltpu.SME...  7.58 us
    all_to_all x1, starting transfers between devices, shards(): back = lax.all_to_all(convolved, ('ctx', 'half'), 0, 0, tiled=True)  5.55 us
    pallas_call x1, Pallas kernels, gate_call(): pl.pallas_call(gate_kernel, grid=(channels // STEP,), in_specs=[pl.BlockS...  4.32 us
    ppermute x1, starting transfers between devices, shards(): lax.ppermute(tail, ('half', 'ctx'), [(i, i + 1) for i in range(positions...  3.14 us
    ppermute x1, waiting for transfers between devices, shards(): lax.ppermute(tail, ('half', 'ctx'), [(i, i + 1) for i in range(positions...  2.98 us
  transfers between devices with their start and end apart: 4, of which 3 were waited for; matrix products, arithmetic and copies ran while one was open for 3% of the time, Pallas kernels for 16%

profile of v5, /device:TPU:1, one launch (start us, length us, event | category | flops | bytes accessed | tf_op | source)
XLA Modules:
  0.0 69.3 jit_solution(8253228606929487219)
XLA Ops:
  0.0 0.0 copy-start.1
  0.0 4.3 %gate.1 = bf16[2304,128]{1,0:T(8,128)(2,1)} custom-call(f32[3,7,512]{2,1,0:T(8,128)} %bitcast.19, bf16[3,512,512]{2,1,0:T(8,128)(2,1)} %q_ref.1, bf16[3,512,512]{2,1,0:T(8,128)(2,1)} %q_ref.1), custom_call_target="tpu_custom_call" | custom-call | flops 15728640 | bytes 1572864 | tf_op jit(solution)/shard_map/gate/pallas_call | solution.py:168
  4.3 12.0 %all-to-all-start = ((bf16[32,72,128]{2,1,0:T(8,128)(2,1)}), bf16[32,72,128]{2,1,0:T(8,128)(2,1)S(1)}, u32[]{:S(2)}, u32[]{:S(2)}) async-start(bf16[32,72,128]{2,1,0:T(8,128)(2,1)} %bitcast.18), calls=%async_computation | async-start | bytes 1179648 | tf_op jit(solution)/shard_map/all_to_all | solution.py:406
  16.4 1.0 %slice.6 = bf16[1,512,6]{2,1,0:T(8,128)(2,1)S(1)} slice(bf16[3,512,512]{2,1,0:T(8,128)(2,1)} %q_ref.1), slice={[0:1], [0:512], [506:512]} | slice | bytes 12288 | tf_op jit(solution)/shard_map/slice | solution.py:408
  17.4 0.1 copy.12
  17.5 3.1 %collective-permute-start = (bf16[6,512]{1,0:T(8,128)(2,1)S(1)}, bf16[6,512]{1,0:T(8,128)(2,1)S(1)}, u32[]{:S(2)}, u32[]{:S(2)}) collective-permute-start(bf16[6,512]{1,0:T(8,128)(2,1)S(1)} %bitcast.22), channel_id=1, source_target_pairs={{0,1},{1,2},{2,3},{3,4},{4,5},{5,6},{6,7},{7,8},{8,9},{9,10},{10,1... | collective-permute-start | bytes 18440 | tf_op jit(solution)/shard_map/ppermute | solution.py:409
  20.6 0.0 copy-done.1
  20.7 0.6 pad_add_fusion.place_ref
  21.2 0.1 dynamic-slice_bitcast_fusion
  21.3 0.0 copy-start
  21.3 8.8 %filter_spectrum.1.h_any = f32[8,256,256]{2,1,0:T(8,128)} custom-call(s32[2]{0:T(128)} %pad_add_fusion.place_ref, f32[512]{0:T(512)} %skip_ref.1, f32[16,32768]{1,0:T(8,128)} %f_ref.1, bf16[2816,256]{1,0:T(8,128)(2,1)} %constant.23.clone.table_any, f32[512,128]{1,0:T(8,128)} %constant.24.clone.twist_ref.twist_any), custom_call_target="tpu_custom_call" | custom-call | flops 1610612736 | bytes 6291456 | tf_op jit(solution)/shard_map/filter_spectrum/pallas_call | solution.py:251
  30.1 0.1 copy.11
  30.2 0.1 broadcast_in_dim.3
  30.3 0.1 reshape.14.taps_ref
  30.4 3.0 %collective-permute-done.halo_ref = bf16[6,512]{1,0:T(8,128)(2,1)S(1)} collective-permute-done((bf16[6,512]{1,0:T(8,128)(2,1)S(1)}, bf16[6,512]{1,0:T(8,128)(2,1)S(1)}, u32[]{:S(2)}, u32[]{:S(2)}) %collective-permute-start) | collective-permute-done | bytes 6176 | tf_op jit(solution)/shard_map/ppermute | solution.py:409
  33.4 0.0 copy-start.2
  33.4 0.0 all-to-all-done
  33.4 2.8 %collective-permute-start.1 = (bf16[2304,128]{1,0:T(8,128)(2,1)S(1)}, bf16[2304,128]{1,0:T(8,128)(2,1)S(1)}, u32[]{:S(2)}, u32[]{:S(2)}) collective-permute-start(bf16[2304,128]{1,0:T(8,128)(2,1)S(1)} %bitcast.16), channel_id=1, source_target_pairs={{0,32},{32,0},{1,33},{33,1},{2,34},{34,2},{3,35},{35,3},{4,36},{36... | collective-permute-start | bytes 1769480 | tf_op jit(solution)/shard_map/ppermute | solution.py:415
  36.2 1.6 %collective-permute-done.1.other_ref = bf16[2304,128]{1,0:T(8,128)(2,1)S(1)} collective-permute-done((bf16[2304,128]{1,0:T(8,128)(2,1)S(1)}, bf16[2304,128]{1,0:T(8,128)(2,1)S(1)}, u32[]{:S(2)}, u32[]{:S(2)}) %collective-permute-start.1) | collective-permute-done | bytes 589856 | tf_op jit(solution)/shard_map/ppermute | solution.py:415
  37.8 0.0 copy-done
  37.8 7.6 %long_convolution.1 = bf16[512,512]{1,0:T(8,128)(2,1)} custom-call(s32[1]{0:T(128)} %bitcast.5.half_ref, bf16[2304,128]{1,0:T(8,128)(2,1)S(1)} %bitcast.17, bf16[2304,128]{1,0:T(8,128)(2,1)S(1)} %collective-permute-done.1.other_ref, f32[8,256,256]{2,1,0:T(8,128)} %filter_spectrum.1.h_any, f32[8,128]{1,0:T(8,128)S(1)} %reshape.14.taps_ref, ...), custom_call_target="tpu_custom_call" | custom-call | flops 2952790016 | bytes 6291456 | tf_op jit(solution)/shard_map/long_convolution/pallas_call | solution.py:373
  45.4 0.0 copy-done.2
  45.4 5.5 %all-to-all-start.1 = ((bf16[64,8,512]{2,1,0:T(8,128)(2,1)}), bf16[64,8,512]{2,1,0:T(8,128)(2,1)S(1)}, u32[]{:S(2)}, u32[]{:S(2)}) async-start(bf16[64,8,512]{2,1,0:T(8,128)(2,1)} %bitcast.9), calls=%async_computation.1 | async-start | bytes 1048576 | tf_op jit(solution)/shard_map/all_to_all | solution.py:419
  51.0 2.4 %query.1 = f32[512,512]{1,0:T(8,128)S(1)} custom-call(f32[3,7,512]{2,1,0:T(8,128)} %bitcast.20, bf16[6,512]{1,0:T(8,128)(2,1)} %copy-done.2, bf16[3,512,512]{2,1,0:T(8,128)(2,1)} %q_ref.1), custom_call_target="tpu_custom_call" | custom-call | flops 7864320 | bytes 1572864 | tf_op jit(solution)/shard_map/query/pallas_call | solution.py:202
  53.4 15.0 %all-to-all-done.1 = bf16[64,8,512]{2,1,0:T(8,128)(2,1)S(1)} async-done(((bf16[64,8,512]{2,1,0:T(8,128)(2,1)}), bf16[64,8,512]{2,1,0:T(8,128)(2,1)S(1)}, u32[]{:S(2)}, u32[]{:S(2)}) %all-to-all-start.1) | async-done | bytes 524320 | tf_op jit(solution)/shard_map/all_to_all | solution.py:419
  68.3 1.0 %fusion = bf16[512,512]{1,0:T(8,128)(2,1)} fusion(f32[512,512]{1,0:T(8,128)S(1)} %query.1, bf16[64,8,512]{2,1,0:T(8,128)(2,1)S(1)} %all-to-all-done.1), kind=kLoop, calls=%fused_computation.1 | loop fusion | flops 786432 | bytes 2097152 | tf_op jit(solution)/shard_map/convert_element_type | solution.py:421
  (2 shorter events, 0.0 us)
Async XLA Ops:
  0.0 20.6 %copy-start.1 = (f32[7,3,512]{2,0,1:T(8,128)S(1)}, f32[7,3,512]{2,0,1:T(8,128)}, u32[]{:S(2)}) copy-start(f32[7,3,512]{2,0,1:T(8,128)} %param.7) | copy-start | bytes 129028
  4.3 29.1 %all-to-all-start = ((bf16[32,72,128]{2,1,0:T(8,128)(2,1)}), bf16[32,72,128]{2,1,0:T(8,128)(2,1)S(1)}, u32[]{:S(2)}, u32[]{:S(2)}) async-start(bf16[32,72,128]{2,1,0:T(8,128)(2,1)} %bitcast.18), calls=%async_computation | async-start | bytes 1179648 | tf_op jit(solution)/shard_map/all_to_all | solution.py:406
  17.5 15.9 %collective-permute-start = (bf16[6,512]{1,0:T(8,128)(2,1)S(1)}, bf16[6,512]{1,0:T(8,128)(2,1)S(1)}, u32[]{:S(2)}, u32[]{:S(2)}) collective-permute-start(bf16[6,512]{1,0:T(8,128)(2,1)S(1)} %bitcast.22), channel_id=1, source_target_pairs={{0,1},{1,2},{2,3},{3,4},{4,5},{5,6},{6,7},{7,8},{8,9},{9,10},{10,1... | collective-permute-start | bytes 18440 | tf_op jit(solution)/shard_map/ppermute | solution.py:409
  21.3 16.5 %copy-start = (f32[512,128]{1,0:T(8,128)S(1)}, f32[512,128]{1,0:T(8,128)}, u32[]{:S(2)}) copy-start(f32[512,128]{1,0:T(8,128)} %constant.24.clone.twist_ref.twist_any) | copy-start | bytes 786436
  33.4 12.1 %copy-start.2 = (bf16[6,512]{1,0:T(8,128)(2,1)}, bf16[6,512]{1,0:T(8,128)(2,1)S(1)}, u32[]{:S(2)}) copy-start(bf16[6,512]{1,0:T(8,128)(2,1)S(1)} %collective-permute-done.halo_ref) | copy-start | bytes 18436
  33.4 4.5 %collective-permute-start.1 = (bf16[2304,128]{1,0:T(8,128)(2,1)S(1)}, bf16[2304,128]{1,0:T(8,128)(2,1)S(1)}, u32[]{:S(2)}, u32[]{:S(2)}) collective-permute-start(bf16[2304,128]{1,0:T(8,128)(2,1)S(1)} %bitcast.16), channel_id=1, source_target_pairs={{0,32},{32,0},{1,33},{33,1},{2,34},{34,2},{3,35},{35,3},{4,36},{36... | collective-permute-start | bytes 1769480 | tf_op jit(solution)/shard_map/ppermute | solution.py:415
  45.4 22.9 %all-to-all-start.1 = ((bf16[64,8,512]{2,1,0:T(8,128)(2,1)}), bf16[64,8,512]{2,1,0:T(8,128)(2,1)S(1)}, u32[]{:S(2)}, u32[]{:S(2)}) async-start(bf16[64,8,512]{2,1,0:T(8,128)(2,1)} %bitcast.9), calls=%async_computation.1 | async-start | bytes 1048576 | tf_op jit(solution)/shard_map/all_to_all | solution.py:419

commit v6 on v5

--- a/solution.py
+++ b/solution.py
@@ -51,7 +51,7 @@
 GATHER = 10 * N1
 FORWARD = slice(0, BACK)
 VMEM_LIMIT = 60 * 1024 * 1024
-CONV_LIMIT = 54525952
+CONV_LIMIT = 52428800
 
 
 def mm(a, b):
@@ -273,8 +273,8 @@
 
 
 def conv_kernel(
-    half_ref, own_ref, other_ref, h_any, taps_ref, table_any, twist_any, o_any,
-    grid_ref, edge_ref, res_ref, h_ref, table, twist, o_ref, h_sem, t_sem, o_sem,
+    half_ref, own_ref, other_ref, h_any, taps_ref, table, twist, o_any,
+    grid_ref, edge_ref, res_ref, h_ref, o_ref, h_sem, o_sem,
 ):
     own = h_ref.shape[0]
     rows, size = o_ref.shape
@@ -283,17 +283,8 @@
     half = blocks // 2
     share = rows // PIECES
     per_piece = half // PIECES
-    cuts = [(0, 4 * N1), (4 * N1, 2 * N1), (BACK, 4 * N1), (GATHER, 2 * LANES)]
-    t_copies = [
-        pltpu.make_async_copy(table_any.at[pl.ds(at, n), :], table.at[pl.ds(at, n), :], t_sem.at[i])
-        for i, (at, n) in enumerate(cuts)
-    ]
-    twist_copy = pltpu.make_async_copy(twist_any, twist, t_sem.at[len(cuts)])
-    h_copies = [
-        pltpu.make_async_copy(h_any.at[pl.ds(2 * i, 2)], h_ref.at[pl.ds(2 * i, 2)], h_sem.at[i]) for i in range(own // 2)
-    ]
-    for copy in [t_copies[3], t_copies[0], twist_copy, t_copies[1], *h_copies, t_copies[2]]:
-        copy.start()
+    h_copy = pltpu.make_async_copy(h_any, h_ref, h_sem)
+    h_copy.start()
 
     place = half_ref[0]
     each = block_rows(tiles)
@@ -309,7 +300,6 @@
     edge_ref[:own, :] = jnp.zeros((own, LANES), F32)
     lane = lax.broadcasted_iota(jnp.int32, (rows, LANES), 1)
     both = jnp.where(lane % (LANES // 4) < EDGE, edge_ref[:rows, :], edge_ref[own:, :]).astype(BF16)
-    t_copies[3].wait()
     terms = mm(both, table[GATHER : GATHER + LANES, :LANES]).reshape(blocks, own, LANES) * taps_ref[...][None]
     hi, lo = split(terms.reshape(rows, LANES))
     add = table[GATHER + LANES : GATHER + 2 * LANES]
@@ -319,8 +309,6 @@
         grid_ref[p * tiles * own : (p * tiles + 1) * own, :EDGE] = gated[p * own : (p + 1) * own, :EDGE]
 
     pairs = range(own // 2)
-    t_copies[0].wait()
-    twist_copy.wait()
     twr, twi = twist[:N1], twist[N1:]
     turned = []
     for c in pairs:
@@ -329,18 +317,15 @@
         for a in range(2):
             re, im = part[:N1, a * N2 : (a + 1) * N2], part[N1:, a * N2 : (a + 1) * N2]
             turned.append(jnp.concatenate([re * twr - im * twi, re * twi + im * twr], 1))
-    t_copies[1].wait()
+    h_copy.wait()
     back = []
     for c in range(own):
-        if c % 2 == 0:
-            h_copies[c // 2].wait()
         spec = mm3(turned[c], table[COLS_HI], table[COLS_LO])
         sr, si = spec[:, :N2], spec[:, N2:]
         hr, hi = h_ref[c, :, :N2], h_ref[c, :, N2:]
         mid = mm3(jnp.concatenate([sr * hr + si * hi, sr * hi - si * hr], 1), table[COLS_HI], table[COLS_LO])
         mr, mi = mid[:, :N2], mid[:, N2:]
         back.append((mr * twr - mi * twi, mi * twr + mr * twi))
-    t_copies[2].wait()
     for c in pairs:
         y = None
         for part in range(2):
@@ -372,7 +357,7 @@
     vmem = pl.BlockSpec(memory_space=pltpu.VMEM)
     return pl.pallas_call(
         conv_kernel,
-        in_specs=[pl.BlockSpec(memory_space=pltpu.SMEM), vmem, vmem, ANY, vmem, ANY, ANY],
+        in_specs=[pl.BlockSpec(memory_space=pltpu.SMEM), vmem, vmem, ANY, vmem, vmem, vmem],
         out_specs=ANY,
         out_shape=jax.ShapeDtypeStruct(out, BF16),
         scratch_shapes=[
@@ -380,11 +365,8 @@
             pltpu.VMEM((rows + own, LANES), F32),
             pltpu.VMEM((N1 * own, N2), F32),
             pltpu.VMEM(spectrum.shape, F32),
-            pltpu.VMEM(table.shape, BF16),
-            pltpu.VMEM(twist.shape, F32),
             pltpu.VMEM(out, BF16),
-            pltpu.SemaphoreType.DMA((own // 2,)),
-            pltpu.SemaphoreType.DMA((5,)),
+            pltpu.SemaphoreType.DMA,
             pltpu.SemaphoreType.DMA((PIECES,)),
         ],
         compiler_params=pltpu.CompilerParams(vmem_limit_bytes=CONV_LIMIT),

time: 69.7 us -> 67.5 us (0.968)
  Pallas kernels: 23.1 us -> 20.8 us
    pallas_call x1, Pallas kernels: 7.58 us -> 5.34 us  [conv_call(): pl.pallas_call(conv_kernel, in_specs=[pl.BlockSpec(memory_space=pltpu.SME...]
  transfers between devices with their start and end apart: 4 -> 4, of which waited for: 3 -> 3; matrix products, arithmetic and copies ran while one was open for 3% -> 3% of each run, Pallas kernels for 16% -> 17%
where the time goes in v6:
time: 67.5 us; the launch traced here: 67 us
  starting transfers between devices  23.5 us (35%)
  Pallas kernels  20.8 us (31%)
  waiting for transfers between devices  19.6 us (29%)
  other arithmetic  1.51 us (2%)
  local copies, waits for them, and re-layouts  1.45 us (2%)
    all_to_all x1, waiting for transfers between devices, shards(): back = lax.all_to_all(convolved, ('ctx', 'half'), 0, 0, tiled=True)  15 us
    all_to_all x1, starting transfers between devices, shards(): blocks = lax.all_to_all(gated, 'ctx', 0, 0, tiled=True)  12 us
    pallas_call x1, Pallas kernels, filter_call(): pl.pallas_call(filter_kernel, grid_spec=pltpu.PrefetchScalarGridSpec(num_...  8.8 us
    all_to_all x1, starting transfers between devices, shards(): back = lax.all_to_all(convolved, ('ctx', 'half'), 0, 0, tiled=True)  5.54 us
    pallas_call x1, Pallas kernels, conv_call(): pl.pallas_call(conv_kernel, in_specs=[pl.BlockSpec(memory_space=pltpu.SME...  5.34 us
    pallas_call x1, Pallas kernels, gate_call(): pl.pallas_call(gate_kernel, grid=(channels // STEP,), in_specs=[pl.BlockS...  4.31 us
    ppermute x1, starting transfers between devices, shards(): lax.ppermute(tail, ('half', 'ctx'), [(i, i + 1) for i in range(positions...  3.14 us
    ppermute x1, waiting for transfers between devices, shards(): lax.ppermute(tail, ('half', 'ctx'), [(i, i + 1) for i in range(positions...  3.01 us
  transfers between devices with their start and end apart: 4, of which 3 were waited for; matrix products, arithmetic and copies ran while one was open for 3% of the time, Pallas kernels for 17%

profile of v6, /device:TPU:1, one launch (start us, length us, event | category | flops | bytes accessed | tf_op | source)
XLA Modules:
  0.0 67.0 jit_solution(11985532637191771429)
XLA Ops:
  0.0 0.0 copy-start.2
  0.0 4.3 %gate.1 = bf16[2304,128]{1,0:T(8,128)(2,1)} custom-call(f32[3,7,512]{2,1,0:T(8,128)} %bitcast.19, bf16[3,512,512]{2,1,0:T(8,128)(2,1)} %q_ref.1, bf16[3,512,512]{2,1,0:T(8,128)(2,1)} %q_ref.1), custom_call_target="tpu_custom_call" | custom-call | flops 15728640 | bytes 1572864 | tf_op jit(solution)/shard_map/gate/pallas_call | solution.py:168
  4.3 12.0 %all-to-all-start = ((bf16[32,72,128]{2,1,0:T(8,128)(2,1)}), bf16[32,72,128]{2,1,0:T(8,128)(2,1)S(1)}, u32[]{:S(2)}, u32[]{:S(2)}) async-start(bf16[32,72,128]{2,1,0:T(8,128)(2,1)} %bitcast.18), calls=%async_computation | async-start | bytes 1179648 | tf_op jit(solution)/shard_map/all_to_all | solution.py:388
  16.4 1.0 %slice.6 = bf16[1,512,6]{2,1,0:T(8,128)(2,1)S(1)} slice(bf16[3,512,512]{2,1,0:T(8,128)(2,1)} %q_ref.1), slice={[0:1], [0:512], [506:512]} | slice | bytes 12288 | tf_op jit(solution)/shard_map/slice | solution.py:390
  17.4 0.1 copy.12
  17.5 3.1 %collective-permute-start = (bf16[6,512]{1,0:T(8,128)(2,1)S(1)}, bf16[6,512]{1,0:T(8,128)(2,1)S(1)}, u32[]{:S(2)}, u32[]{:S(2)}) collective-permute-start(bf16[6,512]{1,0:T(8,128)(2,1)S(1)} %bitcast.22), channel_id=1, source_target_pairs={{0,1},{1,2},{2,3},{3,4},{4,5},{5,6},{6,7},{7,8},{8,9},{9,10},{10,1... | collective-permute-start | bytes 18440 | tf_op jit(solution)/shard_map/ppermute | solution.py:391
  20.6 0.0 copy-done.2
  20.6 0.6 pad_add_fusion.place_ref
  21.2 0.1 dynamic-slice_bitcast_fusion
  21.3 0.0 copy-start
  21.3 0.0 copy-start.1
  21.3 8.8 %filter_spectrum.1.h_any = f32[8,256,256]{2,1,0:T(8,128)} custom-call(s32[2]{0:T(128)} %pad_add_fusion.place_ref, f32[512]{0:T(512)} %skip_ref.1, f32[16,32768]{1,0:T(8,128)} %f_ref.1, bf16[2816,256]{1,0:T(8,128)(2,1)} %constant.23.clone.table_any.table, f32[512,128]{1,0:T(8,128)} %constant.24.clone.twist_ref.twist), custom_call_target="tpu_custom_call" | custom-call | flops 1610612736 | bytes 6291456 | tf_op jit(solution)/shard_map/filter_spectrum/pallas_call | solution.py:251
  30.1 0.1 copy.11
  30.2 0.1 broadcast_in_dim.3
  30.2 0.1 reshape.14.taps_ref
  30.4 3.0 %collective-permute-done.halo_ref = bf16[6,512]{1,0:T(8,128)(2,1)S(1)} collective-permute-done((bf16[6,512]{1,0:T(8,128)(2,1)S(1)}, bf16[6,512]{1,0:T(8,128)(2,1)S(1)}, u32[]{:S(2)}, u32[]{:S(2)}) %collective-permute-start) | collective-permute-done | bytes 6176 | tf_op jit(solution)/shard_map/ppermute | solution.py:391
  33.4 0.0 copy-start.3
  33.4 0.0 all-to-all-done
  33.4 2.8 %collective-permute-start.1 = (bf16[2304,128]{1,0:T(8,128)(2,1)S(1)}, bf16[2304,128]{1,0:T(8,128)(2,1)S(1)}, u32[]{:S(2)}, u32[]{:S(2)}) collective-permute-start(bf16[2304,128]{1,0:T(8,128)(2,1)S(1)} %bitcast.16), channel_id=1, source_target_pairs={{0,32},{32,0},{1,33},{33,1},{2,34},{34,2},{3,35},{35,3},{4,36},{36... | collective-permute-start | bytes 1769480 | tf_op jit(solution)/shard_map/ppermute | solution.py:397
  36.2 1.6 %collective-permute-done.1.other_ref = bf16[2304,128]{1,0:T(8,128)(2,1)S(1)} collective-permute-done((bf16[2304,128]{1,0:T(8,128)(2,1)S(1)}, bf16[2304,128]{1,0:T(8,128)(2,1)S(1)}, u32[]{:S(2)}, u32[]{:S(2)}) %collective-permute-start.1) | collective-permute-done | bytes 589856 | tf_op jit(solution)/shard_map/ppermute | solution.py:397
  37.8 0.0 copy-done
  37.8 0.0 copy-done.1
  37.8 5.3 %long_convolution.1 = bf16[512,512]{1,0:T(8,128)(2,1)} custom-call(s32[1]{0:T(128)} %bitcast.5.half_ref, bf16[2304,128]{1,0:T(8,128)(2,1)S(1)} %bitcast.17, bf16[2304,128]{1,0:T(8,128)(2,1)S(1)} %collective-permute-done.1.other_ref, f32[8,256,256]{2,1,0:T(8,128)} %filter_spectrum.1.h_any, f32[8,128]{1,0:T(8,128)S(1)} %reshape.14.taps_ref, ...), custom_call_target="tpu_custom_call" | custom-call | flops 2952790016 | bytes 6291456 | tf_op jit(solution)/shard_map/long_convolution/pallas_call | solution.py:358
  43.2 0.0 copy-done.3
  43.2 5.5 %all-to-all-start.1 = ((bf16[64,8,512]{2,1,0:T(8,128)(2,1)}), bf16[64,8,512]{2,1,0:T(8,128)(2,1)S(1)}, u32[]{:S(2)}, u32[]{:S(2)}) async-start(bf16[64,8,512]{2,1,0:T(8,128)(2,1)} %bitcast.9), calls=%async_computation.1 | async-start | bytes 1048576 | tf_op jit(solution)/shard_map/all_to_all | solution.py:401
  48.7 2.4 %query.1 = f32[512,512]{1,0:T(8,128)S(1)} custom-call(f32[3,7,512]{2,1,0:T(8,128)} %bitcast.20, bf16[6,512]{1,0:T(8,128)(2,1)} %copy-done.3, bf16[3,512,512]{2,1,0:T(8,128)(2,1)} %q_ref.1), custom_call_target="tpu_custom_call" | custom-call | flops 7864320 | bytes 1572864 | tf_op jit(solution)/shard_map/query/pallas_call | solution.py:202
  51.1 15.0 %all-to-all-done.1 = bf16[64,8,512]{2,1,0:T(8,128)(2,1)S(1)} async-done(((bf16[64,8,512]{2,1,0:T(8,128)(2,1)}), bf16[64,8,512]{2,1,0:T(8,128)(2,1)S(1)}, u32[]{:S(2)}, u32[]{:S(2)}) %all-to-all-start.1) | async-done | bytes 524320 | tf_op jit(solution)/shard_map/all_to_all | solution.py:401
  66.1 1.0 %fusion = bf16[512,512]{1,0:T(8,128)(2,1)} fusion(f32[512,512]{1,0:T(8,128)S(1)} %query.1, bf16[64,8,512]{2,1,0:T(8,128)(2,1)S(1)} %all-to-all-done.1), kind=kLoop, calls=%fused_computation.1 | loop fusion | flops 786432 | bytes 2097152 | tf_op jit(solution)/shard_map/convert_element_type | solution.py:403
  (2 shorter events, 0.0 us)
Async XLA Ops:
  0.0 20.6 %copy-start.2 = (f32[7,3,512]{2,0,1:T(8,128)S(1)}, f32[7,3,512]{2,0,1:T(8,128)}, u32[]{:S(2)}) copy-start(f32[7,3,512]{2,0,1:T(8,128)} %param.7) | copy-start | bytes 129028
  4.3 29.1 %all-to-all-start = ((bf16[32,72,128]{2,1,0:T(8,128)(2,1)}), bf16[32,72,128]{2,1,0:T(8,128)(2,1)S(1)}, u32[]{:S(2)}, u32[]{:S(2)}) async-start(bf16[32,72,128]{2,1,0:T(8,128)(2,1)} %bitcast.18), calls=%async_computation | async-start | bytes 1179648 | tf_op jit(solution)/shard_map/all_to_all | solution.py:388
  17.5 15.9 %collective-permute-start = (bf16[6,512]{1,0:T(8,128)(2,1)S(1)}, bf16[6,512]{1,0:T(8,128)(2,1)S(1)}, u32[]{:S(2)}, u32[]{:S(2)}) collective-permute-start(bf16[6,512]{1,0:T(8,128)(2,1)S(1)} %bitcast.22), channel_id=1, source_target_pairs={{0,1},{1,2},{2,3},{3,4},{4,5},{5,6},{6,7},{7,8},{8,9},{9,10},{10,1... | collective-permute-start | bytes 18440 | tf_op jit(solution)/shard_map/ppermute | solution.py:391
  21.3 16.6 %copy-start = (bf16[2816,256]{1,0:T(8,128)(2,1)S(1)}, bf16[2816,256]{1,0:T(8,128)(2,1)}, u32[]{:S(2)}) copy-start(bf16[2816,256]{1,0:T(8,128)(2,1)} %constant.23.clone.table_any.table) | copy-start | bytes 4325380
  21.3 16.6 %copy-start.1 = (f32[512,128]{1,0:T(8,128)S(1)}, f32[512,128]{1,0:T(8,128)}, u32[]{:S(2)}) copy-start(f32[512,128]{1,0:T(8,128)} %constant.24.clone.twist_ref.twist) | copy-start | bytes 786436
  33.4 9.8 %copy-start.3 = (bf16[6,512]{1,0:T(8,128)(2,1)}, bf16[6,512]{1,0:T(8,128)(2,1)S(1)}, u32[]{:S(2)}) copy-start(bf16[6,512]{1,0:T(8,128)(2,1)S(1)} %collective-permute-done.halo_ref) | copy-start | bytes 18436
  33.4 4.5 %collective-permute-start.1 = (bf16[2304,128]{1,0:T(8,128)(2,1)S(1)}, bf16[2304,128]{1,0:T(8,128)(2,1)S(1)}, u32[]{:S(2)}, u32[]{:S(2)}) collective-permute-start(bf16[2304,128]{1,0:T(8,128)(2,1)S(1)} %bitcast.16), channel_id=1, source_target_pairs={{0,32},{32,0},{1,33},{33,1},{2,34},{34,2},{3,35},{35,3},{4,36},{36... | collective-permute-start | bytes 1769480 | tf_op jit(solution)/shard_map/ppermute | solution.py:397
  43.2 22.9 %all-to-all-start.1 = ((bf16[64,8,512]{2,1,0:T(8,128)(2,1)}), bf16[64,8,512]{2,1,0:T(8,128)(2,1)S(1)}, u32[]{:S(2)}, u32[]{:S(2)}) async-start(bf16[64,8,512]{2,1,0:T(8,128)(2,1)} %bitcast.9), calls=%async_computation.1 | async-start | bytes 1048576 | tf_op jit(solution)/shard_map/all_to_all | solution.py:401

commit v7 on v6

--- a/solution.py
+++ b/solution.py
@@ -222,58 +222,69 @@
     return jnp.concatenate([grid_ref[pl.ds(2 * c + a, N1, stride=own), :] for a in range(2)], 1)
 
 
-def filter_kernel(place_ref, skip_ref, f_ref, table_any, twist_ref, o_ref, grid_ref, table, sem):
+def filter_kernel(half_ref, first_ref, skip_ref, f_ref, table_any, twist_ref, o_any, grid_ref, table, o_ref, sem, o_sem):
     copy = pltpu.make_async_copy(table_any.at[FORWARD, :], table, sem)
     copy.start()
     own = f_ref.shape[0]
     for j in range(N1):
         grid_ref[j * own : (j + 1) * own, :] = f_ref[:, j * N2 : (j + 1) * N2]
     copy.wait()
-
-    def pair(c, carry):
+    twr, twi = twist_ref[:N1], twist_ref[N1:]
+    turned = []
+    for c in range(own // 2):
         hi, lo = split(pair_of(grid_ref, c, own))
         top, low = table[: 2 * N1], table[2 * N1 : 4 * N1]
         part = mm(top, hi) + mm(low, hi) + mm(top, lo)
-        twr, twi = twist_ref[:N1], twist_ref[N1:]
         for a in range(2):
             re, im = part[:N1, a * N2 : (a + 1) * N2], part[N1:, a * N2 : (a + 1) * N2]
-            turned = jnp.concatenate([re * twr - im * twi, re * twi + im * twr], 1)
-            spec = mm3(turned, table[COLS_HI], table[COLS_LO])
-            skip = skip_ref[place_ref[1] + 2 * c + a]
-            o_ref[2 * c + a, :, :N2] = (spec[:, :N2] + skip) * (1.0 / TOTAL)
-            o_ref[2 * c + a, :, N2:] = spec[:, N2:] * (-1.0 / TOTAL)
-        return carry
-
-    lax.fori_loop(0, own // 2, pair, 0)
+            turned.append(jnp.concatenate([re * twr - im * twi, re * twi + im * twr], 1))
+    copies = []
+    for c in range(own):
+        spec = mm3(turned[c], table[COLS_HI], table[COLS_LO])
+        skip = skip_ref[first_ref[0] + c]
+        o_ref[c, :, :N2] = (spec[:, :N2] + skip) * (1.0 / TOTAL)
+        o_ref[c, :, N2:] = spec[:, N2:] * (-1.0 / TOTAL)
+        if c % 4 == 3:
+            done = pl.ds(c - 3, 4)
+            copies.append(pltpu.make_async_copy(o_ref.at[done], o_any.at[done], o_sem.at[c // 4]))
+            copies[-1].start()
+    for copy in copies:
+        copy.wait()
 
 
 def filter_call(filters, skip, half_place, first_channel, own, table, twist):
     return pl.pallas_call(
         filter_kernel,
         grid_spec=pltpu.PrefetchScalarGridSpec(
-            num_scalar_prefetch=1,
+            num_scalar_prefetch=2,
             grid=(1,),
             in_specs=[
                 pl.BlockSpec(memory_space=pltpu.SMEM),
-                pl.BlockSpec((own, filters.shape[1]), lambda g, place: (place[0], 0)),
+                pl.BlockSpec((own, filters.shape[1]), lambda g, half, first: (half[0], 0)),
                 ANY,
-                pl.BlockSpec(twist.shape, lambda g, place: (0, 0)),
+                pl.BlockSpec(twist.shape, lambda g, half, first: (0, 0)),
             ],
-            out_specs=pl.BlockSpec((own, N1, 2 * N2), lambda g, place: (0, 0, 0)),
-            scratch_shapes=[pltpu.VMEM((N1 * own, N2), F32), pltpu.VMEM((BACK, N1), BF16), pltpu.SemaphoreType.DMA],
+            out_specs=ANY,
+            scratch_shapes=[
+                pltpu.VMEM((N1 * own, N2), F32),
+                pltpu.VMEM((BACK, N1), BF16),
+                pltpu.VMEM((own, N1, 2 * N2), F32),
+                pltpu.SemaphoreType.DMA,
+                pltpu.SemaphoreType.DMA((own // 4,)),
+            ],
         ),
         out_shape=jax.ShapeDtypeStruct((own, N1, 2 * N2), F32),
         compiler_params=pltpu.CompilerParams(vmem_limit_bytes=VMEM_LIMIT),
         cost_estimate=pl.CostEstimate(flops=12 * own * N1 * N1 * 2 * N2, bytes_accessed=6 << 20, transcendentals=0),
         name="filter_spectrum",
-    )(jnp.stack([half_place, first_channel]).astype(jnp.int32), skip, filters, table, twist)
+    )(half_place.reshape(1), first_channel.reshape(1), skip, filters, table, twist)
 
 
 PIECES = 4
 
 
 def conv_kernel(
-    half_ref, own_ref, other_ref, h_any, taps_ref, table, twist, o_any,
+    own_ref, other_ref, h_any, taps_ref, table, twist, o_any,
     grid_ref, edge_ref, res_ref, h_ref, o_ref, h_sem, o_sem,
 ):
     own = h_ref.shape[0]
@@ -286,7 +297,7 @@
     h_copy = pltpu.make_async_copy(h_any, h_ref, h_sem)
     h_copy.start()
 
-    place = half_ref[0]
+    place = lax.axis_index("half")
     each = block_rows(tiles)
     for ref, side in ((own_ref, place), (other_ref, 1 - place)):
         for i in range(half):
@@ -351,13 +362,13 @@
         copy.wait()
 
 
-def conv_call(half_place, blocks, others, spectrum, taps, table, twist, out):
+def conv_call(blocks, others, spectrum, taps, table, twist, out):
     own = spectrum.shape[0]
     rows = out[0]
     vmem = pl.BlockSpec(memory_space=pltpu.VMEM)
     return pl.pallas_call(
         conv_kernel,
-        in_specs=[pl.BlockSpec(memory_space=pltpu.SMEM), vmem, vmem, ANY, vmem, vmem, vmem],
+        in_specs=[vmem, vmem, ANY, vmem, vmem, vmem],
         out_specs=ANY,
         out_shape=jax.ShapeDtypeStruct(out, BF16),
         scratch_shapes=[
@@ -372,7 +383,7 @@
         compiler_params=pltpu.CompilerParams(vmem_limit_bytes=CONV_LIMIT),
         cost_estimate=pl.CostEstimate(flops=22 * own * N1 * N1 * 2 * N2, bytes_accessed=6 << 20, transcendentals=0),
         name="long_convolution",
-    )(half_place.reshape(1).astype(jnp.int32), blocks, others, spectrum, taps, table, twist)
+    )(blocks, others, spectrum, taps, table, twist)
 
 
 def shards(features, short_taps, filters, skip):
@@ -397,7 +408,7 @@
     others = lax.ppermute(blocks, "half", [(0, 1), (1, 0)])
 
     out = (positions * own, size)
-    convolved = conv_call(half_place, blocks, others, spectrum, own_taps, table, twist, out)
+    convolved = conv_call(blocks, others, spectrum, own_taps, table, twist, out)
     back = lax.all_to_all(convolved, ("ctx", "half"), 0, 0, tiled=True)
     query = query_call(features, taps, halo)
     return (query * back.astype(F32)).astype(BF16)

time: 67.5 us -> 67.4 us (level)
  waiting for transfers between devices: 19.6 us -> 23.4 us
  Pallas kernels: 20.8 us -> 17.6 us
    ppermute x1, waiting for transfers between devices: 3.01 us -> 6.79 us  [shards(): lax.ppermute(tail, ('half', 'ctx'), [(i, i + 1) for i in range(positions...]
    pallas_call x1, Pallas kernels: 8.8 us -> 5.57 us  [filter_call(): pl.pallas_call(filter_kernel, grid_spec=pltpu.PrefetchScalarGridSpec(num_...]
  transfers between devices with their start and end apart: 4 -> 4, of which waited for: 3 -> 3; matrix products, arithmetic and copies ran while one was open for 3% -> 2% of each run, Pallas kernels for 17% -> 12%
where the time goes in v7:
time: 67.4 us; the launch traced here: 67 us
  starting transfers between devices  23.5 us (35%)
  waiting for transfers between devices  23.4 us (35%)
  Pallas kernels  17.6 us (26%)
  local copies, waits for them, and re-layouts  1.45 us (2%)
  other arithmetic  0.95 us (1%)
    all_to_all x1, waiting for transfers between devices, shards(): back = lax.all_to_all(convolved, ('ctx', 'half'), 0, 0, tiled=True)  15 us
    all_to_all x1, starting transfers between devices, shards(): blocks = lax.all_to_all(gated, 'ctx', 0, 0, tiled=True)  12 us
    ppermute x1, waiting for transfers between devices, shards(): lax.ppermute(tail, ('half', 'ctx'), [(i, i + 1) for i in range(positions...  6.79 us
    pallas_call x1, Pallas kernels, filter_call(): pl.pallas_call(filter_kernel, grid_spec=pltpu.PrefetchScalarGridSpec(num_...  5.57 us
    all_to_all x1, starting transfers between devices, shards(): back = lax.all_to_all(convolved, ('ctx', 'half'), 0, 0, tiled=True)  5.55 us
    pallas_call x1, Pallas kernels, conv_call(): pl.pallas_call(conv_kernel, in_specs=[vmem, vmem, ANY, vmem, vmem, vmem],...  5.33 us
    pallas_call x1, Pallas kernels, gate_call(): pl.pallas_call(gate_kernel, grid=(channels // STEP,), in_specs=[pl.BlockS...  4.31 us
    ppermute x1, starting transfers between devices, shards(): lax.ppermute(tail, ('half', 'ctx'), [(i, i + 1) for i in range(positions...  3.14 us
  transfers between devices with their start and end apart: 4, of which 3 were waited for; matrix products, arithmetic and copies ran while one was open for 2% of the time, Pallas kernels for 12%

profile of v7, /device:TPU:1, one launch (start us, length us, event | category | flops | bytes accessed | tf_op | source)
XLA Modules:
  0.0 67.0 jit_solution(6793110792066055181)
XLA Ops:
  0.0 0.0 copy-start.2
  0.0 4.3 %gate.1 = bf16[2304,128]{1,0:T(8,128)(2,1)} custom-call(f32[3,7,512]{2,1,0:T(8,128)} %bitcast.19, bf16[3,512,512]{2,1,0:T(8,128)(2,1)} %q_ref.1, bf16[3,512,512]{2,1,0:T(8,128)(2,1)} %q_ref.1), custom_call_target="tpu_custom_call" | custom-call | flops 15728640 | bytes 1572864 | tf_op jit(solution)/shard_map/gate/pallas_call | solution.py:168
  4.3 12.0 %all-to-all-start = ((bf16[32,72,128]{2,1,0:T(8,128)(2,1)}), bf16[32,72,128]{2,1,0:T(8,128)(2,1)S(1)}, u32[]{:S(2)}, u32[]{:S(2)}) async-start(bf16[32,72,128]{2,1,0:T(8,128)(2,1)} %bitcast.18), calls=%async_computation | async-start | bytes 1179648 | tf_op jit(solution)/shard_map/all_to_all | solution.py:399
  16.4 1.0 %slice.6 = bf16[1,512,6]{2,1,0:T(8,128)(2,1)S(1)} slice(bf16[3,512,512]{2,1,0:T(8,128)(2,1)} %q_ref.1), slice={[0:1], [0:512], [506:512]} | slice | bytes 12288 | tf_op jit(solution)/shard_map/slice | solution.py:401
  17.4 0.1 copy.12
  17.5 3.1 %collective-permute-start = (bf16[6,512]{1,0:T(8,128)(2,1)S(1)}, bf16[6,512]{1,0:T(8,128)(2,1)S(1)}, u32[]{:S(2)}, u32[]{:S(2)}) collective-permute-start(bf16[6,512]{1,0:T(8,128)(2,1)S(1)} %bitcast.22), channel_id=1, source_target_pairs={{0,1},{1,2},{2,3},{3,4},{4,5},{5,6},{6,7},{7,8},{8,9},{9,10},{10,1... | collective-permute-start | bytes 18440 | tf_op jit(solution)/shard_map/ppermute | solution.py:402
  20.6 0.0 copy-done.2
  20.6 0.1 dynamic-slice_bitcast_fusion
  20.7 0.0 copy-start
  20.7 0.0 copy-start.1
  20.7 5.6 %filter_spectrum.1.h_any = f32[8,256,256]{2,1,0:T(8,128)} custom-call(s32[1]{0:T(128)} %bitcast.5.half_ref, s32[1]{0:T(128)} %bitcast.6.first_ref, f32[512]{0:T(512)} %skip_ref.1, f32[16,32768]{1,0:T(8,128)} %f_ref.1, bf16[2816,256]{1,0:T(8,128)(2,1)} %constant.23.clone.table_any.table, f32[512,128]{1,0:T(8,128)} %constant.24.clone.twist_ref.twist), custom_call_target="tpu_custom_call" | custom-call | flops 1610612736 | bytes 6291456 | tf_op jit(solution)/shard_map/filter_spectrum/pallas_call | solution.py:256
  26.3 0.1 copy.11
  26.4 0.1 broadcast_in_dim.3
  26.5 0.1 reshape.21.taps_ref
  26.6 6.8 %collective-permute-done.halo_ref = bf16[6,512]{1,0:T(8,128)(2,1)S(1)} collective-permute-done((bf16[6,512]{1,0:T(8,128)(2,1)S(1)}, bf16[6,512]{1,0:T(8,128)(2,1)S(1)}, u32[]{:S(2)}, u32[]{:S(2)}) %collective-permute-start) | collective-permute-done | bytes 6176 | tf_op jit(solution)/shard_map/ppermute | solution.py:402
  33.4 0.0 copy-start.3
  33.4 0.0 all-to-all-done
  33.4 2.8 %collective-permute-start.1 = (bf16[2304,128]{1,0:T(8,128)(2,1)S(1)}, bf16[2304,128]{1,0:T(8,128)(2,1)S(1)}, u32[]{:S(2)}, u32[]{:S(2)}) collective-permute-start(bf16[2304,128]{1,0:T(8,128)(2,1)S(1)} %bitcast.16), channel_id=1, source_target_pairs={{0,32},{32,0},{1,33},{33,1},{2,34},{34,2},{3,35},{35,3},{4,36},{36... | collective-permute-start | bytes 1769480 | tf_op jit(solution)/shard_map/ppermute | solution.py:408
  36.2 1.6 %collective-permute-done.1.other_ref = bf16[2304,128]{1,0:T(8,128)(2,1)S(1)} collective-permute-done((bf16[2304,128]{1,0:T(8,128)(2,1)S(1)}, bf16[2304,128]{1,0:T(8,128)(2,1)S(1)}, u32[]{:S(2)}, u32[]{:S(2)}) %collective-permute-start.1) | collective-permute-done | bytes 589856 | tf_op jit(solution)/shard_map/ppermute | solution.py:408
  37.8 0.0 copy-done
  37.8 0.0 copy-done.1
  37.8 5.3 %long_convolution.1 = bf16[512,512]{1,0:T(8,128)(2,1)} custom-call(bf16[2304,128]{1,0:T(8,128)(2,1)S(1)} %bitcast.17, bf16[2304,128]{1,0:T(8,128)(2,1)S(1)} %collective-permute-done.1.other_ref, f32[8,256,256]{2,1,0:T(8,128)} %filter_spectrum.1.h_any, f32[8,128]{1,0:T(8,128)S(1)} %reshape.21.taps_ref, bf16[2816,256]{1,0:T(8,128)(2,1)S(1)} %copy-done, ...), custom_call_target="tpu_custom_call" | custom-call | flops 2952790016 | bytes 6291456 | tf_op jit(solution)/shard_map/long_convolution/pallas_call | solution.py:369
  43.2 0.0 copy-done.3
  43.2 5.5 %all-to-all-start.1 = ((bf16[64,8,512]{2,1,0:T(8,128)(2,1)}), bf16[64,8,512]{2,1,0:T(8,128)(2,1)S(1)}, u32[]{:S(2)}, u32[]{:S(2)}) async-start(bf16[64,8,512]{2,1,0:T(8,128)(2,1)} %bitcast.9), calls=%async_computation.1 | async-start | bytes 1048576 | tf_op jit(solution)/shard_map/all_to_all | solution.py:412
  48.7 2.4 %query.1 = f32[512,512]{1,0:T(8,128)S(1)} custom-call(f32[3,7,512]{2,1,0:T(8,128)} %bitcast.20, bf16[6,512]{1,0:T(8,128)(2,1)} %copy-done.3, bf16[3,512,512]{2,1,0:T(8,128)(2,1)} %q_ref.1), custom_call_target="tpu_custom_call" | custom-call | flops 7864320 | bytes 1572864 | tf_op jit(solution)/shard_map/query/pallas_call | solution.py:202
  51.1 15.0 %all-to-all-done.1 = bf16[64,8,512]{2,1,0:T(8,128)(2,1)S(1)} async-done(((bf16[64,8,512]{2,1,0:T(8,128)(2,1)}), bf16[64,8,512]{2,1,0:T(8,128)(2,1)S(1)}, u32[]{:S(2)}, u32[]{:S(2)}) %all-to-all-start.1) | async-done | bytes 524320 | tf_op jit(solution)/shard_map/all_to_all | solution.py:412
  66.1 1.0 %fusion = bf16[512,512]{1,0:T(8,128)(2,1)} fusion(f32[512,512]{1,0:T(8,128)S(1)} %query.1, bf16[64,8,512]{2,1,0:T(8,128)(2,1)S(1)} %all-to-all-done.1), kind=kLoop, calls=%fused_computation.1 | loop fusion | flops 786432 | bytes 2097152 | tf_op jit(solution)/shard_map/convert_element_type | solution.py:414
  (2 shorter events, 0.0 us)
Async XLA Ops:
  0.0 20.6 %copy-start.2 = (f32[7,3,512]{2,0,1:T(8,128)S(1)}, f32[7,3,512]{2,0,1:T(8,128)}, u32[]{:S(2)}) copy-start(f32[7,3,512]{2,0,1:T(8,128)} %param.7) | copy-start | bytes 129028
  4.3 29.1 %all-to-all-start = ((bf16[32,72,128]{2,1,0:T(8,128)(2,1)}), bf16[32,72,128]{2,1,0:T(8,128)(2,1)S(1)}, u32[]{:S(2)}, u32[]{:S(2)}) async-start(bf16[32,72,128]{2,1,0:T(8,128)(2,1)} %bitcast.18), calls=%async_computation | async-start | bytes 1179648 | tf_op jit(solution)/shard_map/all_to_all | solution.py:399
  17.5 15.9 %collective-permute-start = (bf16[6,512]{1,0:T(8,128)(2,1)S(1)}, bf16[6,512]{1,0:T(8,128)(2,1)S(1)}, u32[]{:S(2)}, u32[]{:S(2)}) collective-permute-start(bf16[6,512]{1,0:T(8,128)(2,1)S(1)} %bitcast.22), channel_id=1, source_target_pairs={{0,1},{1,2},{2,3},{3,4},{4,5},{5,6},{6,7},{7,8},{8,9},{9,10},{10,1... | collective-permute-start | bytes 18440 | tf_op jit(solution)/shard_map/ppermute | solution.py:402
  20.7 17.1 %copy-start = (bf16[2816,256]{1,0:T(8,128)(2,1)S(1)}, bf16[2816,256]{1,0:T(8,128)(2,1)}, u32[]{:S(2)}) copy-start(bf16[2816,256]{1,0:T(8,128)(2,1)} %constant.23.clone.table_any.table) | copy-start | bytes 4325380
  20.7 17.1 %copy-start.1 = (f32[512,128]{1,0:T(8,128)S(1)}, f32[512,128]{1,0:T(8,128)}, u32[]{:S(2)}) copy-start(f32[512,128]{1,0:T(8,128)} %constant.24.clone.twist_ref.twist) | copy-start | bytes 786436
  33.4 9.8 %copy-start.3 = (bf16[6,512]{1,0:T(8,128)(2,1)}, bf16[6,512]{1,0:T(8,128)(2,1)S(1)}, u32[]{:S(2)}) copy-start(bf16[6,512]{1,0:T(8,128)(2,1)S(1)} %collective-permute-done.halo_ref) | copy-start | bytes 18436
  33.4 4.5 %collective-permute-start.1 = (bf16[2304,128]{1,0:T(8,128)(2,1)S(1)}, bf16[2304,128]{1,0:T(8,128)(2,1)S(1)}, u32[]{:S(2)}, u32[]{:S(2)}) collective-permute-start(bf16[2304,128]{1,0:T(8,128)(2,1)S(1)} %bitcast.16), channel_id=1, source_target_pairs={{0,32},{32,0},{1,33},{33,1},{2,34},{34,2},{3,35},{35,3},{4,36},{36... | collective-permute-start | bytes 1769480 | tf_op jit(solution)/shard_map/ppermute | solution.py:408
  43.2 22.9 %all-to-all-start.1 = ((bf16[64,8,512]{2,1,0:T(8,128)(2,1)}), bf16[64,8,512]{2,1,0:T(8,128)(2,1)S(1)}, u32[]{:S(2)}, u32[]{:S(2)}) async-start(bf16[64,8,512]{2,1,0:T(8,128)(2,1)} %bitcast.9), calls=%async_computation.1 | async-start | bytes 1048576 | tf_op jit(solution)/shard_map/all_to_all | solution.py:412

commit v8 on v7

--- a/solution.py
+++ b/solution.py
@@ -280,7 +280,7 @@
     )(half_place.reshape(1), first_channel.reshape(1), skip, filters, table, twist)
 
 
-PIECES = 4
+PIECES = 2
 
 
 def conv_kernel(
@@ -337,19 +337,28 @@
         mid = mm3(jnp.concatenate([sr * hr + si * hi, sr * hi - si * hr], 1), table[COLS_HI], table[COLS_LO])
         mr, mi = mid[:, :N2], mid[:, N2:]
         back.append((mr * twr - mi * twi, mi * twr + mr * twi))
+    parts = []
     for c in pairs:
-        y = None
         for part in range(2):
-            at = BACK + part * N1
-            hi, lo = split(jnp.concatenate([back[2 * c][part], back[2 * c + 1][part]], 1))
-            top, low = table[at : at + N1], table[at + 2 * N1 : at + 3 * N1]
-            term = mm(top, hi) + mm(top, lo) + mm(low, hi)
-            y = term if y is None else y + term
-        for a in range(2):
-            res_ref[pl.ds(2 * c + a, N1, stride=own), :] = y[:, a * N2 : (a + 1) * N2]
-
+            parts.append(split(jnp.concatenate([back[2 * c][part], back[2 * c + 1][part]], 1)))
     o_copies = []
+    stretch = N1 // 2 // PIECES
     for i in range(PIECES):
+        cuts = [h * (N1 // 2) + i * stretch for h in range(2)]
+        for c in pairs:
+            y = None
+            for part in range(2):
+                top, low = (
+                    jnp.concatenate([table[at + cut : at + cut + stretch] for cut in cuts], 0)
+                    for at in (BACK + part * N1, BACK + (part + 2) * N1)
+                )
+                hi, lo = parts[2 * c + part]
+                term = mm(top, hi) + mm(top, lo) + mm(low, hi)
+                y = term if y is None else y + term
+            for a in range(2):
+                for h, cut in enumerate(cuts):
+                    piece = y[h * stretch : (h + 1) * stretch, a * N2 : (a + 1) * N2]
+                    res_ref[pl.ds(cut * own + 2 * c + a, stretch, stride=own), :] = piece
         for g in range(i * per_piece, (i + 1) * per_piece):
             for q in range(tiles):
                 at = [((g + h * half) * tiles + q) * own for h in range(2)]

time: 67.4 us -> 67.4 us (level)
  no operation moved by 1% of the time
where the time goes in v8:
time: 67.4 us; the launch traced here: 67 us
  starting transfers between devices  23.5 us (35%)
  waiting for transfers between devices  23.4 us (35%)
  Pallas kernels  17.5 us (26%)
  local copies, waits for them, and re-layouts  1.45 us (2%)
  other arithmetic  0.95 us (1%)
    all_to_all x1, waiting for transfers between devices, shards(): back = lax.all_to_all(convolved, ('ctx', 'half'), 0, 0, tiled=True)  15 us
    all_to_all x1, starting transfers between devices, shards(): blocks = lax.all_to_all(gated, 'ctx', 0, 0, tiled=True)  12 us
    ppermute x1, waiting for transfers between devices, shards(): lax.ppermute(tail, ('half', 'ctx'), [(i, i + 1) for i in range(positions...  6.79 us
    pallas_call x1, Pallas kernels, filter_call(): pl.pallas_call(filter_kernel, grid_spec=pltpu.PrefetchScalarGridSpec(num_...  5.57 us
    all_to_all x1, starting transfers between devices, shards(): back = lax.all_to_all(convolved, ('ctx', 'half'), 0, 0, tiled=True)  5.55 us
    pallas_call x1, Pallas kernels, conv_call(): pl.pallas_call(conv_kernel, in_specs=[vmem, vmem, ANY, vmem, vmem, vmem],...  5.3 us
    pallas_call x1, Pallas kernels, gate_call(): pl.pallas_call(gate_kernel, grid=(channels // STEP,), in_specs=[pl.BlockS...  4.31 us
    ppermute x1, starting transfers between devices, shards(): lax.ppermute(tail, ('half', 'ctx'), [(i, i + 1) for i in range(positions...  3.14 us
  transfers between devices with their start and end apart: 4, of which 3 were waited for; matrix products, arithmetic and copies ran while one was open for 2% of the time, Pallas kernels for 12%

profile of v8, /device:TPU:1, one launch (start us, length us, event | category | flops | bytes accessed | tf_op | source)
XLA Modules:
  0.0 67.0 jit_solution(11798814001734165895)
XLA Ops:
  0.0 0.0 copy-start.2
  0.0 4.3 %gate.1 = bf16[2304,128]{1,0:T(8,128)(2,1)} custom-call(f32[3,7,512]{2,1,0:T(8,128)} %bitcast.19, bf16[3,512,512]{2,1,0:T(8,128)(2,1)} %q_ref.1, bf16[3,512,512]{2,1,0:T(8,128)(2,1)} %q_ref.1), custom_call_target="tpu_custom_call" | custom-call | flops 15728640 | bytes 1572864 | tf_op jit(solution)/shard_map/gate/pallas_call | solution.py:168
  4.3 12.0 %all-to-all-start = ((bf16[32,72,128]{2,1,0:T(8,128)(2,1)}), bf16[32,72,128]{2,1,0:T(8,128)(2,1)S(1)}, u32[]{:S(2)}, u32[]{:S(2)}) async-start(bf16[32,72,128]{2,1,0:T(8,128)(2,1)} %bitcast.18), calls=%async_computation | async-start | bytes 1179648 | tf_op jit(solution)/shard_map/all_to_all | solution.py:408
  16.4 1.0 %slice.6 = bf16[1,512,6]{2,1,0:T(8,128)(2,1)S(1)} slice(bf16[3,512,512]{2,1,0:T(8,128)(2,1)} %q_ref.1), slice={[0:1], [0:512], [506:512]} | slice | bytes 12288 | tf_op jit(solution)/shard_map/slice | solution.py:410
  17.4 0.1 copy.12
  17.5 3.1 %collective-permute-start = (bf16[6,512]{1,0:T(8,128)(2,1)S(1)}, bf16[6,512]{1,0:T(8,128)(2,1)S(1)}, u32[]{:S(2)}, u32[]{:S(2)}) collective-permute-start(bf16[6,512]{1,0:T(8,128)(2,1)S(1)} %bitcast.22), channel_id=1, source_target_pairs={{0,1},{1,2},{2,3},{3,4},{4,5},{5,6},{6,7},{7,8},{8,9},{9,10},{10,1... | collective-permute-start | bytes 18440 | tf_op jit(solution)/shard_map/ppermute | solution.py:411
  20.6 0.0 copy-done.2
  20.6 0.1 dynamic-slice_bitcast_fusion
  20.7 0.0 copy-start
  20.7 0.0 copy-start.1
  20.7 5.6 %filter_spectrum.1.h_any = f32[8,256,256]{2,1,0:T(8,128)} custom-call(s32[1]{0:T(128)} %bitcast.5.half_ref, s32[1]{0:T(128)} %bitcast.6.first_ref, f32[512]{0:T(512)} %skip_ref.1, f32[16,32768]{1,0:T(8,128)} %f_ref.1, bf16[2816,256]{1,0:T(8,128)(2,1)} %constant.23.clone.table_any.table, f32[512,128]{1,0:T(8,128)} %constant.24.clone.twist_ref.twist), custom_call_target="tpu_custom_call" | custom-call | flops 1610612736 | bytes 6291456 | tf_op jit(solution)/shard_map/filter_spectrum/pallas_call | solution.py:256
  26.3 0.1 copy.11
  26.4 0.1 broadcast_in_dim.3
  26.5 0.1 reshape.21.taps_ref
  26.6 6.8 %collective-permute-done.halo_ref = bf16[6,512]{1,0:T(8,128)(2,1)S(1)} collective-permute-done((bf16[6,512]{1,0:T(8,128)(2,1)S(1)}, bf16[6,512]{1,0:T(8,128)(2,1)S(1)}, u32[]{:S(2)}, u32[]{:S(2)}) %collective-permute-start) | collective-permute-done | bytes 6176 | tf_op jit(solution)/shard_map/ppermute | solution.py:411
  33.4 0.0 copy-start.3
  33.4 0.0 all-to-all-done
  33.4 2.8 %collective-permute-start.1 = (bf16[2304,128]{1,0:T(8,128)(2,1)S(1)}, bf16[2304,128]{1,0:T(8,128)(2,1)S(1)}, u32[]{:S(2)}, u32[]{:S(2)}) collective-permute-start(bf16[2304,128]{1,0:T(8,128)(2,1)S(1)} %bitcast.16), channel_id=1, source_target_pairs={{0,32},{32,0},{1,33},{33,1},{2,34},{34,2},{3,35},{35,3},{4,36},{36... | collective-permute-start | bytes 1769480 | tf_op jit(solution)/shard_map/ppermute | solution.py:417
  36.2 1.6 %collective-permute-done.1.other_ref = bf16[2304,128]{1,0:T(8,128)(2,1)S(1)} collective-permute-done((bf16[2304,128]{1,0:T(8,128)(2,1)S(1)}, bf16[2304,128]{1,0:T(8,128)(2,1)S(1)}, u32[]{:S(2)}, u32[]{:S(2)}) %collective-permute-start.1) | collective-permute-done | bytes 589856 | tf_op jit(solution)/shard_map/ppermute | solution.py:417
  37.8 0.0 copy-done
  37.8 0.0 copy-done.1
  37.8 5.3 %long_convolution.1 = bf16[512,512]{1,0:T(8,128)(2,1)} custom-call(bf16[2304,128]{1,0:T(8,128)(2,1)S(1)} %bitcast.17, bf16[2304,128]{1,0:T(8,128)(2,1)S(1)} %collective-permute-done.1.other_ref, f32[8,256,256]{2,1,0:T(8,128)} %filter_spectrum.1.h_any, f32[8,128]{1,0:T(8,128)S(1)} %reshape.21.taps_ref, bf16[2816,256]{1,0:T(8,128)(2,1)S(1)} %copy-done, ...), custom_call_target="tpu_custom_call" | custom-call | flops 2952790016 | bytes 6291456 | tf_op jit(solution)/shard_map/long_convolution/pallas_call | solution.py:378
  43.1 0.0 copy-done.3
  43.2 5.5 %all-to-all-start.1 = ((bf16[64,8,512]{2,1,0:T(8,128)(2,1)}), bf16[64,8,512]{2,1,0:T(8,128)(2,1)S(1)}, u32[]{:S(2)}, u32[]{:S(2)}) async-start(bf16[64,8,512]{2,1,0:T(8,128)(2,1)} %bitcast.9), calls=%async_computation.1 | async-start | bytes 1048576 | tf_op jit(solution)/shard_map/all_to_all | solution.py:421
  48.7 2.4 %query.1 = f32[512,512]{1,0:T(8,128)S(1)} custom-call(f32[3,7,512]{2,1,0:T(8,128)} %bitcast.20, bf16[6,512]{1,0:T(8,128)(2,1)} %copy-done.3, bf16[3,512,512]{2,1,0:T(8,128)(2,1)} %q_ref.1), custom_call_target="tpu_custom_call" | custom-call | flops 7864320 | bytes 1572864 | tf_op jit(solution)/shard_map/query/pallas_call | solution.py:202
  51.1 15.0 %all-to-all-done.1 = bf16[64,8,512]{2,1,0:T(8,128)(2,1)S(1)} async-done(((bf16[64,8,512]{2,1,0:T(8,128)(2,1)}), bf16[64,8,512]{2,1,0:T(8,128)(2,1)S(1)}, u32[]{:S(2)}, u32[]{:S(2)}) %all-to-all-start.1) | async-done | bytes 524320 | tf_op jit(solution)/shard_map/all_to_all | solution.py:421
  66.0 1.0 %fusion = bf16[512,512]{1,0:T(8,128)(2,1)} fusion(f32[512,512]{1,0:T(8,128)S(1)} %query.1, bf16[64,8,512]{2,1,0:T(8,128)(2,1)S(1)} %all-to-all-done.1), kind=kLoop, calls=%fused_computation.1 | loop fusion | flops 786432 | bytes 2097152 | tf_op jit(solution)/shard_map/convert_element_type | solution.py:423
  (2 shorter events, 0.0 us)
Async XLA Ops:
  0.0 20.6 %copy-start.2 = (f32[7,3,512]{2,0,1:T(8,128)S(1)}, f32[7,3,512]{2,0,1:T(8,128)}, u32[]{:S(2)}) copy-start(f32[7,3,512]{2,0,1:T(8,128)} %param.7) | copy-start | bytes 129028
  4.3 29.1 %all-to-all-start = ((bf16[32,72,128]{2,1,0:T(8,128)(2,1)}), bf16[32,72,128]{2,1,0:T(8,128)(2,1)S(1)}, u32[]{:S(2)}, u32[]{:S(2)}) async-start(bf16[32,72,128]{2,1,0:T(8,128)(2,1)} %bitcast.18), calls=%async_computation | async-start | bytes 1179648 | tf_op jit(solution)/shard_map/all_to_all | solution.py:408
  17.5 15.9 %collective-permute-start = (bf16[6,512]{1,0:T(8,128)(2,1)S(1)}, bf16[6,512]{1,0:T(8,128)(2,1)S(1)}, u32[]{:S(2)}, u32[]{:S(2)}) collective-permute-start(bf16[6,512]{1,0:T(8,128)(2,1)S(1)} %bitcast.22), channel_id=1, source_target_pairs={{0,1},{1,2},{2,3},{3,4},{4,5},{5,6},{6,7},{7,8},{8,9},{9,10},{10,1... | collective-permute-start | bytes 18440 | tf_op jit(solution)/shard_map/ppermute | solution.py:411
  20.7 17.1 %copy-start = (bf16[2816,256]{1,0:T(8,128)(2,1)S(1)}, bf16[2816,256]{1,0:T(8,128)(2,1)}, u32[]{:S(2)}) copy-start(bf16[2816,256]{1,0:T(8,128)(2,1)} %constant.23.clone.table_any.table) | copy-start | bytes 4325380
  20.7 17.1 %copy-start.1 = (f32[512,128]{1,0:T(8,128)S(1)}, f32[512,128]{1,0:T(8,128)}, u32[]{:S(2)}) copy-start(f32[512,128]{1,0:T(8,128)} %constant.24.clone.twist_ref.twist) | copy-start | bytes 786436
  33.4 9.8 %copy-start.3 = (bf16[6,512]{1,0:T(8,128)(2,1)}, bf16[6,512]{1,0:T(8,128)(2,1)S(1)}, u32[]{:S(2)}) copy-start(bf16[6,512]{1,0:T(8,128)(2,1)S(1)} %collective-permute-done.halo_ref) | copy-start | bytes 18436
  33.4 4.5 %collective-permute-start.1 = (bf16[2304,128]{1,0:T(8,128)(2,1)S(1)}, bf16[2304,128]{1,0:T(8,128)(2,1)S(1)}, u32[]{:S(2)}, u32[]{:S(2)}) collective-permute-start(bf16[2304,128]{1,0:T(8,128)(2,1)S(1)} %bitcast.16), channel_id=1, source_target_pairs={{0,32},{32,0},{1,33},{33,1},{2,34},{34,2},{3,35},{35,3},{4,36},{36... | collective-permute-start | bytes 1769480 | tf_op jit(solution)/shard_map/ppermute | solution.py:417
  43.2 22.9 %all-to-all-start.1 = ((bf16[64,8,512]{2,1,0:T(8,128)(2,1)}), bf16[64,8,512]{2,1,0:T(8,128)(2,1)S(1)}, u32[]{:S(2)}, u32[]{:S(2)}) async-start(bf16[64,8,512]{2,1,0:T(8,128)(2,1)} %bitcast.9), calls=%async_computation.1 | async-start | bytes 1048576 | tf_op jit(solution)/shard_map/all_to_all | solution.py:421

commit v9 on v6

--- a/solution.py
+++ b/solution.py
@@ -273,7 +273,7 @@
 
 
 def conv_kernel(
-    half_ref, own_ref, other_ref, h_any, taps_ref, table, twist, o_any,
+    own_ref, other_ref, h_any, taps_ref, table, twist, o_any,
     grid_ref, edge_ref, res_ref, h_ref, o_ref, h_sem, o_sem,
 ):
     own = h_ref.shape[0]
@@ -286,7 +286,7 @@
     h_copy = pltpu.make_async_copy(h_any, h_ref, h_sem)
     h_copy.start()
 
-    place = half_ref[0]
+    place = lax.axis_index("half")
     each = block_rows(tiles)
     for ref, side in ((own_ref, place), (other_ref, 1 - place)):
         for i in range(half):
@@ -351,13 +351,13 @@
         copy.wait()
 
 
-def conv_call(half_place, blocks, others, spectrum, taps, table, twist, out):
+def conv_call(blocks, others, spectrum, taps, table, twist, out):
     own = spectrum.shape[0]
     rows = out[0]
     vmem = pl.BlockSpec(memory_space=pltpu.VMEM)
     return pl.pallas_call(
         conv_kernel,
-        in_specs=[pl.BlockSpec(memory_space=pltpu.SMEM), vmem, vmem, ANY, vmem, vmem, vmem],
+        in_specs=[vmem, vmem, ANY, vmem, vmem, vmem],
         out_specs=ANY,
         out_shape=jax.ShapeDtypeStruct(out, BF16),
         scratch_shapes=[
@@ -372,7 +372,7 @@
         compiler_params=pltpu.CompilerParams(vmem_limit_bytes=CONV_LIMIT),
         cost_estimate=pl.CostEstimate(flops=22 * own * N1 * N1 * 2 * N2, bytes_accessed=6 << 20, transcendentals=0),
         name="long_convolution",
-    )(half_place.reshape(1).astype(jnp.int32), blocks, others, spectrum, taps, table, twist)
+    )(blocks, others, spectrum, taps, table, twist)
 
 
 def shards(features, short_taps, filters, skip):
@@ -397,7 +397,7 @@
     others = lax.ppermute(blocks, "half", [(0, 1), (1, 0)])
 
     out = (positions * own, size)
-    convolved = conv_call(half_place, blocks, others, spectrum, own_taps, table, twist, out)
+    convolved = conv_call(blocks, others, spectrum, own_taps, table, twist, out)
     back = lax.all_to_all(convolved, ("ctx", "half"), 0, 0, tiled=True)
     query = query_call(features, taps, halo)
     return (query * back.astype(F32)).astype(BF16)

time: 67.5 us -> 67.5 us (level)
  no operation moved by 1% of the time
where the time goes in v9:
time: 67.5 us; the launch traced here: 67 us
  starting transfers between devices  23.5 us (35%)
  Pallas kernels  20.8 us (31%)
  waiting for transfers between devices  19.6 us (29%)
  other arithmetic  1.51 us (2%)
  local copies, waits for them, and re-layouts  1.45 us (2%)
    all_to_all x1, waiting for transfers between devices, shards(): back = lax.all_to_all(convolved, ('ctx', 'half'), 0, 0, tiled=True)  15 us
    all_to_all x1, starting transfers between devices, shards(): blocks = lax.all_to_all(gated, 'ctx', 0, 0, tiled=True)  12 us
    pallas_call x1, Pallas kernels, filter_call(): pl.pallas_call(filter_kernel, grid_spec=pltpu.PrefetchScalarGridSpec(num_...  8.8 us
    all_to_all x1, starting transfers between devices, shards(): back = lax.all_to_all(convolved, ('ctx', 'half'), 0, 0, tiled=True)  5.55 us
    pallas_call x1, Pallas kernels, conv_call(): pl.pallas_call(conv_kernel, in_specs=[vmem, vmem, ANY, vmem, vmem, vmem],...  5.33 us
    pallas_call x1, Pallas kernels, gate_call(): pl.pallas_call(gate_kernel, grid=(channels // STEP,), in_specs=[pl.BlockS...  4.31 us
    ppermute x1, starting transfers between devices, shards(): lax.ppermute(tail, ('half', 'ctx'), [(i, i + 1) for i in range(positions...  3.14 us
    ppermute x1, waiting for transfers between devices, shards(): lax.ppermute(tail, ('half', 'ctx'), [(i, i + 1) for i in range(positions...  3.01 us
  transfers between devices with their start and end apart: 4, of which 3 were waited for; matrix products, arithmetic and copies ran while one was open for 3% of the time, Pallas kernels for 17%

profile of v9, /device:TPU:1, one launch (start us, length us, event | category | flops | bytes accessed | tf_op | source)
XLA Modules:
  0.0 67.0 jit_solution(5733367967040804857)
XLA Ops:
  0.0 0.0 copy-start.2
  0.0 4.3 %gate.1 = bf16[2304,128]{1,0:T(8,128)(2,1)} custom-call(f32[3,7,512]{2,1,0:T(8,128)} %bitcast.19, bf16[3,512,512]{2,1,0:T(8,128)(2,1)} %q_ref.1, bf16[3,512,512]{2,1,0:T(8,128)(2,1)} %q_ref.1), custom_call_target="tpu_custom_call" | custom-call | flops 15728640 | bytes 1572864 | tf_op jit(solution)/shard_map/gate/pallas_call | solution.py:168
  4.3 12.0 %all-to-all-start = ((bf16[32,72,128]{2,1,0:T(8,128)(2,1)}), bf16[32,72,128]{2,1,0:T(8,128)(2,1)S(1)}, u32[]{:S(2)}, u32[]{:S(2)}) async-start(bf16[32,72,128]{2,1,0:T(8,128)(2,1)} %bitcast.18), calls=%async_computation | async-start | bytes 1179648 | tf_op jit(solution)/shard_map/all_to_all | solution.py:388
  16.4 1.0 %slice.6 = bf16[1,512,6]{2,1,0:T(8,128)(2,1)S(1)} slice(bf16[3,512,512]{2,1,0:T(8,128)(2,1)} %q_ref.1), slice={[0:1], [0:512], [506:512]} | slice | bytes 12288 | tf_op jit(solution)/shard_map/slice | solution.py:390
  17.4 0.1 copy.12
  17.5 3.1 %collective-permute-start = (bf16[6,512]{1,0:T(8,128)(2,1)S(1)}, bf16[6,512]{1,0:T(8,128)(2,1)S(1)}, u32[]{:S(2)}, u32[]{:S(2)}) collective-permute-start(bf16[6,512]{1,0:T(8,128)(2,1)S(1)} %bitcast.22), channel_id=1, source_target_pairs={{0,1},{1,2},{2,3},{3,4},{4,5},{5,6},{6,7},{7,8},{8,9},{9,10},{10,1... | collective-permute-start | bytes 18440 | tf_op jit(solution)/shard_map/ppermute | solution.py:391
  20.6 0.0 copy-done.2
  20.6 0.6 pad_add_fusion.place_ref
  21.2 0.1 dynamic-slice_bitcast_fusion
  21.3 0.0 copy-start
  21.3 0.0 copy-start.1
  21.3 8.8 %filter_spectrum.1.h_any = f32[8,256,256]{2,1,0:T(8,128)} custom-call(s32[2]{0:T(128)} %pad_add_fusion.place_ref, f32[512]{0:T(512)} %skip_ref.1, f32[16,32768]{1,0:T(8,128)} %f_ref.1, bf16[2816,256]{1,0:T(8,128)(2,1)} %constant.23.clone.table_any.table, f32[512,128]{1,0:T(8,128)} %constant.24.clone.twist_ref.twist), custom_call_target="tpu_custom_call" | custom-call | flops 1610612736 | bytes 6291456 | tf_op jit(solution)/shard_map/filter_spectrum/pallas_call | solution.py:251
  30.1 0.1 copy.11
  30.2 0.1 broadcast_in_dim.3
  30.2 0.1 reshape.13.taps_ref
  30.4 3.0 %collective-permute-done.halo_ref = bf16[6,512]{1,0:T(8,128)(2,1)S(1)} collective-permute-done((bf16[6,512]{1,0:T(8,128)(2,1)S(1)}, bf16[6,512]{1,0:T(8,128)(2,1)S(1)}, u32[]{:S(2)}, u32[]{:S(2)}) %collective-permute-start) | collective-permute-done | bytes 6176 | tf_op jit(solution)/shard_map/ppermute | solution.py:391
  33.4 0.0 copy-start.3
  33.4 0.0 all-to-all-done
  33.4 2.8 %collective-permute-start.1 = (bf16[2304,128]{1,0:T(8,128)(2,1)S(1)}, bf16[2304,128]{1,0:T(8,128)(2,1)S(1)}, u32[]{:S(2)}, u32[]{:S(2)}) collective-permute-start(bf16[2304,128]{1,0:T(8,128)(2,1)S(1)} %bitcast.16), channel_id=1, source_target_pairs={{0,32},{32,0},{1,33},{33,1},{2,34},{34,2},{3,35},{35,3},{4,36},{36... | collective-permute-start | bytes 1769480 | tf_op jit(solution)/shard_map/ppermute | solution.py:397
  36.2 1.6 %collective-permute-done.1.other_ref = bf16[2304,128]{1,0:T(8,128)(2,1)S(1)} collective-permute-done((bf16[2304,128]{1,0:T(8,128)(2,1)S(1)}, bf16[2304,128]{1,0:T(8,128)(2,1)S(1)}, u32[]{:S(2)}, u32[]{:S(2)}) %collective-permute-start.1) | collective-permute-done | bytes 589856 | tf_op jit(solution)/shard_map/ppermute | solution.py:397
  37.8 0.0 copy-done
  37.8 0.0 copy-done.1
  37.8 5.3 %long_convolution.1 = bf16[512,512]{1,0:T(8,128)(2,1)} custom-call(bf16[2304,128]{1,0:T(8,128)(2,1)S(1)} %bitcast.17, bf16[2304,128]{1,0:T(8,128)(2,1)S(1)} %collective-permute-done.1.other_ref, f32[8,256,256]{2,1,0:T(8,128)} %filter_spectrum.1.h_any, f32[8,128]{1,0:T(8,128)S(1)} %reshape.13.taps_ref, bf16[2816,256]{1,0:T(8,128)(2,1)S(1)} %copy-done, ...), custom_call_target="tpu_custom_call" | custom-call | flops 2952790016 | bytes 6291456 | tf_op jit(solution)/shard_map/long_convolution/pallas_call | solution.py:358
  43.2 0.0 copy-done.3
  43.2 5.5 %all-to-all-start.1 = ((bf16[64,8,512]{2,1,0:T(8,128)(2,1)}), bf16[64,8,512]{2,1,0:T(8,128)(2,1)S(1)}, u32[]{:S(2)}, u32[]{:S(2)}) async-start(bf16[64,8,512]{2,1,0:T(8,128)(2,1)} %bitcast.9), calls=%async_computation.1 | async-start | bytes 1048576 | tf_op jit(solution)/shard_map/all_to_all | solution.py:401
  48.7 2.4 %query.1 = f32[512,512]{1,0:T(8,128)S(1)} custom-call(f32[3,7,512]{2,1,0:T(8,128)} %bitcast.20, bf16[6,512]{1,0:T(8,128)(2,1)} %copy-done.3, bf16[3,512,512]{2,1,0:T(8,128)(2,1)} %q_ref.1), custom_call_target="tpu_custom_call" | custom-call | flops 7864320 | bytes 1572864 | tf_op jit(solution)/shard_map/query/pallas_call | solution.py:202
  51.1 15.0 %all-to-all-done.1 = bf16[64,8,512]{2,1,0:T(8,128)(2,1)S(1)} async-done(((bf16[64,8,512]{2,1,0:T(8,128)(2,1)}), bf16[64,8,512]{2,1,0:T(8,128)(2,1)S(1)}, u32[]{:S(2)}, u32[]{:S(2)}) %all-to-all-start.1) | async-done | bytes 524320 | tf_op jit(solution)/shard_map/all_to_all | solution.py:401
  66.1 1.0 %fusion = bf16[512,512]{1,0:T(8,128)(2,1)} fusion(f32[512,512]{1,0:T(8,128)S(1)} %query.1, bf16[64,8,512]{2,1,0:T(8,128)(2,1)S(1)} %all-to-all-done.1), kind=kLoop, calls=%fused_computation.1 | loop fusion | flops 786432 | bytes 2097152 | tf_op jit(solution)/shard_map/convert_element_type | solution.py:403
  (2 shorter events, 0.0 us)
Async XLA Ops:
  0.0 20.6 %copy-start.2 = (f32[7,3,512]{2,0,1:T(8,128)S(1)}, f32[7,3,512]{2,0,1:T(8,128)}, u32[]{:S(2)}) copy-start(f32[7,3,512]{2,0,1:T(8,128)} %param.7) | copy-start | bytes 129028
  4.3 29.1 %all-to-all-start = ((bf16[32,72,128]{2,1,0:T(8,128)(2,1)}), bf16[32,72,128]{2,1,0:T(8,128)(2,1)S(1)}, u32[]{:S(2)}, u32[]{:S(2)}) async-start(bf16[32,72,128]{2,1,0:T(8,128)(2,1)} %bitcast.18), calls=%async_computation | async-start | bytes 1179648 | tf_op jit(solution)/shard_map/all_to_all | solution.py:388
  17.5 15.9 %collective-permute-start = (bf16[6,512]{1,0:T(8,128)(2,1)S(1)}, bf16[6,512]{1,0:T(8,128)(2,1)S(1)}, u32[]{:S(2)}, u32[]{:S(2)}) collective-permute-start(bf16[6,512]{1,0:T(8,128)(2,1)S(1)} %bitcast.22), channel_id=1, source_target_pairs={{0,1},{1,2},{2,3},{3,4},{4,5},{5,6},{6,7},{7,8},{8,9},{9,10},{10,1... | collective-permute-start | bytes 18440 | tf_op jit(solution)/shard_map/ppermute | solution.py:391
  21.3 16.6 %copy-start = (bf16[2816,256]{1,0:T(8,128)(2,1)S(1)}, bf16[2816,256]{1,0:T(8,128)(2,1)}, u32[]{:S(2)}) copy-start(bf16[2816,256]{1,0:T(8,128)(2,1)} %constant.23.clone.table_any.table) | copy-start | bytes 4325380
  21.3 16.6 %copy-start.1 = (f32[512,128]{1,0:T(8,128)S(1)}, f32[512,128]{1,0:T(8,128)}, u32[]{:S(2)}) copy-start(f32[512,128]{1,0:T(8,128)} %constant.24.clone.twist_ref.twist) | copy-start | bytes 786436
  33.4 9.8 %copy-start.3 = (bf16[6,512]{1,0:T(8,128)(2,1)}, bf16[6,512]{1,0:T(8,128)(2,1)S(1)}, u32[]{:S(2)}) copy-start(bf16[6,512]{1,0:T(8,128)(2,1)S(1)} %collective-permute-done.halo_ref) | copy-start | bytes 18436
  33.4 4.5 %collective-permute-start.1 = (bf16[2304,128]{1,0:T(8,128)(2,1)S(1)}, bf16[2304,128]{1,0:T(8,128)(2,1)S(1)}, u32[]{:S(2)}, u32[]{:S(2)}) collective-permute-start(bf16[2304,128]{1,0:T(8,128)(2,1)S(1)} %bitcast.16), channel_id=1, source_target_pairs={{0,32},{32,0},{1,33},{33,1},{2,34},{34,2},{3,35},{35,3},{4,36},{36... | collective-permute-start | bytes 1769480 | tf_op jit(solution)/shard_map/ppermute | solution.py:397
  43.2 22.9 %all-to-all-start.1 = ((bf16[64,8,512]{2,1,0:T(8,128)(2,1)}), bf16[64,8,512]{2,1,0:T(8,128)(2,1)S(1)}, u32[]{:S(2)}, u32[]{:S(2)}) async-start(bf16[64,8,512]{2,1,0:T(8,128)(2,1)} %bitcast.9), calls=%async_computation.1 | async-start | bytes 1048576 | tf_op jit(solution)/shard_map/all_to_all | solution.py:401
